TPU v7x, 32 devices: a whole 2x2x4 slice. The times are simulated.
32 devices in a mesh: seq: 8 (over y, x, core), tp: 4 (over z).
Axes of the slice: x: 2, y: 2, z: 4, core: 2. Of those that a mesh axis runs over, the one named last changes fastest.
Arguments:
- tokens: bfloat16 [8192, 2048], P('seq'), may hold values from -6 to 6
- attn_gain: bfloat16 [2048], P('seq'), may hold values from 0.3984375 to 1.59375
- w_query: bfloat16 [2048, 2048], P('seq', 'tp'), may hold values from -0.125 to 0.125
- w_key: bfloat16 [2048, 2048], P('seq', 'tp'), may hold values from -0.125 to 0.125
- w_value: bfloat16 [2048, 4096], P('seq', 'tp'), may hold values from -0.125 to 0.125
- w_gate_out: bfloat16 [2048, 4096], P('seq', 'tp'), may hold values from -0.125 to 0.125
- w_alpha: bfloat16 [2048, 16], P('seq', 'tp'), may hold values from -0.125 to 0.125
- w_beta: bfloat16 [2048, 16], P('seq', 'tp'), may hold values from -0.125 to 0.125
- conv_query: float32 [4, 2048], P(None, 'tp'), may hold values from -3 to 3
- conv_key: float32 [4, 2048], P(None, 'tp'), may hold values from -3 to 3
- conv_value: float32 [4, 4096], P(None, 'tp'), may hold values from -3 to 3
- decay_scale: float32 [16], P('tp'), may hold values from 0.00012207031 to 0.08
- dt_bias: float32 [16], P('tp'), may hold values from -1 to 1
- out_gain: float32 [256], replicated, may hold values from 0.4 to 1.6
- w_out: bfloat16 [2048, 4096], P('seq', 'tp'), may hold values from -0.15625 to 0.15625
- mlp_gain: bfloat16 [2048], P('seq'), may hold values from 0.3984375 to 1.59375
- w_mlp_gate: bfloat16 [2048, 5504], P('seq', 'tp'), may hold values from -0.125 to 0.125
- w_mlp_up: bfloat16 [2048, 5504], P('seq', 'tp'), may hold values from -0.125 to 0.125
- w_mlp_down: bfloat16 [2048, 5504], P('seq', 'tp'), may hold values from -0.125 to 0.125
- init_state: float32 [16, 128, 256], P('tp'), may hold values from -3 to 3
- seg_starts: int32 [5], replicated, may hold values from 0 to 8128, as said below
- continues: int32 [4], replicated, may hold values 0 or 1
- cotangent: bfloat16 [8192, 2048], P('seq'), may hold values from -6 to 6
Outputs:
- block_out: bfloat16 [8192, 2048], P('seq')
- final_state: float32 [16, 128, 256], P('tp', 'seq')
- grad_tokens: float32 [8192, 2048], P('seq')
- grad_attn_gain: float32 [2048], P('seq')
- grad_w_query: float32 [2048, 2048], P('seq', 'tp')
- grad_w_key: float32 [2048, 2048], P('seq', 'tp')
- grad_w_value: float32 [2048, 4096], P('seq', 'tp')
- grad_w_gate_out: float32 [2048, 4096], P('seq', 'tp')
- grad_w_alpha: float32 [2048, 16], P('seq', 'tp')
- grad_w_beta: float32 [2048, 16], P('seq', 'tp')
- grad_conv_query: float32 [4, 2048], P(None, 'tp')
- grad_conv_key: float32 [4, 2048], P(None, 'tp')
- grad_conv_value: float32 [4, 4096], P(None, 'tp')
- grad_decay_scale: float32 [16], P('tp')
- grad_dt_bias: float32 [16], P('tp')
- grad_out_gain: float32 [256], replicated
- grad_w_out: float32 [2048, 4096], P('seq', 'tp')
- grad_mlp_gain: float32 [2048], P('seq')
- grad_w_mlp_gate: float32 [2048, 5504], P('seq', 'tp')
- grad_w_mlp_up: float32 [2048, 5504], P('seq', 'tp')
- grad_w_mlp_down: float32 [2048, 5504], P('seq', 'tp')
Inputs may be any that keep to these rules, and one draw needn't show every extreme that they name: `seg_starts`: strictly increasing multiples of 64: the first is 0, the second lies within the first 1024 tokens, all later ones within the last 1024 tokens of the stream. Entry j is 1 where segment j + 1 continues the document before it (no reset of state or convolution at its start) and 0 where it opens a new document; the first segment always continues from init_state.
All inputs are finite; a program needn't handle non-finite values.
Results may differ from a plain program's by a relative error of at most 0.019.
Values may be sent and summed in bfloat16 or wider, within the bound.
No kernel may reach another device: no remote copies, remote signals or barrier semaphores. Data moves between devices by JAX's collectives and lax.ppermute only.
A program may use at most 384 MiB of HBM per device.

v0:
```python
from functools import partial

import jax
import jax.numpy as jnp
from jax import lax
from jax.sharding import PartitionSpec as P

DK = 128
GROUP = 64


full_precision = lax.Precision.HIGHEST
norm_epsilon = 1e-06
tap_count = 4


def passed_along(block, axis, distance):
    devices = range(lax.axis_size(axis))
    route = [(i - distance, i) for i in devices if i - distance in devices]
    return lax.ppermute(block, axis, route)


def lower_solve(matrix, rhs):
    return lax.linalg.triangular_solve(matrix, rhs, left_side=True, lower=True, unit_diagonal=True)


def project_rows(left, right):
    return jnp.dot(left, right, preferred_element_type=jnp.float32)


def project_back(left, right):
    return jnp.einsum("tc,dc->td", left, right, preferred_element_type=jnp.float32)


def weight_grad(left, right):
    return jnp.einsum("td,tc->dc", left, right, preferred_element_type=jnp.float32)


def batch_product(left, right):
    return jnp.einsum("...ij,...jk->...ik", left, right, precision=full_precision)


def rms_scale(values, scales):
    return (
        values
        * lax.rsqrt(jnp.mean(values * values, axis=-1, keepdims=True) + norm_epsilon)
        * scales
    )


def doc_numbers(positions, seg_starts, continues):
    opens = 1 - continues
    passed = (positions[:, None] >= seg_starts[None, 1:]).astype(jnp.int32)
    return jnp.sum(passed * opens[None, :], axis=1)


def tap_masks(positions, seg_starts, continues):
    own_doc = doc_numbers(positions, seg_starts, continues)
    columns = []
    for tap_index in range(tap_count):
        earlier = positions - tap_index
        same_doc = (earlier >= 0) & (doc_numbers(earlier, seg_starts, continues) == own_doc)
        columns.append(same_doc.astype(jnp.float32))
    return jnp.stack(columns, axis=1)


def group_masks(positions, seg_starts, continues):
    firsts = positions[::GROUP]
    same_doc = doc_numbers(firsts, seg_starts, continues) == doc_numbers(
        firsts - 1, seg_starts, continues
    )
    return same_doc.astype(jnp.float32)


def conv_silu(features, rim_rows, weights, tap_keep):
    padded = jnp.concatenate([rim_rows, features], axis=0)
    length = features.shape[0]
    total = features * weights[0]
    for tap_index in range(1, tap_count):
        begin = tap_count - 1 - tap_index
        total = (
            total
            + padded[begin : begin + length]
            * weights[tap_index]
            * tap_keep[:, tap_index : tap_index + 1]
        )
    return jax.nn.silu(total)


def unit_rows(values, factor):
    return (
        values * lax.rsqrt(jnp.sum(values * values, axis=-1, keepdims=True) + norm_epsilon) * factor
    )


def mixer_inputs(
    q_proj,
    k_proj,
    v_proj,
    rim_rows,
    conv_query,
    conv_key,
    conv_value,
    alpha_proj,
    beta_proj,
    decay_scale,
    dt_bias,
    tap_keep,
):
    key_width = q_proj.shape[1]
    head_count = alpha_proj.shape[1]
    length = q_proj.shape[0]
    queries = conv_silu(q_proj, rim_rows[:, :key_width], conv_query, tap_keep)
    key_rows = conv_silu(k_proj, rim_rows[:, key_width : 2 * key_width], conv_key, tap_keep)
    value_rows = conv_silu(v_proj, rim_rows[:, 2 * key_width :], conv_value, tap_keep)
    queries = unit_rows(queries.reshape(length, head_count, -1), DK ** (-0.5))
    key_rows = unit_rows(key_rows.reshape(length, head_count, -1), 1.0)
    value_rows = value_rows.reshape(length, head_count, -1)
    log_decay = -decay_scale * jax.nn.softplus(alpha_proj + dt_bias)
    beta_gate = jax.nn.sigmoid(beta_proj)
    return (queries, key_rows, value_rows, log_decay, beta_gate)


def group_rows(values):
    shaped = values.reshape((values.shape[0] // GROUP, GROUP) + values.shape[1:])
    return shaped.transpose(0, 2, 1, 3)


def group_scalars(values):
    shaped = values.reshape((values.shape[0] // GROUP, GROUP) + values.shape[1:])
    return shaped.transpose(0, 2, 1)


def rows_from_groups(values):
    shaped = values.transpose(0, 2, 1, 3)
    return shaped.reshape((shaped.shape[0] * shaped.shape[1],) + shaped.shape[2:])


def scalars_from_groups(values):
    shaped = values.transpose(0, 2, 1)
    return shaped.reshape((shaped.shape[0] * shaped.shape[1],) + shaped.shape[2:])


def group_terms(key_rows, value_rows, log_decay, beta_gate):
    cum_decay = jnp.cumsum(log_decay, axis=-1)
    block_size = log_decay.shape[-1]
    row_ids = lax.broadcasted_iota(jnp.int32, (block_size, block_size), 0)
    col_ids = lax.broadcasted_iota(jnp.int32, (block_size, block_size), 1)
    gap_decay = cum_decay[..., :, None] - cum_decay[..., None, :]
    decay_in = jnp.where(
        row_ids >= col_ids, jnp.exp(jnp.where(row_ids >= col_ids, gap_decay, 0.0)), 0.0
    )
    key_gram = jnp.einsum("...ik,...jk->...ij", key_rows, key_rows, precision=full_precision)
    unit_lower = jnp.eye(block_size, dtype=jnp.float32) + jnp.where(
        row_ids > col_ids, beta_gate[..., :, None] * decay_in * key_gram, 0.0
    )
    solved_values = lower_solve(unit_lower, beta_gate[..., None] * value_rows)
    solved_keys = lower_solve(unit_lower, (beta_gate * jnp.exp(cum_decay))[..., None] * key_rows)
    key_tail = jnp.exp(cum_decay[..., -1:] - cum_decay)[..., None] * key_rows
    return (cum_decay, decay_in, solved_values, solved_keys, key_tail, key_rows)


def group_apply(carry_state, query_block, parts):
    cum_decay, decay_in, solved_values, solved_keys, key_tail, key_rows = parts
    fresh_values = solved_values - batch_product(solved_keys, carry_state)
    scores = (
        jnp.einsum("...ik,...jk->...ij", query_block, key_rows, precision=full_precision) * decay_in
    )
    block_out = jnp.exp(cum_decay)[..., None] * batch_product(
        query_block, carry_state
    ) + batch_product(scores, fresh_values)
    new_state = jnp.exp(cum_decay[..., -1])[..., None, None] * carry_state + jnp.einsum(
        "...ck,...cv->...kv", key_tail, fresh_values, precision=full_precision
    )
    return (new_state, block_out)


def state_pass(start_state, query_blocks, group_parts, keep_group):

    def state_advance(carry_state, pieces):
        query_block, parts, keep_block = pieces
        return group_apply(carry_state * keep_block, query_block, parts)

    end_state, out_blocks = lax.scan(
        state_advance, start_state, (query_blocks, group_parts, keep_group)
    )
    return (out_blocks, end_state)


def group_maps(group_parts, keep_group):
    cum_decay, decay_in, solved_values, solved_keys, key_tail, key_rows = group_parts
    identity = jnp.eye(key_rows.shape[-1], dtype=jnp.float32)
    map_mats = jnp.exp(cum_decay[..., -1])[..., None, None] * identity - jnp.einsum(
        "...ck,...cl->...kl", key_tail, solved_keys, precision=full_precision
    )
    map_offs = jnp.einsum("...ck,...cv->...kv", key_tail, solved_values, precision=full_precision)
    return (map_mats * keep_group[:, None, None, None], map_offs)


def compose_maps(earlier, later):
    return (batch_product(later[0], earlier[0]), batch_product(later[0], earlier[1]) + later[1])


def compose_groups(map_mats, map_offs):
    identity = jnp.broadcast_to(jnp.eye(map_mats.shape[-1], dtype=jnp.float32), map_mats.shape[1:])

    def compose_advance(carried, pieces):
        return (compose_maps(carried, pieces), None)

    composed, unused_rest = lax.scan(
        compose_advance,
        (identity, jnp.zeros(map_offs.shape[1:], jnp.float32)),
        (map_mats, map_offs),
    )
    return composed


def gate_norm(out_rows, gate_proj, out_gain):
    normed = rms_scale(out_rows, out_gain)
    return (normed * jax.nn.silu(gate_proj.reshape(out_rows.shape))).reshape(gate_proj.shape)


def swiglu(gate_values, up_values):
    return jax.nn.silu(gate_values) * up_values


def add_rims(grad_rows, rim_grad):
    tail_rows = tap_count - 1
    return jnp.concatenate([grad_rows[:-tail_rows], grad_rows[-tail_rows:] + rim_grad], axis=0)


def body(
    tokens,
    attn_gain,
    w_query,
    w_key,
    w_value,
    w_gate_out,
    w_alpha,
    w_beta,
    conv_query,
    conv_key,
    conv_value,
    decay_scale,
    dt_bias,
    out_gain,
    w_out,
    mlp_gain,
    w_mlp_gate,
    w_mlp_up,
    w_mlp_down,
    init_state,
    seg_starts,
    continues,
    cotangent,
):
    axis_size = lax.axis_size("seq")
    my_index = lax.axis_index("seq")
    row_count = tokens.shape[0]
    gathered = (
        lax.all_gather(w_query, "seq", axis=0, tiled=True),
        lax.all_gather(w_key, "seq", axis=0, tiled=True),
        lax.all_gather(w_value, "seq", axis=0, tiled=True),
        lax.all_gather(w_gate_out, "seq", axis=0, tiled=True),
        lax.all_gather(w_alpha, "seq", axis=0, tiled=True),
        lax.all_gather(w_beta, "seq", axis=0, tiled=True),
        lax.all_gather(w_out, "seq", axis=0, tiled=True),
        lax.all_gather(w_mlp_gate, "seq", axis=0, tiled=True),
        lax.all_gather(w_mlp_up, "seq", axis=0, tiled=True),
        lax.all_gather(w_mlp_down, "seq", axis=0, tiled=True),
        lax.all_gather(attn_gain, "seq", axis=0, tiled=True),
        lax.all_gather(mlp_gain, "seq", axis=0, tiled=True),
    )
    (
        full_query,
        full_key,
        full_value,
        full_gate,
        full_alpha,
        full_beta,
        full_out,
        full_mlp_gate,
        full_mlp_up,
        full_mlp_down,
        full_attn_gain,
        full_mlp_gain,
    ) = gathered
    positions = my_index * row_count + jnp.arange(row_count, dtype=jnp.int32)
    tap_keep = tap_masks(positions, seg_starts, continues)
    keep_group = group_masks(positions, seg_starts, continues)
    inputs_f = tokens.astype(jnp.float32)
    normed_one, norm_one_back = jax.vjp(rms_scale, inputs_f, full_attn_gain.astype(jnp.float32))
    normed_low = normed_one.astype(jnp.bfloat16)
    q_proj = project_rows(normed_low, full_query)
    k_proj = project_rows(normed_low, full_key)
    v_proj = project_rows(normed_low, full_value)
    gate_proj = project_rows(normed_low, full_gate)
    alpha_proj = project_rows(normed_low, full_alpha)
    beta_proj = project_rows(normed_low, full_beta)
    tail_rows = tap_count - 1
    rim_send = jnp.concatenate(
        [q_proj[-tail_rows:], k_proj[-tail_rows:], v_proj[-tail_rows:]], axis=1
    )
    rim_rows = passed_along(rim_send, "seq", 1)
    mixed, mixer_back = jax.vjp(
        partial(mixer_inputs, tap_keep=tap_keep),
        q_proj,
        k_proj,
        v_proj,
        rim_rows,
        conv_query,
        conv_key,
        conv_value,
        alpha_proj,
        beta_proj,
        decay_scale,
        dt_bias,
    )
    queries, key_rows, value_rows, log_decay, beta_gate = mixed
    group_parts, terms_back = jax.vjp(
        group_terms,
        group_rows(key_rows),
        group_rows(value_rows),
        group_scalars(log_decay),
        group_scalars(beta_gate),
    )
    map_mats, map_offs = group_maps(group_parts, keep_group)
    map_mat, map_off = compose_groups(map_mats, map_offs)

    def relay_step(turn_index, carried):
        incoming = passed_along(carried[1], "seq", 1)
        begin_state = jnp.where(my_index == 0, init_state, incoming)
        return (begin_state, batch_product(map_mat, begin_state) + map_off)

    start_state, unused_end = lax.fori_loop(
        0, axis_size - 1, relay_step, (init_state, batch_product(map_mat, init_state) + map_off)
    )
    (out_blocks, end_state), pass_back = jax.vjp(
        partial(state_pass, keep_group=keep_group), start_state, group_rows(queries), group_parts
    )
    last_state = jnp.where(my_index == axis_size - 1, end_state, jnp.zeros_like(end_state))
    final_state = lax.psum_scatter(
        last_state.astype(jnp.bfloat16), "seq", scatter_dimension=1, tiled=True
    ).astype(jnp.float32)
    gated_rows, gate_back = jax.vjp(gate_norm, rows_from_groups(out_blocks), gate_proj, out_gain)
    gated_low = gated_rows.astype(jnp.bfloat16)
    attn_terms = project_back(gated_low, full_out)
    middle = inputs_f + lax.psum(attn_terms, "tp")
    normed_two, norm_two_back = jax.vjp(rms_scale, middle, full_mlp_gain.astype(jnp.float32))
    normed_two_low = normed_two.astype(jnp.bfloat16)
    gate_mlp = project_rows(normed_two_low, full_mlp_gate)
    up_mlp = project_rows(normed_two_low, full_mlp_up)
    hidden_rows, swiglu_back = jax.vjp(swiglu, gate_mlp, up_mlp)
    hidden_low = hidden_rows.astype(jnp.bfloat16)
    mlp_terms = project_back(hidden_low, full_mlp_down)
    block_rows = middle + lax.psum(mlp_terms.astype(jnp.bfloat16), "tp").astype(jnp.float32)
    grad_hidden = project_rows(cotangent, full_mlp_down)
    grad_w_mlp_down = weight_grad(cotangent, hidden_low)
    grad_gate_mlp, grad_up_mlp = swiglu_back(grad_hidden)
    grad_gate_low = grad_gate_mlp.astype(jnp.bfloat16)
    grad_up_low = grad_up_mlp.astype(jnp.bfloat16)
    grad_w_mlp_gate = weight_grad(normed_two_low, grad_gate_low)
    grad_w_mlp_up = weight_grad(normed_two_low, grad_up_low)
    grad_normed_terms = project_back(grad_gate_low, full_mlp_gate) + project_back(
        grad_up_low, full_mlp_up
    )
    grad_normed_two = lax.psum(grad_normed_terms, "tp")
    cot_rows = cotangent.astype(jnp.float32)
    grad_middle_norm, grad_mlp_gain_part = norm_two_back(grad_normed_two)
    grad_middle = cot_rows + grad_middle_norm
    block_out = block_rows.astype(jnp.bfloat16)
    grad_attn = grad_middle.astype(jnp.bfloat16)
    grad_gated = project_rows(grad_attn, full_out)
    grad_w_out = weight_grad(grad_attn, gated_low)
    grad_out_rows, grad_gate_proj, grad_out_gain_part = gate_back(grad_gated)
    lead_grad, grad_query_blocks, grad_parts_out = pass_back(
        (group_rows(grad_out_rows), jnp.zeros_like(end_state))
    )
    transposed = jnp.swapaxes(map_mat, 1, 2)

    def relay_back(turn_index, carried):
        incoming = passed_along(carried[1].astype(jnp.bfloat16), "seq", -1).astype(jnp.float32)
        return (incoming, batch_product(transposed, incoming) + lead_grad)

    grad_end, unused_start = lax.fori_loop(
        0, axis_size - 1, relay_back, (jnp.zeros_like(lead_grad), lead_grad)
    )
    unused_state, unused_query, grad_parts_end = pass_back((jnp.zeros_like(out_blocks), grad_end))
    grad_parts = jax.tree.map(jnp.add, grad_parts_out, grad_parts_end)
    grad_key_blocks, grad_value_blocks, grad_decay_blocks, grad_beta_blocks = terms_back(grad_parts)
    mixer_grads = mixer_back(
        (
            rows_from_groups(grad_query_blocks),
            rows_from_groups(grad_key_blocks),
            rows_from_groups(grad_value_blocks),
            scalars_from_groups(grad_decay_blocks),
            scalars_from_groups(grad_beta_blocks),
        )
    )
    (
        grad_q_proj,
        grad_k_proj,
        grad_v_proj,
        grad_rims,
        grad_conv_query,
        grad_conv_key,
        grad_conv_value,
        grad_alpha_proj,
        grad_beta_proj,
        grad_decay_part,
        grad_dt_part,
    ) = mixer_grads
    rim_grad = passed_along(grad_rims, "seq", -1)
    key_width = q_proj.shape[1]
    grad_q_low = add_rims(grad_q_proj, rim_grad[:, :key_width]).astype(jnp.bfloat16)
    grad_k_low = add_rims(grad_k_proj, rim_grad[:, key_width : 2 * key_width]).astype(jnp.bfloat16)
    grad_v_low = add_rims(grad_v_proj, rim_grad[:, 2 * key_width :]).astype(jnp.bfloat16)
    grad_gate_proj_low = grad_gate_proj.astype(jnp.bfloat16)
    grad_alpha_low = grad_alpha_proj.astype(jnp.bfloat16)
    grad_beta_low = grad_beta_proj.astype(jnp.bfloat16)
    grad_normed_part = (
        project_back(grad_q_low, full_query)
        + project_back(grad_k_low, full_key)
        + project_back(grad_v_low, full_value)
    )
    grad_normed_part = (
        grad_normed_part
        + project_back(grad_gate_proj_low, full_gate)
        + project_back(grad_alpha_low, full_alpha)
        + project_back(grad_beta_low, full_beta)
    )
    gain_term = jnp.zeros_like(grad_mlp_gain_part)
    grad_normed, grad_out_gain_tp, gain_summed = (
        lax.psum(grad_normed_part.astype(jnp.bfloat16), "tp").astype(jnp.float32),
        lax.psum(grad_out_gain_part.astype(jnp.bfloat16), "tp").astype(jnp.float32),
        lax.psum(gain_term.astype(jnp.bfloat16), "tp").astype(jnp.float32),
    )
    grad_inputs_norm, grad_attn_gain_part = norm_one_back(grad_normed)
    grad_tokens = grad_middle + grad_inputs_norm
    shards = (
        lax.psum_scatter(
            weight_grad(normed_low, grad_q_low).astype(jnp.bfloat16),
            "seq",
            scatter_dimension=0,
            tiled=True,
        ).astype(jnp.float32),
        lax.psum_scatter(
            weight_grad(normed_low, grad_k_low).astype(jnp.bfloat16),
            "seq",
            scatter_dimension=0,
            tiled=True,
        ).astype(jnp.float32),
        lax.psum_scatter(
            weight_grad(normed_low, grad_v_low).astype(jnp.bfloat16),
            "seq",
            scatter_dimension=0,
            tiled=True,
        ).astype(jnp.float32),
        lax.psum_scatter(
            weight_grad(normed_low, grad_gate_proj_low).astype(jnp.bfloat16),
            "seq",
            scatter_dimension=0,
            tiled=True,
        ).astype(jnp.float32),
        lax.psum_scatter(
            weight_grad(normed_low, grad_alpha_low).astype(jnp.bfloat16),
            "seq",
            scatter_dimension=0,
            tiled=True,
        ).astype(jnp.float32),
        lax.psum_scatter(
            weight_grad(normed_low, grad_beta_low).astype(jnp.bfloat16),
            "seq",
            scatter_dimension=0,
            tiled=True,
        ).astype(jnp.float32),
        lax.psum_scatter(
            grad_w_out.astype(jnp.bfloat16), "seq", scatter_dimension=0, tiled=True
        ).astype(jnp.float32),
        lax.psum_scatter(
            grad_w_mlp_gate.astype(jnp.bfloat16), "seq", scatter_dimension=0, tiled=True
        ).astype(jnp.float32),
        lax.psum_scatter(
            grad_w_mlp_up.astype(jnp.bfloat16), "seq", scatter_dimension=0, tiled=True
        ).astype(jnp.float32),
        lax.psum_scatter(
            grad_w_mlp_down.astype(jnp.bfloat16), "seq", scatter_dimension=0, tiled=True
        ).astype(jnp.float32),
        lax.psum_scatter(
            grad_attn_gain_part.astype(jnp.bfloat16), "seq", scatter_dimension=0, tiled=True
        ).astype(jnp.float32),
        lax.psum_scatter(
            grad_mlp_gain_part.astype(jnp.bfloat16), "seq", scatter_dimension=0, tiled=True
        ).astype(jnp.float32),
    )
    (
        grad_w_query,
        grad_w_key,
        grad_w_value,
        grad_w_gate_out,
        grad_w_alpha,
        grad_w_beta,
        grad_w_out_s,
        grad_w_mlp_gate_s,
        grad_w_mlp_up_s,
        grad_w_mlp_down_s,
        grad_attn_gain,
        grad_mlp_gain_s,
    ) = shards
    smalls = (
        lax.psum(grad_conv_query.astype(jnp.bfloat16), "seq").astype(jnp.float32),
        lax.psum(grad_conv_key.astype(jnp.bfloat16), "seq").astype(jnp.float32),
        lax.psum(grad_conv_value.astype(jnp.bfloat16), "seq").astype(jnp.float32),
        lax.psum(grad_decay_part.astype(jnp.bfloat16), "seq").astype(jnp.float32),
        lax.psum(grad_dt_part.astype(jnp.bfloat16), "seq").astype(jnp.float32),
        lax.psum(grad_out_gain_tp.astype(jnp.bfloat16), "seq").astype(jnp.float32),
    )
    (
        grad_conv_query_s,
        grad_conv_key_s,
        grad_conv_value_s,
        grad_decay_scale,
        grad_dt_bias,
        grad_out_gain,
    ) = smalls
    return (
        block_out,
        final_state,
        grad_tokens,
        grad_attn_gain,
        grad_w_query,
        grad_w_key,
        grad_w_value,
        grad_w_gate_out,
        grad_w_alpha,
        grad_w_beta,
        grad_conv_query_s,
        grad_conv_key_s,
        grad_conv_value_s,
        grad_decay_scale,
        grad_dt_bias,
        grad_out_gain,
        grad_w_out_s,
        grad_mlp_gain_s,
        grad_w_mlp_gate_s,
        grad_w_mlp_up_s,
        grad_w_mlp_down_s,
    )


def solution(mesh):
    in_specs = (
        P("seq", None),
        P("seq"),
        P("seq", "tp"),
        P("seq", "tp"),
        P("seq", "tp"),
        P("seq", "tp"),
        P("seq", "tp"),
        P("seq", "tp"),
        P(None, "tp"),
        P(None, "tp"),
        P(None, "tp"),
        P("tp"),
        P("tp"),
        P(),
        P("seq", "tp"),
        P("seq"),
        P("seq", "tp"),
        P("seq", "tp"),
        P("seq", "tp"),
        P("tp", None, None),
        P(),
        P(),
        P("seq", None),
    )
    out_specs = (
        P("seq", None),
        P("tp", "seq", None),
        P("seq", None),
        P("seq"),
        P("seq", "tp"),
        P("seq", "tp"),
        P("seq", "tp"),
        P("seq", "tp"),
        P("seq", "tp"),
        P("seq", "tp"),
        P(None, "tp"),
        P(None, "tp"),
        P(None, "tp"),
        P("tp"),
        P("tp"),
        P(),
        P("seq", "tp"),
        P("seq"),
        P("seq", "tp"),
        P("seq", "tp"),
        P("seq", "tp"),
    )
    return jax.shard_map(body, mesh=mesh, in_specs=in_specs, out_specs=out_specs, check_vma=False)
```

profile of v0, /device:TPU:0, one launch (start us, length us, event | category | flops | bytes accessed | tf_op | source)
XLA Modules:
  0.0 3656.4 jit_solution(5728110924072308668)
XLA Ops:
  14.6 10.3 all-gather
  25.6 8.9 all_gather.37
  38.8 7.9 all_gather.41
  59.2 11.2 all-gather.11.cloned.1.call-done
  75.6 33.4 all-gather.15.cloned.1.call-done
  109.0 7.5 fusion.280
  131.5 6.6 fusion.266
  156.7 316.0 %custom-call.12 = f32[16,4,1,64,64]{3,4,2,1,0:T(8,128)} custom-call(f32[16,4,1,64,64]{4,3,2,1,0:T(8,128)} %get-tuple-element.2049), custom_call_target="InvertDiagBlocksLowerTriangular" | custom-call | tf_op jit(solution)/shard_map/jvp()/triangular_solve | solution.py:24
  472.7 11.7 fusion.173
  490.1 8.0 fusion.171
  502.3 9.7 fusion.282
  512.0 9.0 subtract_multiply_fusion.3
  521.0 50.8 %while.134 = (s32[]{:T(128)}, f32[4,128,128]{2,1,0:T(8,128)S(1)}, f32[4,128,256]{2,1,0:T(8,128)S(1)}, f32[16,4,128,128]{3,2,1,0:T(8,128)}, f32[16,4,128,256]{3,2,1,0:T(8,128)}) while((s32[]{:T(128)}, f32[4,128,128]{2,1,0:T(8,128)S(1)}, f32[4,128,256]{2,1,0:T(8,128)S(1)}, f32[16,4,128,128]{3,2,1,0:T(8,128)}, ...), condition=%wide.region_10.11_spmd.clone.clone, body=%wide.region_9.10_spmd.clone.sunk.clone | while | flops 302252032 | bytes 4195911 | solution.py:210
  577.2 87.1 %while.130 = (s32[]{:T(128)}, f32[4,128,256]{1,2,0:T(8,128)}, f32[4,128,256]{1,2,0:T(8,128)}, pred[]{:T(512)}, f32[4,128,256]{1,2,0:T(8,128)}, /*index=5*/f32[4,128,128]{2,1,0:T(8,128)S(1)}, f32[4,128,256]{1,2,0:T(8,128)}) while((s32[]{:T(128)}, f32[4,128,256]{1,2,0:T(8,128)}, f32[4,128,256]{1,2,0:T(8,128)}, pred[]{:T(512)}, ...), condition=%wide.region_12.13_spmd.clone, body=%wide.region_11.12_spmd.sunk.clone | while | flops 201588736 | bytes 7602322 | solution.py:335
  597.3 8.0 collective-permute-start
  610.7 8.0 collective-permute-start
  624.1 8.0 collective-permute-start
  637.5 8.0 collective-permute-start
  651.0 8.0 collective-permute-start
  683.3 367.4 %while.131 = (s32[]{:T(128)}, f32[4,128,256]{2,1,0:T(8,128)S(1)}, f32[16,4,64,256]{3,2,1,0:T(8,128)}, f32[16,4,128,256]{3,2,1,0:T(8,128)}, f32[16,4,64,64]{3,2,1...) while((s32[]{:T(128)}, f32[4,128,256]{2,1,0:T(8,128)S(1)}, ...), condition=%wide.region_15.16_spmd.clone, body=%wide.region_14.15_spmd.sunk.clone | while | flops 378503168 | bytes 7115097 | solution.py:184
  1065.1 12.9 multiply_convert_fusion.3
  1078.0 9.7 fusion.283
  1090.1 22.2 all-gather.1
  1112.2 279.8 %all-reduce.35.cloned.1.call-done = f32[1024,2048]{1,0:T(8,128)} async-done(((f32[1024,2048]{1,0:T(8,128)}), f32[1024,2048]{1,0:T(8,128)}) %all-reduce.35.cloned.1.call-update) | async-done | bytes 8388624 | tf_op jit(solution)/shard_map/psum | solution.py:348
  1403.9 32.9 all-gather.21.cloned.1.call-done
  1436.8 11.0 fusion.284
  1447.8 34.7 all-gather.23.cloned.1.call-done
  1482.5 10.8 fusion.285
  1493.3 34.9 all-gather.25.cloned.1.call-done
  1528.2 14.9 multiply_convert_fusion.1
  1543.1 11.1 fusion.286
  1554.2 9.6 convolution_add_fusion.11
  1570.5 284.3 %all-reduce.37.cloned.1.call-done = f32[1024,2048]{1,0:T(8,128)} async-done(((f32[1024,2048]{1,0:T(8,128)}), f32[1024,2048]{1,0:T(8,128)}) %all-reduce.37.cloned.1.call-update) | async-done | bytes 8388624 | tf_op jit(solution)/shard_map/psum | solution.py:367
  1854.8 7.7 multiply_reduce_fusion.1
  1869.2 13.9 fusion.169
  1888.7 7.4 multiply_reduce_fusion.4
  1909.3 412.1 %while.135 = (s32[]{:T(128)}, f32[4,128,256]{2,1,0:T(8,128)S(1)}, f32[16,4,64,128]{3,2,1,0:T(8,128)}, f32[16,4,64]{2,0,1:T(8,128)S(1)}, f32[16,4,64,64]{3,2,1,0:...) while((s32[]{:T(128)}, f32[4,128,256]{2,1,0:T(8,128)S(1)}, ...), condition=%wide.region_27.28_spmd.clone.clone, body=%wide.region_24.27_spmd.clone.sunk.clone | while | flops 756826368 | bytes 11294724 | solution.py:184
  2321.4 57.4 %while.132 = (s32[]{:T(128)}, f32[4,128,256]{2,1,0:T(8,128)}, bf16[4,128,256]{2,1,0:T(8,128)(2,1)S(1)}, f32[4,128,128]{2,1,0:T(8,128)S(1)}, f32[4,128,256]{2,1,0:T(8,128)S(1)}) while((s32[]{:T(128)}, f32[4,128,256]{2,1,0:T(8,128)}, bf16[4,128,256]{2,1,0:T(8,128)(2,1)S(1)}, f32[4,128,128]{2,1,0:T(8,128)S(1)}, ...), condition=%wide.region_30.31_spmd.clone, body=%wide.region_29.30_spmd.sunk.clone | while | flops 201719808 | bytes 3145829 | solution.py:385
  2335.7 6.4 collective-permute-done.1
  2387.8 344.9 %while.133 = (s32[]{:T(128)}, f32[4,128,256]{2,1,0:T(8,128)S(1)}, f32[16,4,64]{2,0,1:T(8,128)S(1)}, f32[16,4,64,64]{3,2,1,0:T(8,128)}, f32[16,4,64,256]{3,2,1,0:...) while((s32[]{:T(128)}, f32[4,128,256]{2,1,0:T(8,128)S(1)}, ...), condition=%wide.region_34.35_spmd.clone, body=%wide.region_31.34_spmd.sunk.clone | while | flops 630292992 | bytes 8666597 | solution.py:184
  2732.7 12.0 fusion.172
  2763.6 10.4 multiply_reduce_fusion.19
  2785.8 10.3 convolution_convert_fusion.1
  2796.2 10.3 convolution_convert_fusion
  2807.4 10.2 fusion.157
  2817.8 6.6 fusion.213
  2900.1 9.7 convolution_convert_fusion.4
  2911.4 8.3 convolution_convert_fusion.5
  2920.4 8.2 fusion.170
  2937.4 11.7 convolution_convert_fusion.3
  2954.3 6.9 fusion.287
  2972.4 6.9 fusion.214
  2979.3 16.8 add_convert_fusion
  2999.4 9.9 psum.86
  3017.3 32.3 reduce-scatter.32.cloned.1.call-done
  3051.9 42.4 %reduce-scatter.20.cloned.1.call-done = bf16[256,512]{1,0:T(8,128)(2,1)} async-done(((bf16[2048,512]{1,0:T(8,128)(2,1)}), bf16[256,512]{1,0:T(8,128)(2,1)}) %reduce-scatter.20.cloned.1.call-update) | async-done | bytes 262160 | tf_op jit(solution)/shard_map/reduce_scatter | solution.py:447
  3096.1 42.6 %reduce-scatter.18.cloned.1.call-done = bf16[256,512]{1,0:T(8,128)(2,1)} async-done(((bf16[2048,512]{1,0:T(8,128)(2,1)}), bf16[256,512]{1,0:T(8,128)(2,1)}) %reduce-scatter.18.cloned.1.call-update) | async-done | bytes 262160 | tf_op jit(solution)/shard_map/reduce_scatter | solution.py:441
  3140.5 53.3 %reduce-scatter.26.cloned.1.call-done = bf16[256,1024]{1,0:T(8,128)(2,1)} async-done(((bf16[2048,1024]{1,0:T(8,128)(2,1)}), bf16[256,1024]{1,0:T(8,128)(2,1)}) %reduce-scatter.26.cloned.1.call-update) | async-done | bytes 524304 | tf_op jit(solution)/shard_map/reduce_scatter | solution.py:477
  3195.9 52.4 %reduce-scatter.24.cloned.1.call-done = bf16[256,1024]{1,0:T(8,128)(2,1)} async-done(((bf16[2048,1024]{1,0:T(8,128)(2,1)}), bf16[256,1024]{1,0:T(8,128)(2,1)}) %reduce-scatter.24.cloned.1.call-update) | async-done | bytes 524304 | tf_op jit(solution)/shard_map/reduce_scatter | solution.py:459
  3250.4 53.0 %reduce-scatter.22.cloned.1.call-done = bf16[256,1024]{1,0:T(8,128)(2,1)} async-done(((bf16[2048,1024]{1,0:T(8,128)(2,1)}), bf16[256,1024]{1,0:T(8,128)(2,1)}) %reduce-scatter.22.cloned.1.call-update) | async-done | bytes 524304 | tf_op jit(solution)/shard_map/reduce_scatter | solution.py:453
  3305.5 292.6 %all-reduce.39.cloned.1.call-done = (bf16[1024,2048]{1,0:T(8,128)(2,1)}, bf16[1024,2048]{1,0:T(8,128)(2,1)}) async-done(((bf16[1024,2048]{1,0:T(8,128)(2,1)}, bf16[1024,2048]{1,0:T(8,128)(2,1)}), (bf16[1024,2048]{1,0:T(8,128)(2,1)}, bf16[1024,2048]{1,0:T(8,128)(2,1)})) %all-reduce.39.cloned.1.call-update) | async-done | bytes 8388624 | tf_op jit(solution)/shard_map/psum | solution.py:356
  3604.1 24.1 all-reduce.29
  3632.8 9.7 fusion.154
  3642.5 6.9 add_convert_fusion.1
  (1752 shorter events, 1603.9 us)
Async XLA Ops:
  7.2 45.4 %all-gather.13.cloned.1.call-start = ((), (), s32[]{:S(2)}) async-start(), calls=%async_computation.12 | async-start | bytes 2359296 | tf_op jit(solution)/shard_map/all_gather | solution.py:261
  7.9 62.4 %all-gather.11.cloned.1.call-start = ((), (), s32[]{:S(2)}) async-start(), calls=%async_computation.11 | async-start | bytes 2359296 | tf_op jit(solution)/shard_map/all_gather | solution.py:262
  8.7 100.3 %all-gather.15.cloned.1.call-start = ((), (), s32[]{:S(2)}) async-start(), calls=%async_computation.13 | async-start | bytes 4718592 | tf_op jit(solution)/shard_map/all_gather | solution.py:263
  9.4 1055.7 %all-gather.17.cloned.1.call-start = ((), (), s32[]{:S(2)}) async-start(), calls=%async_computation.14 | async-start | bytes 4718592 | tf_op jit(solution)/shard_map/all_gather | solution.py:264
  10.0 1068.0 %all-gather.19.cloned.1.call-start = ((), (), s32[]{:S(2)}) async-start(), calls=%async_computation.15 | async-start | bytes 4718592 | tf_op jit(solution)/shard_map/all_gather | solution.py:267
  10.6 1381.5 %all-reduce.35.cloned.1.call-start = ((), (), s32[]{:S(2)}) async-start(), calls=%async_computation.16 | async-start | bytes 16777216 | tf_op jit(solution)/shard_map/psum | solution.py:348
  10.8 23.7 copy-start.160
  10.8 23.7 copy-start.9
  25.6 97.1 %copy-start.125 = (f32[1,512]{1,0:T(1,128)}, f32[1,512]{1,0:T(1,128)S(1)}, u32[]{:S(2)}) copy-start(f32[1,512]{1,0:T(1,128)S(1)} %get-tuple-element.2071) | copy-start | bytes 6148
  25.6 97.1 %copy-start.127 = (f32[1,512]{1,0:T(1,128)}, f32[1,512]{1,0:T(1,128)S(1)}, u32[]{:S(2)}) copy-start(f32[1,512]{1,0:T(1,128)S(1)} %get-tuple-element.2072) | copy-start | bytes 6148
  38.6 80.4 %copy-start.60 = (f32[16,4,64]{2,0,1:T(8,128)}, f32[16,4,64]{2,0,1:T(8,128)S(1)}, u32[]{:S(2)}) copy-start(f32[16,4,64]{2,0,1:T(8,128)S(1)} %reduce_window_sum.22) | copy-start | bytes 49156
  38.8 80.2 %copy-start.111 = (f32[16,4]{0,1:T(4,128)}, f32[16,4]{0,1:T(4,128)S(1)}, u32[]{:S(2)}) copy-start(f32[16,4]{0,1:T(4,128)S(1)} %slice_reduce_fusion) | copy-start | bytes 772
  50.3 68.9 %copy-start.66 = (f32[16,64,4]{1,0,2:T(8,128)}, f32[16,64,4]{1,0,2:T(8,128)S(1)}, u32[]{:S(2)}) copy-start(f32[16,64,4]{1,0,2:T(8,128)S(1)} %reshape.539) | copy-start | bytes 49156
  50.3 103.7 %copy-start.107 = (pred[64,64]{1,0:T(8,128)(4,1)}, pred[64,64]{1,0:T(8,128)(4,1)S(1)}, u32[]{:S(2)}) copy-start(pred[64,64]{1,0:T(8,128)(4,1)S(1)} %get-tuple-element.2093) | copy-start | bytes 12292
  50.4 422.3 %copy-start.113 = (f32[1,1024]{1,0:T(1,128)}, f32[1,1024]{1,0:T(1,128)S(1)}, u32[]{:S(2)}) copy-start(f32[1,1024]{1,0:T(1,128)S(1)} %get-tuple-element.2060) | copy-start | bytes 12292
  50.4 422.3 %copy-start.115 = (f32[1,1024]{1,0:T(1,128)}, f32[1,1024]{1,0:T(1,128)S(1)}, u32[]{:S(2)}) copy-start(f32[1,1024]{1,0:T(1,128)S(1)} %get-tuple-element.2061) | copy-start | bytes 12292
  50.4 422.3 %copy-start.117 = (f32[1,1024]{1,0:T(1,128)}, f32[1,1024]{1,0:T(1,128)S(1)}, u32[]{:S(2)}) copy-start(f32[1,1024]{1,0:T(1,128)S(1)} %get-tuple-element.2062) | copy-start | bytes 12292
  50.4 422.3 %copy-start.121 = (f32[1,1024]{1,0:T(1,128)}, f32[1,1024]{1,0:T(1,128)S(1)}, u32[]{:S(2)}) copy-start(f32[1,1024]{1,0:T(1,128)S(1)} %get-tuple-element.2059) | copy-start | bytes 12292
  51.1 80.4 %copy-start.123 = (f32[1,512]{1,0:T(1,128)}, f32[1,512]{1,0:T(1,128)S(1)}, u32[]{:S(2)}) copy-start(f32[1,512]{1,0:T(1,128)S(1)} %get-tuple-element.2066) | copy-start | bytes 6148
  52.5 420.2 %copy-start.72 = (f32[1024]{0:T(1024)}, f32[1024]{0:T(1024)S(1)}, u32[]{:S(2)}) copy-start(f32[1024]{0:T(1024)S(1)} %get-tuple-element.2074) | copy-start | bytes 12292
  52.5 420.2 %copy-start.74 = (f32[1024]{0:T(1024)}, f32[1024]{0:T(1024)S(1)}, u32[]{:S(2)}) copy-start(f32[1024]{0:T(1024)S(1)} %get-tuple-element.2075) | copy-start | bytes 12292
  52.5 420.2 %copy-start.76 = (f32[1024]{0:T(1024)}, f32[1024]{0:T(1024)S(1)}, u32[]{:S(2)}) copy-start(f32[1024]{0:T(1024)S(1)} %get-tuple-element.2076) | copy-start | bytes 12292
  75.6 47.2 %copy-start.46 = (f32[1024,512]{1,0:T(8,128)}, f32[1024,512]{1,0:T(8,128)S(1)}, u32[]{:S(2)}) copy-start(f32[1024,512]{1,0:T(8,128)S(1)} %fusion.278) | copy-start | bytes 6291460
  116.6 6.1 collective-permute-start.2
  119.0 35.1 copy-start.78
  119.0 35.1 copy-start.105
  119.0 35.0 copy-start.56
  119.1 28.0 copy-start.68
  119.2 370.9 %copy-start.62 = (f32[16,4,64]{2,1,0:T(4,128)}, f32[16,4,64]{2,1,0:T(4,128)S(1)}, u32[]{:S(2)}) copy-start(f32[16,4,64]{2,1,0:T(4,128)S(1)} %copy.393) | copy-start | bytes 49156
  119.2 378.9 %copy-start.70 = (f32[16,4,64]{2,1,0:T(4,128)}, f32[16,4,64]{2,1,0:T(4,128)S(1)}, u32[]{:S(2)}) copy-start(f32[16,4,64]{2,1,0:T(4,128)S(1)} %copy.398) | copy-start | bytes 49156
  577.2 4.9 collective-permute-start
  585.9 7.6 collective-permute-start
  597.3 9.7 collective-permute-start
  610.7 9.7 collective-permute-start
  624.1 9.7 collective-permute-start
  637.5 9.7 collective-permute-start
  651.0 9.7 collective-permute-start
  1087.8 349.0 %all-gather.21.cloned.1.call-start = ((), (), s32[]{:S(2)}) async-start(), calls=%async_computation.17 | async-start | bytes 6340608 | tf_op jit(solution)/shard_map/all_gather | solution.py:268
  1088.5 393.9 %all-gather.23.cloned.1.call-start = ((), (), s32[]{:S(2)}) async-start(), calls=%async_computation.18 | async-start | bytes 6340608 | tf_op jit(solution)/shard_map/all_gather | solution.py:269
  1089.3 438.9 %all-gather.25.cloned.1.call-start = ((), (), s32[]{:S(2)}) async-start(), calls=%async_computation.19 | async-start | bytes 6340608 | tf_op jit(solution)/shard_map/all_gather | solution.py:270
  1090.0 764.9 %all-reduce.37.cloned.1.call-start = ((), (), s32[]{:S(2)}) async-start(), calls=%async_computation.21 | async-start | bytes 16777216 | tf_op jit(solution)/shard_map/psum | solution.py:367
  1563.9 1434.2 %reduce-scatter.16.cloned.1.call-start = ((), (), s32[]{:S(2)}) async-start(), calls=%async_computation.20 | async-start | bytes 294912 | tf_op jit(solution)/shard_map/reduce_scatter | solution.py:342
  1570.5 1438.9 %reduce-scatter.36.cloned.1.call-start = ((), (), s32[]{:S(2)}) async-start(), calls=%async_computation.31 | async-start | bytes 589824
  2321.5 3.4 collective-permute-start.1
  2326.1 7.1 collective-permute-start.1
  2334.4 7.7 collective-permute-start.1
  2343.3 7.7 collective-permute-start.1
  2352.2 7.7 collective-permute-start.1
  2361.1 7.7 collective-permute-start.1
  2370.0 7.7 collective-permute-start.1
  2781.8 229.2 %reduce-scatter.34.cloned.1.call-start = ((), (), s32[]{:S(2)}) async-start(), calls=%async_computation.30 | async-start | bytes 589824
  2785.8 226.7 %reduce-scatter.28.cloned.1.call-start = ((), (), s32[]{:S(2)}) async-start(), calls=%async_computation.27 | async-start | bytes 6340608 | tf_op jit(solution)/shard_map/reduce_scatter | solution.py:480
  2796.1 218.7 %reduce-scatter.30.cloned.1.call-start = ((), (), s32[]{:S(2)}) async-start(), calls=%async_computation.28 | async-start | bytes 6340608 | tf_op jit(solution)/shard_map/reduce_scatter | solution.py:483
  2806.5 243.1 %reduce-scatter.32.cloned.1.call-start = ((), (), s32[]{:S(2)}) async-start(), calls=%async_computation.29 | async-start | bytes 6340608 | tf_op jit(solution)/shard_map/reduce_scatter | solution.py:486
  2817.7 276.6 %reduce-scatter.20.cloned.1.call-start = ((), (), s32[]{:S(2)}) async-start(), calls=%async_computation.23 | async-start | bytes 2359296 | tf_op jit(solution)/shard_map/reduce_scatter | solution.py:447
  2880.2 7.0 collective-permute-start.3
  2891.0 247.7 %reduce-scatter.18.cloned.1.call-start = ((), (), s32[]{:S(2)}) async-start(), calls=%async_computation.22 | async-start | bytes 2359296 | tf_op jit(solution)/shard_map/reduce_scatter | solution.py:441
  2898.6 295.2 %reduce-scatter.26.cloned.1.call-start = ((), (), s32[]{:S(2)}) async-start(), calls=%async_computation.26 | async-start | bytes 4718592 | tf_op jit(solution)/shard_map/reduce_scatter | solution.py:477
  2909.8 338.5 %reduce-scatter.24.cloned.1.call-start = ((), (), s32[]{:S(2)}) async-start(), calls=%async_computation.25 | async-start | bytes 4718592 | tf_op jit(solution)/shard_map/reduce_scatter | solution.py:459
  2919.8 383.6 %reduce-scatter.22.cloned.1.call-start = ((), (), s32[]{:S(2)}) async-start(), calls=%async_computation.24 | async-start | bytes 4718592 | tf_op jit(solution)/shard_map/reduce_scatter | solution.py:453
  2937.2 660.9 %all-reduce.39.cloned.1.call-start = ((), (), s32[]{:S(2)}) async-start(), calls=%async_computation.32 | async-start | bytes 16777216 | tf_op jit(solution)/shard_map/psum | solution.py:356
  3140.5 457.6 %copy-start.95 = (f32[8,1,256]{2,1,0:T(1,128)S(1)}, f32[8,1,256]{2,1,0:T(1,128)}, u32[]{:S(2)}) copy-start(f32[8,1,256]{2,1,0:T(1,128)} %copy-done.94) | copy-start | bytes 24580
  3140.5 457.6 %copy-start.110 = (f32[1024]{0:T(1024)S(1)}, f32[1024]{0:T(1024)}, u32[]{:S(2)}) copy-start(f32[1024]{0:T(1024)} %copy-done.109) | copy-start | bytes 12292
  3598.1 34.7 copy-start.120
  (163 other events, 831.0 us)
Sparse Core Ops, SparseCore 0:
  9.9 30.6 all-gather.12
  42.5 27.8 all-gather.10
  72.3 36.7 all-gather.14
  110.8 36.8 all-gather.16
  149.4 36.8 all-gather.18
  1087.9 304.1 all-reduce.34
  1393.9 42.7 all-gather.20
  1438.6 43.7 all-gather.22
  1484.3 43.7 all-gather.24
  1564.0 290.8 all-reduce.36
  1858.4 32.6 reduce-scatter.15
  2781.9 42.9 reduce-scatter.35
  2828.6 34.1 reduce-scatter.33
  2866.5 58.6 reduce-scatter.27
  2928.9 58.4 reduce-scatter.29
  2991.1 58.4 reduce-scatter.31
  3053.1 41.1 reduce-scatter.19
  3097.4 41.1 reduce-scatter.17
  3142.4 51.3 reduce-scatter.25
  3197.0 51.2 reduce-scatter.23
  3252.0 51.3 reduce-scatter.21
  3306.6 291.4 all-reduce.38
where the time goes:
time: 3690 us; the launch traced here: 3660 us
  waiting for transfers between devices  1340 us (36%)
  matrix products  1160 us (31%)
  other arithmetic  635 us (17%)
  local copies, waits for them, and re-layouts  354 us (10%)
  blocking collectives  83.2 us (2%)
  starting transfers between devices  63 us (2%)
    dot_general x271, matrix products, batch_product(): jnp.einsum('...ij,...jk->...ik', left, right, precision=full_precision)  561 us
    another operation x4, other arithmetic, lower_solve(): lax.linalg.triangular_solve(matrix, rhs, left_side=True, lower=True, unit...  316 us
    psum x1, waiting for transfers between devices, body(): lax.psum(mlp_terms.astype(jnp.bfloat16), 'tp').astype(jnp.float32)  293 us
    psum x1, waiting for transfers between devices, body(): grad_normed_two = lax.psum(grad_normed_terms, 'tp')  284 us
    psum x1, waiting for transfers between devices, body(): middle = inputs_f + lax.psum(attn_terms, 'tp')  280 us
    dot_general x80, matrix products, group_apply(): jnp.einsum('...ck,...cv->...kv', key_tail, fresh_values, precision=full_p...  151 us
    dot_general x64, matrix products, group_apply(): jnp.einsum('...ik,...jk->...ij', query_block, key_rows, precision=full_pr...  114 us
    dot_general x10, matrix products, project_back(): jnp.einsum('tc,dc->td', left, right, preferred_element_type=jnp.float32)  89.1 us
  transfers between devices with their start and end apart: 38, of which 29 were waited for; matrix products, arithmetic and copies ran while one was open for 56% of the time, Pallas kernels for 0%

commit v1 on v0

v1 whole, which is shorter than its diff:
```python
from functools import partial

import jax
import jax.numpy as jnp
from jax import lax
from jax.experimental import pallas as pl
from jax.experimental.pallas import tpu as pltpu
from jax.sharding import PartitionSpec as P

DK = 128
DV = 256
DOC_STEP = 64
BLOCK = 128
WIDE = DK + DV
eps = 1e-06
f32 = jnp.float32
bf16 = jnp.bfloat16
CLOSED = -128.0


def low(v):
    return v.astype(bf16)


def mm(a, b):
    return lax.dot_general(low(a), low(b), (((1,), (0,)), ((), ())), preferred_element_type=f32)


def mm_t(a, b):
    return lax.dot_general(low(a), low(b), (((1,), (1,)), ((), ())), preferred_element_type=f32)


def t_mm(a, b):
    return lax.dot_general(low(a), low(b), (((0,), (0,)), ((), ())), preferred_element_type=f32)


def exact_mm(a, b):
    return lax.dot_general(
        a, b, (((1,), (0,)), ((), ())), precision=lax.Precision.HIGHEST, preferred_element_type=f32
    )


def sigmoid(v):
    return 1.0 / (1.0 + jnp.exp(-v))


def square_ids():
    return (
        lax.broadcasted_iota(jnp.int32, (BLOCK, BLOCK), 0),
        lax.broadcasted_iota(jnp.int32, (BLOCK, BLOCK), 1),
    )


def softplus(v):
    return jnp.maximum(v, 0.0) + jnp.log(1.0 + jnp.exp(-jnp.abs(v)))


def decay_rows(ab, hp, keep_a, keep_b, heads):
    lane = lax.broadcasted_iota(jnp.int32, (heads, BLOCK), 1)
    opens = ((lane == 0) & (keep_a < 0.5)) | ((lane == DOC_STEP) & (keep_b < 0.5))
    moved = ab[:heads] + hp[heads:]
    log_decay = jnp.where(opens, CLOSED, -hp[:heads] * softplus(moved))
    return log_decay, sigmoid(ab[heads:]), moved, opens


def to_column(row, diag):
    return jnp.sum(jnp.where(diag, row, 0.0), axis=1, keepdims=True)


def to_row(column, diag):
    return jnp.sum(jnp.where(diag, column, 0.0), axis=0, keepdims=True)


def tap_mask(tap, keep_a, keep_b):
    row = lax.broadcasted_iota(jnp.int32, (BLOCK, DK), 0)
    inner = (row >= DOC_STEP) & (row < DOC_STEP + tap)
    return jnp.where(row < tap, keep_a, jnp.where(inner, keep_b, 1.0))


def tap_mask_back(tap, keep_b):
    row = lax.broadcasted_iota(jnp.int32, (BLOCK, DK), 0)
    return jnp.where((row >= DOC_STEP - tap) & (row < DOC_STEP), keep_b, 1.0)


def conv_total(rows_ref, taps_ref, col, masks):
    cols = slice(col, col + DK)
    total = rows_ref[8 : 8 + BLOCK, cols] * taps_ref[0:1, cols]
    for tap in range(1, 4):
        total = total + rows_ref[8 - tap : 8 - tap + BLOCK, cols] * masks[tap] * taps_ref[
            tap : tap + 1, cols
        ]
    return total


def inverse_lower(a_list, row, col):
    eye = (row == col).astype(f32)
    low_a = [low(a) for a in a_list]
    base = (row >> 3) == (col >> 3)
    x1 = [jnp.where(base, -a, 0.0) for a in a_list]
    x2 = [mm(x, x) for x in x1]
    t = [eye + x + y + mm(x, y) for x, y in zip(x1, x2)]
    x4 = [mm(x, x) for x in x2]
    t = [v + mm(v, x) for v, x in zip(t, x4)]
    for level in (3, 4, 5, 6):
        off = ((row >> (level + 1)) == (col >> (level + 1))) & ((row >> level) != (col >> level))
        part = [mm(jnp.where(off, a, 0.0), v) for a, v in zip(a_list, t)]
        t = [v - mm(v, p) for v, p in zip(t, part)]
    head = [low(v) for v in t]
    tail = [low(v - h.astype(f32)) for v, h in zip(t, head)]
    left = [eye - v - mm(a, h) - mm(a, s) for v, a, h, s in zip(t, low_a, head, tail)]
    return [v + mm(h, r) for v, h, r in zip(t, head, left)]


def load_rows(rows_ref, x_ref, halo_ref, rim_ref, first):
    rows_ref[0:8, :] = jnp.where(first, rim_ref[...], halo_ref[...])
    rows_ref[8 : 8 + BLOCK, :] = x_ref[...]


def unit(v, factor):
    scale = lax.rsqrt(jnp.sum(v * v, axis=1, keepdims=True) + eps) * factor
    return v * scale, scale


def silu(v):
    s = sigmoid(v)
    return v * s, s


def forward_kernel(
    heads,
    keep_ref,
    hp_ref,
    ab_ref,
    x_ref,
    halo_ref,
    rim_ref,
    taps_ref,
    gb_ref,
    t_ref,
    u_ref,
    w_ref,
    pre_ref,
    qf_ref,
    ob_ref,
    map_ref,
    rows_ref,
    state_ref,
):
    c = pl.program_id(0)
    hs = range(heads)
    row, col = square_ids()
    diag = row == col

    @pl.when(c == 0)
    def _():
        for h in hs:
            state_ref[h] = jnp.concatenate(
                [diag.astype(f32), jnp.zeros((DK, DV), f32)], axis=1
            )

    load_rows(rows_ref, x_ref, halo_ref, rim_ref, c == 0)
    keep_a, keep_b = keep_ref[2 * c], keep_ref[2 * c + 1]
    log_decay, beta, _, _ = decay_rows(ab_ref[...], hp_ref[...], keep_a, keep_b, heads)
    cum = exact_mm(log_decay, (row <= col).astype(f32))
    gb_ref[...] = jnp.concatenate([cum, beta], axis=0)
    masks = [None] + [tap_mask(j, keep_a, keep_b) for j in (1, 2, 3)]
    key_at, value_at = heads * DK, 2 * heads * DK

    keys = [
        unit(silu(conv_total(rows_ref, taps_ref, key_at + h * DK, masks))[0], 1.0)[0] for h in hs
    ]
    g_row = [cum[h : h + 1] for h in hs]
    g_col = [to_column(g_row[h], diag) for h in hs]
    b_col = [to_column(beta[h : h + 1], diag) for h in hs]
    decay = [jnp.exp(jnp.where(row >= col, g_col[h] - g_row[h], -1e30)) for h in hs]
    grams = [mm_t(k, k) for k in keys]
    a = [jnp.where(row > col, b_col[h] * decay[h] * grams[h], 0.0) for h in hs]
    t = [low(v) for v in inverse_lower(a, row, col)]
    values = [
        jnp.concatenate(
            [
                silu(conv_total(rows_ref, taps_ref, value_at + h * DV + s * DK, masks))[0]
                for s in range(DV // DK)
            ],
            axis=1,
        )
        for h in hs
    ]
    u = [mm(t[h], b_col[h] * values[h]) for h in hs]
    grow = [jnp.exp(g) for g in g_col]
    w = [low(mm(t[h], (b_col[h] * grow[h]) * keys[h])) for h in hs]
    queries = [
        unit(silu(conv_total(rows_ref, taps_ref, h * DK, masks))[0], DK ** (-0.5))[0] for h in hs
    ]
    scores = [low(mm_t(queries[h], keys[h]) * decay[h]) for h in hs]
    last = [cum[h : h + 1, BLOCK - 1 : BLOCK] for h in hs]
    tail = [low(jnp.exp(last[h] - g_col[h]) * keys[h]) for h in hs]
    state = [state_ref[h] for h in hs]
    low_state = [low(s) for s in state]
    fresh = [
        jnp.concatenate([jnp.zeros((BLOCK, DK), f32), u[h]], axis=1) - mm(w[h], low_state[h])
        for h in hs
    ]
    low_fresh = [low(v) for v in fresh]
    for h in hs:
        new = jnp.exp(last[h]) * state[h] + t_mm(tail[h], low_fresh[h])
        state_ref[h] = new
        map_ref[h] = low(new)
    both = [mm(grow[h] * queries[h], low_state[h]) + mm(scores[h], low_fresh[h]) for h in hs]
    for h in hs:
        t_ref[0, h] = t[h]
        u_ref[:, h * DV : (h + 1) * DV] = low(u[h])
        w_ref[:, h * DK : (h + 1) * DK] = w[h]
        pre_ref[0, h] = low_state[h]
        qf_ref[:, h * DK : (h + 1) * DK] = low(both[h][:, :DK])
        ob_ref[:, h * DV : (h + 1) * DV] = both[h][:, DK:]


def const_spec(shape):
    return pl.BlockSpec(shape, lambda c: (0,) * len(shape))


def params():
    return pltpu.CompilerParams(
        dimension_semantics=("arbitrary",), vmem_limit_bytes=56 * 1024 * 1024
    )


SMEM = pl.BlockSpec(memory_space=pltpu.SMEM)


ANY = pl.BlockSpec(memory_space=pl.ANY)


def ordered(kernel, first, extra):
    def run(*refs):
        return kernel(*refs[:first], *refs[first + extra :])

    return run


def cost(us):
    return pl.CostEstimate(
        flops=int(us * 1.0e9), bytes_accessed=int(us * 1.0e6), transcendentals=0
    )


def forward_local(keep, hp, ab, proj, rim, taps, after=()):
    heads = hp.shape[0] // 2
    length = proj.shape[0]
    blocks = length // BLOCK
    kd, vd = heads * DK, heads * DV
    width = 2 * kd + vd
    shape = jax.ShapeDtypeStruct
    return pl.pallas_call(
        ordered(partial(forward_kernel, heads), 7, len(after)),
        grid=(blocks,),
        in_specs=[
            SMEM,
            const_spec((2 * heads, BLOCK)),
            pl.BlockSpec((2 * heads, BLOCK), lambda c: (0, c)),
            pl.BlockSpec((BLOCK, width), lambda c: (c, 0)),
            pl.BlockSpec((8, width), lambda c: (jnp.maximum(c * (BLOCK // 8) - 1, 0), 0)),
            const_spec((8, width)),
            const_spec((4, width)),
        ]
        + [ANY] * len(after),
        out_specs=[
            pl.BlockSpec((2 * heads, BLOCK), lambda c: (0, c)),
            pl.BlockSpec((1, heads, BLOCK, BLOCK), lambda c: (c, 0, 0, 0)),
            pl.BlockSpec((BLOCK, vd), lambda c: (c, 0)),
            pl.BlockSpec((BLOCK, kd), lambda c: (c, 0)),
            pl.BlockSpec((1, heads, DK, WIDE), lambda c: (c, 0, 0, 0)),
            pl.BlockSpec((BLOCK, kd), lambda c: (c, 0)),
            pl.BlockSpec((BLOCK, vd), lambda c: (c, 0)),
            const_spec((heads, DK, WIDE)),
        ],
        out_shape=[
            shape((2 * heads, length), f32),
            shape((blocks, heads, BLOCK, BLOCK), bf16),
            shape((length, vd), bf16),
            shape((length, kd), bf16),
            shape((blocks, heads, DK, WIDE), bf16),
            shape((length, kd), bf16),
            shape((length, vd), f32),
            shape((heads, DK, WIDE), bf16),
        ],
        scratch_shapes=[
            pltpu.VMEM((8 + BLOCK, width), f32),
            pltpu.VMEM((heads, DK, WIDE), f32),
        ],
        compiler_params=params(),
        cost_estimate=cost(30),
        name="delta_forward",
    )(keep, hp, ab, proj, proj, rim, taps, *after)


def out_norm(ob, qf, start, gain):
    out = ob + mm(qf, start)
    inv = lax.rsqrt(jnp.mean(out * out, axis=1, keepdims=True) + eps)
    return out, inv


def gate_kernel(
    heads, place_ref, maps_ref, init_ref, ob_ref, qf_ref, gate_ref, gain_ref,
    gated_ref, start_ref, final_ref,
):
    c = pl.program_id(0)
    hs = range(heads)

    @pl.when(c == 0)
    def _():
        def step(p, states):
            return tuple(
                mm(maps_ref[p, h, :, :DK], states[h]) + maps_ref[p, h, :, DK:].astype(f32)
                for h in hs
            )

        begin = lax.fori_loop(0, place_ref[0], step, tuple(init_ref[h] for h in hs))
        for h in hs:
            start_ref[h] = begin[h]
        end = lax.fori_loop(place_ref[0], place_ref[1], step, begin)
        for h in hs:
            final_ref[h] = end[h]

    for h in hs:
        vs = slice(h * DV, (h + 1) * DV)
        out, inv = out_norm(
            ob_ref[:, vs], qf_ref[:, h * DK : (h + 1) * DK], start_ref[h], gain_ref[...]
        )
        gated_ref[:, vs] = low(out * inv * gain_ref[...] * silu(gate_ref[:, vs])[0])


def gate_forward(place, maps, init_state, ob, qf, gate_proj, gain, after=()):
    heads = init_state.shape[0]
    length, vd = ob.shape
    kd = heads * DK
    rows = 256
    shape = jax.ShapeDtypeStruct
    return pl.pallas_call(
        ordered(partial(gate_kernel, heads), 7, len(after)),
        grid=(length // rows,),
        in_specs=[
            SMEM,
            const_spec(maps.shape),
            const_spec(init_state.shape),
            pl.BlockSpec((rows, vd), lambda c: (c, 0)),
            pl.BlockSpec((rows, kd), lambda c: (c, 0)),
            pl.BlockSpec((rows, vd), lambda c: (c, gate_proj.shape[1] // vd - 1)),
            const_spec((1, DV)),
        ]
        + [ANY] * len(after),
        out_specs=[
            pl.BlockSpec((rows, vd), lambda c: (c, 0)),
            const_spec(init_state.shape),
            const_spec(init_state.shape),
        ],
        out_shape=[
            shape((length, vd), bf16),
            shape(init_state.shape, f32),
            shape(init_state.shape, f32),
        ],
        compiler_params=params(),
        cost_estimate=cost(10),
        name="gate_forward",
    )(place, maps, init_state, ob, qf, gate_proj, gain, *after)


def gate_back_kernel(
    heads, start_ref, ob_ref, qf_ref, gate_ref, gain_ref, grad_ref,
    dout_ref, dgate_ref, dgain_ref, lead_ref, total_ref,
):
    c = pl.program_id(0)

    @pl.when(c == 0)
    def _():
        dgain_ref[...] = jnp.zeros_like(dgain_ref)
        total_ref[...] = jnp.zeros_like(total_ref)

    gain = gain_ref[...]
    for h in range(heads):
        vs = slice(h * DV, (h + 1) * DV)
        qf = qf_ref[:, h * DK : (h + 1) * DK]
        out, inv = out_norm(ob_ref[:, vs], qf, start_ref[h], gain)
        gate = gate_ref[:, vs]
        act, s = silu(gate)
        grad = grad_ref[:, vs].astype(f32)
        hat = out * inv
        dn = grad * act
        dgate_ref[:, vs] = low(grad * hat * gain * (s * (1.0 + gate * (1.0 - s))))
        part = dn * hat
        rows = part.shape[0]
        dgain_ref[...] += jnp.sum(part.reshape(rows // 8, 8, DV), axis=0)
        dh = dn * gain
        dout = low(inv * (dh - hat * jnp.mean(dh * hat, axis=1, keepdims=True)))
        dout_ref[:, vs] = dout
        total_ref[h] += t_mm(qf, dout)

    @pl.when(c == pl.num_programs(0) - 1)
    def _():
        lead_ref[...] = low(total_ref[...])


def gate_backward(start, ob, qf, gate_proj, gain, grad, after=()):
    heads = start.shape[0]
    length, vd = ob.shape
    kd = heads * DK
    rows = 256
    shape = jax.ShapeDtypeStruct
    block_v = pl.BlockSpec((rows, vd), lambda c: (c, 0))
    return pl.pallas_call(
        ordered(partial(gate_back_kernel, heads), 6, len(after)),
        grid=(length // rows,),
        in_specs=[
            const_spec(start.shape),
            block_v,
            pl.BlockSpec((rows, kd), lambda c: (c, 0)),
            pl.BlockSpec((rows, vd), lambda c: (c, gate_proj.shape[1] // vd - 1)),
            const_spec((1, DV)),
            block_v,
        ]
        + [ANY] * len(after),
        out_specs=[
            block_v,
            pl.BlockSpec((rows, vd), lambda c: (c, 2 * kd // vd + 1)),
            const_spec((8, DV)),
            const_spec(start.shape),
        ],
        out_shape=[
            shape((length, vd), bf16),
            shape((length, 2 * kd + 2 * vd), bf16),
            shape((8, DV), f32),
            shape(start.shape, bf16),
        ],
        scratch_shapes=[pltpu.VMEM(start.shape, f32)],
        compiler_params=params(),
        cost_estimate=cost(11),
        name="gate_backward",
    )(start, ob, qf, gate_proj, gain, grad, *after)


def eights(v):
    return jnp.sum(v.reshape(v.shape[0] // 8, 8, v.shape[1]), axis=0)


def backward_kernel(
    heads, blocks,
    place_ref, keep_ref, hp_ref, ab_ref, x_ref, halo_ref, rim_ref, taps_ref,
    gb_ref, t_ref, u_ref, w_ref, pre_ref, dout_ref, start_ref, maps_ref, leads_ref,
    dx_ref, dlast_ref, drim_ref, dab_ref, dtaps_ref, dhp_ref,
    rows_ref, grads_ref, dstate_ref,
):
    step = pl.program_id(0)
    c = blocks - 1 - step
    hs = range(heads)
    row, col = square_ids()
    diag = row == col
    key_at, value_at = heads * DK, 2 * heads * DK

    @pl.when(step == 0)
    def _():
        me, count = place_ref[0], place_ref[1]

        def relay(i, grads):
            p = count - 1 - i
            return tuple(
                t_mm(maps_ref[p, h, :, :DK], grads[h]) + leads_ref[p - me - 1, h].astype(f32) for h in hs
            )

        end = lax.fori_loop(
            0, count - 1 - me, relay, tuple(jnp.zeros((DK, DV), f32) for h in hs)
        )
        for h in hs:
            dstate_ref[h] = end[h]
        grads_ref[BLOCK:, :] = jnp.zeros_like(grads_ref[BLOCK:, :])
        dtaps_ref[...] = jnp.zeros_like(dtaps_ref)
        dhp_ref[...] = jnp.zeros_like(dhp_ref)

    load_rows(rows_ref, x_ref, halo_ref, rim_ref, c == 0)
    keep_a, keep_b = keep_ref[2 * c], keep_ref[2 * c + 1]
    log_decay, beta, moved, opens = decay_rows(ab_ref[...], hp_ref[...], keep_a, keep_b, heads)
    cum = gb_ref[:heads]
    masks = [None] + [tap_mask(j, keep_a, keep_b) for j in (1, 2, 3)]
    masks_back = [None] + [tap_mask_back(j, keep_b) for j in (1, 2, 3)]

    q_sum = [conv_total(rows_ref, taps_ref, h * DK, masks) for h in hs]
    k_sum = [conv_total(rows_ref, taps_ref, key_at + h * DK, masks) for h in hs]
    q_act = [silu(v) for v in q_sum]
    k_act = [silu(v) for v in k_sum]
    q_unit = [unit(v[0], DK ** (-0.5)) for v in q_act]
    k_unit = [unit(v[0], 1.0) for v in k_act]
    queries = [v[0] for v in q_unit]
    keys = [v[0] for v in k_unit]
    low_q = [low(v) for v in queries]
    low_k = [low(v) for v in keys]
    g_row = [cum[h : h + 1] for h in hs]
    g_col = [to_column(g_row[h], diag) for h in hs]
    b_col = [to_column(beta[h : h + 1], diag) for h in hs]
    grow = [jnp.exp(v) for v in g_col]
    last = [cum[h : h + 1, BLOCK - 1 : BLOCK] for h in hs]
    tail = [jnp.exp(last[h] - g_col[h]) for h in hs]
    decay = [jnp.exp(jnp.where(row >= col, g_col[h] - g_row[h], -1e30)) for h in hs]
    grams = [mm_t(k, k) for k in low_k]
    raw = [mm_t(low_q[h], low_k[h]) for h in hs]
    scores = [low(raw[h] * decay[h]) for h in hs]
    begin = [low(start_ref[h]) for h in hs]
    state = [
        mm(pre_ref[0, h, :, :DK], begin[h]) + pre_ref[0, h, :, DK:].astype(f32) for h in hs
    ]
    low_state = [low(v) for v in state]
    u = [u_ref[:, h * DV : (h + 1) * DV] for h in hs]
    w = [w_ref[:, h * DK : (h + 1) * DK] for h in hs]
    t = [t_ref[0, h] for h in hs]
    fresh = [low(u[h].astype(f32) - mm(w[h], low_state[h])) for h in hs]
    dout = [dout_ref[:, h * DV : (h + 1) * DV] for h in hs]
    dstate = [dstate_ref[h] for h in hs]
    low_dstate = [low(v) for v in dstate]
    key_tail = [tail[h] * keys[h] for h in hs]
    dfresh = [t_mm(scores[h], dout[h]) + mm(key_tail[h], low_dstate[h]) for h in hs]
    low_df = [low(v) for v in dfresh]
    q_grow = [grow[h] * queries[h] for h in hs]
    for h in hs:
        dstate_ref[h] = (
            jnp.exp(last[h]) * dstate[h] + t_mm(q_grow[h], dout[h]) - t_mm(w[h], low_df[h])
        )
    dscores = [mm_t(dout[h], fresh[h]) for h in hs]
    dq_grow = [mm_t(dout[h], low_state[h]) for h in hs]
    dk_tail = [mm_t(fresh[h], low_dstate[h]) for h in hs]
    dw = [-mm_t(low_df[h], low_state[h]) for h in hs]
    r_value = [t_mm(t[h], low_df[h]) for h in hs]
    r_key = [t_mm(t[h], dw[h]) for h in hs]
    da = [
        jnp.where(row > col, -(mm_t(r_value[h], u[h]) + mm_t(r_key[h], w[h])), 0.0) for h in hs
    ]
    dsd = [dscores[h] * decay[h] for h in hs]
    dad = [da[h] * decay[h] for h in hs]
    mixed = [dad[h] * grams[h] for h in hs]
    both = [b_col[h] * mixed[h] + dsd[h] * raw[h] for h in hs]
    lift = [b_col[h] * grow[h] for h in hs]
    low_dsd = [low(v) for v in dsd]
    hmat = [b_col[h] * dad[h] for h in hs]
    dq = [grow[h] * dq_grow[h] + mm(low_dsd[h], low_k[h]) for h in hs]
    dk = [
        t_mm(low_dsd[h], low_q[h])
        + tail[h] * dk_tail[h]
        + lift[h] * r_key[h]
        + mm(hmat[h], low_k[h])
        + t_mm(hmat[h], low_k[h])
        for h in hs
    ]

    cum_parts, beta_parts = [], []
    for h in hs:
        rk = jnp.sum(r_key[h] * keys[h], axis=1, keepdims=True)
        tails = jnp.sum(dk_tail[h] * key_tail[h], axis=1, keepdims=True)
        part = (
            jnp.sum(both[h], axis=1, keepdims=True)
            + jnp.sum(dq_grow[h] * q_grow[h], axis=1, keepdims=True)
            + lift[h] * rk
            - tails
        )
        end_part = jnp.sum(tails, axis=0, keepdims=True) + jnp.exp(last[h]) * jnp.sum(
            jnp.sum(dstate[h] * state[h], axis=1, keepdims=True), axis=0, keepdims=True
        )
        dcum = to_row(part, diag) - jnp.sum(both[h], axis=0, keepdims=True)
        lane = lax.broadcasted_iota(jnp.int32, (1, BLOCK), 1)
        cum_parts.append(dcum + jnp.where(lane == BLOCK - 1, end_part, 0.0))
        beta_parts.append(
            jnp.sum(mixed[h], axis=1, keepdims=True) + grow[h] * rk
        )

    def conv_back(dact, total, s, at):
        dtot = dact * (s * (1.0 + total * (1.0 - s)))
        cols = slice(at, at + DK)
        grads_ref[0:BLOCK, cols] = dtot
        dtaps_ref[0, :, cols] += eights(dtot * rows_ref[8 : 8 + BLOCK, cols])
        dx = dtot * taps_ref[0:1, cols]
        for j in (1, 2, 3):
            dtaps_ref[j, :, cols] += eights(
                dtot * masks[j] * rows_ref[8 - j : 8 - j + BLOCK, cols]
            )
            dx = dx + grads_ref[j : j + BLOCK, cols] * masks_back[j] * taps_ref[j : j + 1, cols]
        dx_ref[:, cols] = low(dx)

        @pl.when(step == 0)
        def _():
            dlast_ref[:, cols] = dx[BLOCK - 8 :]

        grads_ref[BLOCK : BLOCK + 8, cols] = dtot[0:8] * keep_a

    def unit_back(grad, normal, scale, factor):
        inner = jnp.sum(grad * normal, axis=1, keepdims=True) * (1.0 / (factor * factor))
        return scale * (grad - normal * inner)

    for h in hs:
        conv_back(
            unit_back(dq[h], queries[h], q_unit[h][1], DK ** (-0.5)),
            q_sum[h], q_act[h][1], h * DK,
        )
        conv_back(
            unit_back(dk[h], keys[h], k_unit[h][1], 1.0), k_sum[h], k_act[h][1], key_at + h * DK
        )
        dot_v = 0.0
        for s in range(DV // DK):
            at = value_at + h * DV + s * DK
            total = conv_total(rows_ref, taps_ref, at, masks)
            act, sig = silu(total)
            rv = r_value[h][:, s * DK : (s + 1) * DK]
            dot_v = dot_v + jnp.sum(rv * act, axis=1, keepdims=True)
            conv_back(b_col[h] * rv, total, sig, at)
        beta_parts[h] = to_row(beta_parts[h] + dot_v, diag)

    dcum = jnp.concatenate(cum_parts, axis=0)
    dlog = jnp.where(opens, 0.0, exact_mm(dcum, (row >= col).astype(f32)))
    dbeta = jnp.concatenate(beta_parts, axis=0)
    dalpha = -dlog * hp_ref[:heads] * sigmoid(moved)
    dab_ref[...] = jnp.concatenate([dalpha, dbeta * beta * (1.0 - beta)], axis=0)
    dhp_ref[...] += jnp.concatenate([-dlog * softplus(moved), dalpha], axis=0)

    @pl.when(step == blocks - 1)
    def _():
        grads_ref[BLOCK - 8 : BLOCK, :] = jnp.zeros((8, grads_ref.shape[1]), f32)
        total = jnp.zeros((8, grads_ref.shape[1]), f32)
        for j in (1, 2, 3):
            total = total + grads_ref[BLOCK - 8 + j : BLOCK + j, :] * taps_ref[j : j + 1, :]
        drim_ref[...] = total


def backward_local(
    place, keep, hp, ab, proj, rim, taps, gb, t, u, w, pre, dout, start, maps, leads, grads,
    after=(),
):
    heads = hp.shape[0] // 2
    length = proj.shape[0]
    blocks = length // BLOCK
    kd, vd = heads * DK, heads * DV
    width = 2 * kd + vd
    shape = jax.ShapeDtypeStruct
    back = blocks - 1
    eighth = BLOCK // 8
    return pl.pallas_call(
        ordered(partial(backward_kernel, heads, blocks), 17, 1 + len(after)),
        grid=(blocks,),
        in_specs=[
            SMEM,
            SMEM,
            const_spec((2 * heads, BLOCK)),
            pl.BlockSpec((2 * heads, BLOCK), lambda c: (0, back - c)),
            pl.BlockSpec((BLOCK, width), lambda c: (back - c, 0)),
            pl.BlockSpec((8, width), lambda c: (jnp.maximum((back - c) * eighth - 1, 0), 0)),
            const_spec((8, width)),
            const_spec((4, width)),
            pl.BlockSpec((2 * heads, BLOCK), lambda c: (0, back - c)),
            pl.BlockSpec((1, heads, BLOCK, BLOCK), lambda c: (back - c, 0, 0, 0)),
            pl.BlockSpec((BLOCK, vd), lambda c: (back - c, 0)),
            pl.BlockSpec((BLOCK, kd), lambda c: (back - c, 0)),
            pl.BlockSpec((1, heads, DK, WIDE), lambda c: (back - c, 0, 0, 0)),
            pl.BlockSpec((BLOCK, vd), lambda c: (back - c, 0)),
            const_spec(start.shape),
            const_spec(maps.shape),
            const_spec(leads.shape),
        ]
        + [ANY] * (1 + len(after)),
        out_specs=[
            pl.BlockSpec((BLOCK, width), lambda c: (back - c, 0)),
            const_spec((8, width)),
            const_spec((8, width)),
            pl.BlockSpec((2 * heads, BLOCK), lambda c: (0, back - c)),
            const_spec((4, 8, width)),
            const_spec((2 * heads, BLOCK)),
        ],
        out_shape=[
            shape(grads.shape, bf16),
            shape((8, width), f32),
            shape((8, width), f32),
            shape((2 * heads, length), f32),
            shape((4, 8, width), f32),
            shape((2 * heads, BLOCK), f32),
        ],
        scratch_shapes=[
            pltpu.VMEM((8 + BLOCK, width), f32),
            pltpu.VMEM((8 + BLOCK, width), f32),
            pltpu.VMEM(start.shape, f32),
        ],
        compiler_params=params(),
        input_output_aliases={17: 0},
        cost_estimate=cost(50),
        name="delta_backward",
    )(
        place, keep, hp, ab, proj, proj, rim, taps, gb, t, u, w, pre, dout, start, maps, leads,
        grads, *after,
    )


def tie(block, *after):
    return pl.pallas_call(
        lambda *refs: None,
        in_specs=[ANY] * (1 + len(after)),
        out_specs=ANY,
        out_shape=jax.ShapeDtypeStruct(block.shape, block.dtype),
        input_output_aliases={0: 0},
        cost_estimate=cost(1),
        name="tie",
    )(block, *after)


def swiglu_kernel(units, gate_ref, up_ref, grad_ref, hidden_ref, grads_ref):
    gate, up = gate_ref[...], up_ref[...]
    act, s = silu(gate)
    hidden_ref[...] = low(act * up)
    grad = grad_ref[...].astype(f32)
    grads_ref[:, :units] = low(grad * up * (s * (1.0 + gate * (1.0 - s))))
    grads_ref[:, units:] = low(grad * act)


def swiglu_both(gate, up, grad):
    rows, units = grad.shape
    step = 64
    spec = lambda columns: pl.BlockSpec((step, columns), lambda c: (c, 0))
    shape = jax.ShapeDtypeStruct
    return pl.pallas_call(
        partial(swiglu_kernel, units),
        grid=(rows // step,),
        in_specs=[spec(units)] * 3,
        out_specs=[spec(units), spec(2 * units)],
        out_shape=[shape((rows, units), bf16), shape((rows, 2 * units), bf16)],
        compiler_params=params(),
        cost_estimate=cost(8),
        name="swiglu_both",
    )(gate, up, grad)


def rms_scale(values, scales):
    return (
        values * lax.rsqrt(jnp.mean(values * values, axis=-1, keepdims=True) + eps) * scales
    )


def doc_numbers(positions, seg_starts, continues):
    opens = 1 - continues
    passed = (positions[:, None] >= seg_starts[None, 1:]).astype(jnp.int32)
    return jnp.sum(passed * opens[None, :], axis=1)


def passed_along(block, axis, distance):
    devices = range(lax.axis_size(axis))
    route = [(i - distance, i) for i in devices if i - distance in devices]
    return lax.ppermute(block, axis, route)


def rows_times(left, right):
    return jnp.dot(left, right, preferred_element_type=f32)


def times_back(left, right):
    return jnp.einsum("tc,dc->td", left, right, preferred_element_type=f32)


def weight_grad(left, right):
    return low(jnp.einsum("td,tc->dc", left, right, preferred_element_type=f32))


def gather_rows(block, axis="seq"):
    return lax.all_gather(block, axis, axis=0, tiled=True)


def scatter_rows(block, axis="seq"):
    return lax.psum_scatter(low(block), axis, scatter_dimension=0, tiled=True)


def next_hop(pair, axis, step):
    n = lax.axis_size(axis)
    return (
        lax.ppermute(pair[0], axis, [(i, i + 1) for i in range(step, n - 1)]),
        lax.ppermute(pair[1], axis, [(n - 1 - i, n - 2 - i) for i in range(step, n - 1)]),
    )


def line_steps(rows, axis):
    n = lax.axis_size(axis)
    me = lax.axis_index(axis)
    own = rows.shape[0] // n
    chunk = lambda at: lax.dynamic_slice_in_dim(rows, jnp.clip(at, 0, n - 1) * own, own, 0)

    def payload(step, came):
        up, down = chunk(n - 1 + me - step), chunk(me - (n - 1) + step)
        if came is None:
            return up, down
        return low(up.astype(f32) + came[0].astype(f32)), low(
            down.astype(f32) + came[1].astype(f32)
        )

    def send(step, pair):
        return (
            lax.ppermute(pair[0], axis, [(i, i + 1) for i in range(step + 1)]),
            lax.ppermute(pair[1], axis, [(n - 1 - i, n - 2 - i) for i in range(step + 1)]),
        )

    return payload, send, lambda came: (
        chunk(me).astype(f32) + came[0].astype(f32) + came[1].astype(f32)
    )


def line_scatter(rows, axis):
    payload, send, total = line_steps(rows, axis)
    came = None
    for step in range(lax.axis_size(axis) - 1):
        came = send(step, payload(step, came))
    return total(came)


def assembled(block, came, axis):
    n = lax.axis_size(axis)
    me = lax.axis_index(axis)
    own = block.shape[0]
    out = jnp.zeros((n * own,) + block.shape[1:], block.dtype)
    put = lambda out, part, at: lax.dynamic_update_slice_in_dim(
        out, part, jnp.clip(at, 0, n - 1) * own, 0
    )
    for step in range(n - 2, -1, -1):
        right, left = came[step]
        out = put(put(out, right, me - 1 - step), left, me + 1 + step)
    return put(out, block, me)


def line_gather(block, axis):
    came = [(block, block)]
    for step in range(lax.axis_size(axis) - 1):
        came.append(next_hop(came[-1], axis, step))
    return assembled(block, came[1:], axis)


def swapped(block, axis, bit):
    return lax.ppermute(block, axis, [(i, i ^ bit) for i in range(lax.axis_size(axis))])


def exchange_step(values, axis, step):
    return values + swapped(values, axis, 1 << step)


def tree_sum(values, axis, first):
    for step in range(first, lax.axis_size(axis).bit_length() - 1):
        values = exchange_step(values, axis, step)
    return values


def body(
    tokens, attn_gain, w_query, w_key, w_value, w_gate_out, w_alpha, w_beta,
    conv_query, conv_key, conv_value, decay_scale, dt_bias, out_gain, w_out, mlp_gain,
    w_mlp_gate, w_mlp_up, w_mlp_down, init_state, seg_starts, continues, cotangent,
):
    count = lax.axis_size("seq")
    me = lax.axis_index("seq")
    lane = lax.axis_index("tp")
    length, width = tokens.shape
    heads = decay_scale.shape[0]
    kd, vd = heads * DK, heads * DV
    own = length // lax.axis_size("tp")
    rows_of = lambda rows, at: lax.dynamic_slice_in_dim(rows, at * own, own, 0)
    mine = lambda rows: rows_of(rows, lane)
    pair = lambda rows: jnp.concatenate([rows_of(rows, lane), rows_of(rows, lane ^ 1)], axis=0)

    after = lambda pair, *awaited: [tie(v, *awaited) for v in pair]

    units = w_mlp_gate.shape[1]
    fill = jnp.zeros((w_mlp_gate.shape[0], -units % 128), bf16)
    half_units = units + fill.shape[1]
    all_units = 2 * half_units
    other_down = swapped(w_mlp_down, "tp", 2)
    other_gate = swapped(w_mlp_gate, "tp", 2)
    first_part = units * 2 // 7 // 128 * 128
    other_up = [
        swapped(w_mlp_up[:, :first_part], "tp", 2),
        swapped(w_mlp_up[:, first_part:], "tp", 2),
    ]
    small = gather_rows(
        jnp.concatenate(
            [w_alpha, w_beta, attn_gain[:, None], mlp_gain[:, None]]
            + [jnp.zeros((w_alpha.shape[0], 6), bf16)],
            axis=1,
        )
    )
    full_ab = small[:, : 2 * heads]
    gain_one = small[:, 2 * heads].astype(f32)
    gain_two = small[:, 2 * heads + 1].astype(f32)
    full_qkv = gather_rows(jnp.concatenate([w_query, w_key, w_value], axis=1))
    full_go = gather_rows(jnp.concatenate([w_gate_out, w_out], axis=1))
    full_gate, full_out = full_go[:, :vd], full_go[:, vd:]
    full_dg = gather_rows(
        jnp.concatenate(
            [w_mlp_down, fill, other_down, fill, w_mlp_gate, fill, other_gate, fill], axis=1
        )
    )
    full_down, full_mlp_gate = full_dg[:, :all_units], full_dg[:, all_units:]

    firsts = me * length + DOC_STEP * jnp.arange(length // DOC_STEP, dtype=jnp.int32)
    keep = (
        doc_numbers(firsts, seg_starts, continues)
        == doc_numbers(firsts - 1, seg_starts, continues)
    ).astype(f32)
    place = jnp.stack([me, jnp.int32(count)]).astype(jnp.int32)
    hp = jnp.broadcast_to(jnp.concatenate([decay_scale, dt_bias])[:, None], (2 * heads, BLOCK))
    taps = jnp.concatenate([conv_query, conv_key, conv_value], axis=1)
    gain_row = out_gain[None, :]

    normed = low(rms_scale(tokens.astype(f32), gain_one))
    proj = rows_times(normed, full_qkv)
    ab = jnp.einsum("dc,td->ct", full_ab, normed, preferred_element_type=f32)
    gate_proj = rows_times(normed, full_gate)
    rim = passed_along(proj[-8:], "seq", 1)
    gb, t_inv, u, w, pre, qf, ob, own_map = forward_local(
        keep, hp, ab, proj, rim, taps, (other_down, other_gate, other_up[0])
    )
    maps = lax.all_gather(own_map, "seq", axis=0)
    gated, start, final = gate_forward(
        place, maps, init_state, ob, qf, gate_proj, gain_row
    )
    full_mlp_up = gather_rows(jnp.concatenate([w_mlp_up, fill, *other_up, fill], axis=1))
    piece = final.shape[1] // count
    final_state = lax.dynamic_slice_in_dim(final, me * piece, piece, 1)

    middle = mine(tokens).astype(f32) + line_scatter(low(times_back(gated, full_out)), "tp")
    normed_two_f, norm_two_back = jax.vjp(rms_scale, middle, gain_two)
    own_two = low(normed_two_f)
    normed_two = jnp.concatenate([own_two, swapped(own_two, "tp", 1)], axis=0)
    cot_pair = pair(cotangent)
    grad_hidden = low(rows_times(cot_pair, full_down))
    gate_mlp = rows_times(normed_two, full_mlp_gate)
    up_mlp = rows_times(tie(normed_two, gate_mlp, grad_hidden), full_mlp_up)
    hidden, grad_both = swiglu_both(gate_mlp, up_mlp, grad_hidden)
    grad_two_part = times_back(grad_both[:, :all_units], full_mlp_gate) + times_back(
        grad_both[:, all_units:], full_mlp_up
    )
    part_two = low(grad_two_part[own:])
    part_two = swapped(part_two, "tp", 1)
    grad_two = grad_two_part[:own] + part_two.astype(f32)
    term_both = tie(weight_grad(normed_two, grad_both), part_two)
    grad_middle_norm, grad_mlp_gain_part = norm_two_back(grad_two)
    grad_middle = mine(cotangent).astype(f32) + grad_middle_norm
    own_attn = tie(low(grad_middle), term_both)
    grad_w_both = scatter_rows(term_both)
    mlp_part = times_back(hidden, full_down)
    part_back = low(mlp_part[own:])
    term_down = weight_grad(cot_pair, hidden)
    came = [next_hop((own_attn, own_attn), "tp", 0)]
    came.append(next_hop(after(came[0], part_back), "tp", 1))
    came.append(next_hop(after(came[1], term_down), "tp", 2))
    grad_attn = assembled(own_attn, came, "tp")

    grad_gated = rows_times(grad_attn, full_out)
    dout, d_all, dgain, lead = gate_backward(
        start, ob, qf, gate_proj, gain_row, grad_gated, (part_back, term_down)
    )
    leads = [passed_along(lead, "seq", -d) for d in range(1, count)]
    grad_w_down = scatter_rows(term_down)
    term_out = weight_grad(tie(grad_attn, leads[0]), gated)
    grad_w_out = scatter_rows(term_out)
    part_back = swapped(tie(part_back, grad_attn), "tp", 1)
    block_own = low(middle + mlp_part[:own] + part_back.astype(f32))
    d_all, dlast, drim, dab, dtaps, dhp = backward_local(
        place, keep, hp, ab, proj, rim, taps, gb, t_inv, u, w, pre, dout, start, maps,
        jnp.stack(leads),
        d_all, (term_out, block_own),
    )
    came = [next_hop((block_own, block_own), "tp", 0)]
    back_gate = swapped(grad_w_both[:, half_units:all_units], "tp", 2)
    d_all = tie(d_all, *came[0], back_gate)
    back_up = swapped(tie(grad_w_both[:, all_units + half_units :], d_all), "tp", 2)

    fixed = low(dlast + passed_along(drim, "seq", -1))
    d_all = lax.dynamic_update_slice(d_all, fixed, (length - 8, 0))
    dab = low(dab)
    wide = taps.shape[1]
    grad_normed = (
        times_back(d_all[:, :wide], full_qkv)
        + times_back(d_all[:, wide:], full_gate)
        + jnp.einsum("ct,dc->td", dab, full_ab, preferred_element_type=f32)
    )
    tokens_f = tokens.astype(f32)
    grad_attn_gain_part = jnp.sum(
        grad_normed
        * (tokens_f * lax.rsqrt(jnp.mean(tokens_f * tokens_f, axis=-1, keepdims=True) + eps)),
        axis=0,
    )
    grad_ab = jnp.einsum("td,ct->dc", normed, dab, preferred_element_type=f32)
    ab_at, gain_at = 4 * wide, 4 * wide + 2 * heads * width
    hp_at = gain_at + DV + 2 * width
    smalls = [
        jnp.sum(dtaps, axis=1).reshape(-1),
        grad_ab.reshape(-1),
        jnp.sum(dgain, axis=0),
        grad_attn_gain_part,
        grad_mlp_gain_part,
        jnp.sum(dhp, axis=1),
    ]
    grad_normed = tie(low(grad_normed), back_up)
    payload, send, total = line_steps(grad_normed, "tp")
    came.append(next_hop(after(came[0], grad_normed), "tp", 1))
    moved = send(0, payload(0, None))
    by_seq = tree_sum(jnp.concatenate(smalls), "seq", 0)
    pair = after(payload(1, moved), by_seq, *came[1])
    came.append(next_hop(after(came[1], pair[0]), "tp", 2))
    moved = send(1, pair)
    by_all = tree_sum(by_seq[gain_at:hp_at], "tp", 0)
    moved = send(2, after(payload(2, moved), by_all, *came[2]))
    term_proj = tie(weight_grad(normed, d_all), *moved)
    grad_one = total(moved)
    block_out = assembled(block_own, came, "tp")
    grad_proj = scatter_rows(term_proj).astype(f32)
    _, norm_one_back = jax.vjp(lambda v: rms_scale(v, gain_one), mine(tokens).astype(f32))
    (grad_tokens_norm,) = norm_one_back(grad_one)
    own_grad = low(grad_middle + grad_tokens_norm)
    came = [next_hop((own_grad, own_grad), "tp", 0)]
    came.append(next_hop(came[0], "tp", 1))
    back_down = swapped(tie(grad_w_down[:, half_units:], came[0][0]), "tp", 2)
    came.append(next_hop(came[1], "tp", 2))
    grad_tokens = assembled(own_grad, came, "tp").astype(f32)

    grad_w_gate = grad_w_both[:, :units].astype(f32) + back_gate[:, :units].astype(f32)
    grad_w_up = grad_w_both[:, all_units : all_units + units].astype(f32) + back_up[:, :units].astype(f32)
    grad_w_down = grad_w_down[:, :units].astype(f32) + back_down[:, :units].astype(f32)

    rows_in = width // count
    taps_sum = by_seq[:ab_at].reshape(4, wide)
    ab_sum = lax.dynamic_slice_in_dim(
        by_seq[ab_at:gain_at].reshape(width, 2 * heads), me * rows_in, rows_in, 0
    )
    hp_sum = by_seq[hp_at:]
    own_gain = lambda at: lax.dynamic_slice_in_dim(by_all, at + me * rows_in, rows_in, 0)
    return (
        block_out,
        final_state,
        grad_tokens,
        own_gain(DV),
        grad_proj[:, :kd],
        grad_proj[:, kd : 2 * kd],
        grad_proj[:, 2 * kd : wide],
        grad_proj[:, wide:],
        ab_sum[:, :heads],
        ab_sum[:, heads:],
        taps_sum[:, :kd],
        taps_sum[:, kd : 2 * kd],
        taps_sum[:, 2 * kd :],
        hp_sum[:heads],
        hp_sum[heads:],
        by_all[:DV],
        grad_w_out.astype(f32),
        own_gain(DV + width),
        grad_w_gate,
        grad_w_up,
        grad_w_down,
    )


def solution(mesh):
    in_specs = (
        P("seq", None),
        P("seq"),
        P("seq", "tp"),
        P("seq", "tp"),
        P("seq", "tp"),
        P("seq", "tp"),
        P("seq", "tp"),
        P("seq", "tp"),
        P(None, "tp"),
        P(None, "tp"),
        P(None, "tp"),
        P("tp"),
        P("tp"),
        P(),
        P("seq", "tp"),
        P("seq"),
        P("seq", "tp"),
        P("seq", "tp"),
        P("seq", "tp"),
        P("tp", None, None),
        P(),
        P(),
        P("seq", None),
    )
    out_specs = (
        P("seq", None),
        P("tp", "seq", None),
        P("seq", None),
        P("seq"),
        P("seq", "tp"),
        P("seq", "tp"),
        P("seq", "tp"),
        P("seq", "tp"),
        P("seq", "tp"),
        P("seq", "tp"),
        P(None, "tp"),
        P(None, "tp"),
        P(None, "tp"),
        P("tp"),
        P("tp"),
        P(),
        P("seq", "tp"),
        P("seq"),
        P("seq", "tp"),
        P("seq", "tp"),
        P("seq", "tp"),
    )
    return jax.shard_map(body, mesh=mesh, in_specs=in_specs, out_specs=out_specs, check_vma=False)
```

time: 3690 us -> 998 us (0.27)
  waiting for transfers between devices: 1340 us -> 358 us
  matrix products: 1160 us -> 199 us
  other arithmetic: 635 us -> 60.5 us
  local copies, waits for them, and re-layouts: 354 us -> 107 us
  Pallas kernels: 0 us -> 116 us
  blocking collectives: 83.2 us -> 9.73 us
  starting transfers between devices: 63 us -> 122 us
    dot_general x452 -> x19, matrix products: 1120 us -> 199 us  [the longest x6 66.6 us: rows_times(): return jnp.dot(left, right, preferred_element_type=f32)]
    psum x3 -> x0, waiting for transfers between devices: 857 us -> none  [the longest x1 293 us: body(): lax.psum(mlp_terms.astype(jnp.bfloat16), 'tp').astype(jnp.float32)]
    another operation x10 -> x1, other arithmetic: 319 us -> 0.59 us  [body(): place = jnp.stack([me, jnp.int32(count)]).astype(jnp.int32)]
    ppermute x0 -> x45, waiting for transfers between devices: none -> 287 us  [the longest x15 96.4 us: swapped(): lax.ppermute(block, axis, [(i, i ^ bit) for i in range(lax.axis_size(axis...]
    reduce_scatter x9 -> x4, waiting for transfers between devices: 276 us -> 0.03 us  [scatter_rows(): return lax.psum_scatter(low(block), axis, scatter_dimension=0, tiled=True)]
    pallas_call x0 -> x27, Pallas kernels: none -> 116 us  [the longest x1 51 us: backward_local(): pl.pallas_call(ordered(partial(backward_kernel, heads, blocks), 17, 1 + l...]
    reduce_sum x79 -> x7, other arithmetic: 127 us -> 13.5 us  [the longest x3 9.33 us: rms_scale(): jnp.mean(values * values, axis=-1, keepdims=True) + eps]
    ppermute x0 -> x45, starting transfers between devices: none -> 108 us  [the longest x15 46 us: swapped(): lax.ppermute(block, axis, [(i, i ^ bit) for i in range(lax.axis_size(axis...]
  transfers between devices with their start and end apart: 38 -> 63, of which waited for: 29 -> 33; matrix products, arithmetic and copies ran while one was open for 56% -> 31% of each run, Pallas kernels for 0% -> 11%
where the time goes in v1:
time: 998 us; the launch traced here: 987 us
  waiting for transfers between devices  358 us (36%)
  matrix products  199 us (20%)
  starting transfers between devices  122 us (12%)
  Pallas kernels  116 us (12%)
  local copies, waits for them, and re-layouts  107 us (11%)
  other arithmetic  60.5 us (6%)
  between operations  15.9 us (2%)
    ppermute x15, waiting for transfers between devices, swapped(): lax.ppermute(block, axis, [(i, i ^ bit) for i in range(lax.axis_size(axis...  96.4 us
    ppermute x6, waiting for transfers between devices, send(): lax.ppermute(pair[0], axis, [(i, i + 1) for i in range(step + 1)])  75.3 us
    ppermute x9, waiting for transfers between devices, next_hop(): lax.ppermute(pair[1], axis, [(n - 1 - i, n - 2 - i) for i in range(step,...  71.8 us
    dot_general x6, matrix products, rows_times(): return jnp.dot(left, right, preferred_element_type=f32)  66.6 us
    dot_general x4, matrix products, weight_grad(): return low(jnp.einsum('td,tc->dc', left, right, preferred_element_type=f32))  60.7 us
    dot_general x6, matrix products, times_back(): return jnp.einsum('tc,dc->td', left, right, preferred_element_type=f32)  59.1 us
    pallas_call x1, Pallas kernels, backward_local(): pl.pallas_call(ordered(partial(backward_kernel, heads, blocks), 17, 1 + l...  51 us
    unnamed x207, local copies, waits for them, and re-layouts  49.6 us
  transfers between devices with their start and end apart: 63, of which 33 were waited for; matrix products, arithmetic and copies ran while one was open for 31% of the time, Pallas kernels for 11%

profile of v1, /device:TPU:0, one launch (start us, length us, event | category | flops | bytes accessed | tf_op | source)
XLA Modules:
  0.0 987.5 jit_solution(14913247798826134496)
XLA Ops:
  12.2 4.1 collective-permute-start.1
  19.6 9.7 all_gather.21
  35.1 32.6 %all-gather.7.cloned.1.call-done = bf16[2048,2048]{1,0:T(8,128)(2,1)} async-done(((bf16[256,2048]{1,0:T(8,128)(2,1)}), bf16[2048,2048]{1,0:T(8,128)(2,1)}) %all-gather.7.cloned.1.call-update) | async-done | bytes 8388624 | tf_op jit(solution)/shard_map/all_gather | solution.py:764
  67.7 12.6 %fusion.56.refs_3_.refs_4_.refs_5_ = f32[1024,2048]{1,0:T(8,128)S(1)} fusion(bf16[2048,2048]{1,0:T(8,128)(2,1)} %all-gather.7.cloned.1.call-done, bf16[1024,2048]{1,0:T(8,128)(2,1)} %param.23, f32[2048]{0:T(1024)S(1)} %bitcast.40, f32[1024]{0:T(1024)S(1)} %add_rsqrt_fusion), kind=kOutput, calls=%fused_computation.160 | convolution fusion | flops 8598323200 | bytes 20983808 | tf_op jit(solution)/shard_map/dot_general | solution.py:752
  86.8 30.5 %delta_forward.1 = (f32[8,1024]{1,0:T(8,128)}, bf16[8,4,128,128]{3,2,1,0:T(8,128)(2,1)}, bf16[1024,1024]{1,0:T(8,128)(2,1)}, bf16[1024,512]{1,0:T(8,128)(2,1)}, ...) custom-call(f32[16]{0:T(128)} %compare_convert_fusion.refs_0_.refs_1, ...), custom_call_target="tpu_custom_call" | custom-call | flops 30000001024 | bytes 30000000 | tf_op jit(solution)/shard_map/delta_forward/pallas_call | solution.py:255
  127.7 21.9 %collective-permute-done.11 = bf16[256,992]{0,1:T(8,128)(2,1)S(1)} collective-permute-done((bf16[256,992]{0,1:T(8,128)(2,1)S(1)}, bf16[256,992]{0,1:T(8,128)(2,1)S(1)}, u32[]{:S(2)}, u32[]{:S(2)}) %collective-permute-start.11) | collective-permute-done | bytes 507936 | tf_op jit(solution)/shard_map/ppermute | solution.py:834
  151.7 10.2 %fusion.23.refs_5_.refs_3_ = f32[1024,1024]{1,0:T(8,128)} fusion(bf16[2048,2048]{1,0:T(8,128)(2,1)} %all-gather.9.cloned.1.call-done, bf16[1024,2048]{1,0:T(8,128)(2,1)} %param.23, f32[2048]{0:T(1024)S(1)} %bitcast.41, f32[1024]{0:T(1024)S(1)} %add_rsqrt_fusion), kind=kOutput, calls=%fused_computation.29 | convolution fusion | flops 4303355904 | bytes 12595200 | tf_op jit(solution)/shard_map/dot_general | solution.py:752
  161.9 11.0 %gate_forward.1 = (bf16[1024,1024]{1,0:T(8,128)(2,1)}, f32[4,128,256]{2,1,0:T(8,128)}, f32[4,128,256]{2,1,0:T(8,128)}) custom-call(s32[2]{0:T(128)} %pad_add_fusion.refs_0_, bf16[8,4,128,384]{3,2,1,0:T(8,128)(2,1)} %bitcast.48, f32[4,128,256]{2,1,0:T(8,128)} %refs_2_.1, f32[1024,1024]{1,0:T(8,128)} %get-tuple-element.45.refs_3_.refs_1_, ...), custom_call_target="tpu_custom_call" | custom-call | flops 10000000000 | bytes 10000000 | tf_op jit(solution)/shard_map/gate_forward/pallas_call | solution.py:340
  173.0 7.6 convolution_convert_fusion.4
  186.9 20.9 %collective-permute-done.4 = bf16[256,2048]{1,0:T(8,128)(2,1)S(1)} collective-permute-done((bf16[256,2048]{1,0:T(8,128)(2,1)S(1)}, bf16[256,2048]{1,0:T(8,128)(2,1)S(1)}, u32[]{:S(2)}, u32[]{:S(2)}) %collective-permute-start.4) | collective-permute-done | bytes 1048608 | tf_op jit(solution)/shard_map/ppermute | solution.py:795
  209.5 5.4 collective-permute-start.5
  214.9 20.8 %collective-permute-done.5 = bf16[256,2048]{1,0:T(8,128)(2,1)} collective-permute-done((bf16[256,2048]{1,0:T(8,128)(2,1)S(1)}, bf16[256,2048]{1,0:T(8,128)(2,1)}, u32[]{:S(2)}, u32[]{:S(2)}) %collective-permute-start.5) | collective-permute-done | bytes 1048608 | tf_op jit(solution)/shard_map/ppermute | solution.py:795
  239.4 6.0 collective-permute-start.6
  248.5 16.9 %collective-permute-done.6 = bf16[256,2048]{1,0:T(8,128)(2,1)} collective-permute-done((bf16[256,2048]{1,0:T(8,128)(2,1)S(1)}, bf16[256,2048]{1,0:T(8,128)(2,1)}, u32[]{:S(2)}, u32[]{:S(2)}) %collective-permute-start.6) | collective-permute-done | bytes 1048608 | tf_op jit(solution)/shard_map/ppermute | solution.py:795
  265.4 25.6 %collective-permute-done.9 = bf16[256,2048]{1,0:T(8,128)(2,1)} collective-permute-done((bf16[256,2048]{1,0:T(8,128)(2,1)S(1)}, bf16[256,2048]{1,0:T(8,128)(2,1)}, u32[]{:S(2)}, u32[]{:S(2)}) %collective-permute-start.9) | collective-permute-done | bytes 1048608 | tf_op jit(solution)/shard_map/ppermute | solution.py:796
  291.0 3.4 multiply_reduce_fusion.2
  300.1 17.3 %collective-permute-done.10 = bf16[256,2048]{1,0:T(8,128)(2,1)} collective-permute-done((bf16[256,2048]{1,0:T(8,128)(2,1)}, bf16[256,2048]{1,0:T(8,128)(2,1)}, u32[]{:S(2)}, u32[]{:S(2)}) %collective-permute-start.10) | collective-permute-done | bytes 1048608 | tf_op jit(solution)/shard_map/ppermute | solution.py:834
  317.4 3.4 pad_maximum_fusion.refs_0_
  320.7 12.4 %fusion.6.refs_1_.gate_ref = f32[512,2816]{1,0:T(8,128)} fusion(bf16[2048,5632]{0,1:T(8,128)(2,1)} %all-gather.11.cloned.1.call-done, bf16[256,2048]{1,0:T(8,128)(2,1)} %collective-permute-done.10, bf16[256,2048]{1,0:T(8,128)(2,1)} %multiply_convert_fusion), kind=kOutput, calls=%fused_computation.11 | convolution fusion | flops 5909774336 | bytes 19398656 | tf_op jit(solution)/shard_map/dot_general | solution.py:752
  333.2 12.7 %fusion.13.refs_2_.grad_ref = bf16[512,2816]{1,0:T(8,128)(2,1)} fusion(bf16[2048,5632]{0,1:T(8,128)(2,1)} %all-gather.11.cloned.1.call-done, bf16[256,2048]{1,0:T(8,128)(2,1)S(1)} %copy-done.48, bf16[256,2048]{1,0:T(8,128)(2,1)S(1)} %get-tuple-element.167), kind=kOutput, calls=%fused_computation.19 | convolution fusion | flops 5911216128 | bytes 16515072 | tf_op jit(solution)/shard_map/dot_general | solution.py:752
  345.9 8.2 all-gather.13.cloned.1.call-done
  354.1 12.6 %fusion.68.up_ref = f32[512,2816]{1,0:T(8,128)} fusion(bf16[512,2048]{1,0:T(8,128)(2,1)} %tie.22, bf16[2048,2816]{0,1:T(8,128)(2,1)} %all-gather.13.cloned.1.call-done), kind=kOutput, calls=%fused_computation.169 | convolution fusion | flops 5905580032 | bytes 19398656 | tf_op jit(solution)/shard_map/dot_general | solution.py:752
  366.7 10.9 %swiglu_both.1 = (bf16[512,2816]{1,0:T(8,128)(2,1)}, bf16[512,5632]{1,0:T(8,128)(2,1)}) custom-call(f32[512,2816]{1,0:T(8,128)} %fusion.6.refs_1_.gate_ref, f32[512,2816]{1,0:T(8,128)} %fusion.68.up_ref, bf16[512,2816]{1,0:T(8,128)(2,1)} %fusion.13.refs_2_.grad_ref), custom_call_target="tpu_custom_call" | custom-call | flops 8000000000 | bytes 8000000 | tf_op jit(solution)/shard_map/swiglu_both/pallas_call | solution.py:721
  377.6 10.0 %fusion.28 = f32[512,2048]{1,0:T(8,128)S(1)} fusion(bf16[2048,2816]{0,1:T(8,128)(2,1)} %all-gather.13.cloned.1.call-done, bf16[512,5632]{1,0:T(8,128)(2,1)} %get-tuple-element.49), kind=kOutput, calls=%fused_computation.38 | convolution fusion | flops 5905580032 | bytes 18612224 | tf_op jit(solution)/shard_map/tc,dc->td/dot_general | solution.py:756
  387.5 9.1 fusion.25
  401.2 19.7 %convolution_convert_fusion.refs_0_ = bf16[2048,5632]{1,0:T(8,128)(2,1)} fusion(bf16[512,5632]{1,0:T(8,128)(2,1)} %get-tuple-element.49, bf16[256,2048]{1,0:T(8,128)(2,1)} %collective-permute-done.10, bf16[256,2048]{1,0:T(8,128)(2,1)} %multiply_convert_fusion), kind=kOutput, calls=%fused_computation | convolution fusion | flops 11826888704 | bytes 30932992 | tf_op jit(solution)/shard_map/td,tc->dc/dot_general | solution.py:760
  420.9 4.4 collective-permute-done.12.refs_1_
  433.1 3.6 collective-permute-start.13
  438.0 11.8 %fusion = f32[512,2048]{1,0:T(8,128)S(1)} fusion(bf16[512,2816]{1,0:T(8,128)(2,1)} %get-tuple-element.48, bf16[2048,5632]{0,1:T(8,128)(2,1)} %all-gather.11.cloned.1.call-done), kind=kOutput, calls=%fused_computation.5 | convolution fusion | flops 5905580032 | bytes 18612224 | tf_op jit(solution)/shard_map/tc,dc->td/dot_general | solution.py:756
  451.0 7.7 collective-permute-done.13
  466.8 11.1 %convolution_convert_fusion.2.refs_1_.refs_7_ = bf16[2048,2816]{1,0:T(8,128)(2,1)} fusion(bf16[512,2816]{1,0:T(8,128)(2,1)} %get-tuple-element.48, bf16[256,2048]{1,0:T(8,128)(2,1)} %get-tuple-element.168, bf16[256,2048]{1,0:T(8,128)(2,1)S(1)} %copy-done.32), kind=kOutput, calls=%fused_computation.2 | convolution fusion | flops 5915541504 | bytes 16515072 | tf_op jit(solution)/shard_map/td,tc->dc/dot_general | solution.py:760
  481.1 12.8 %collective-permute-done.17 = bf16[256,2048]{1,0:T(8,128)(2,1)} collective-permute-done((bf16[256,2048]{1,0:T(8,128)(2,1)}, bf16[256,2048]{1,0:T(8,128)(2,1)}, u32[]{:S(2)}, u32[]{:S(2)}) %collective-permute-start.17) | collective-permute-done | bytes 1048608 | tf_op jit(solution)/shard_map/ppermute | solution.py:775
  498.2 22.4 %collective-permute-done.18 = bf16[256,2048]{1,0:T(8,128)(2,1)S(1)} collective-permute-done((bf16[256,2048]{1,0:T(8,128)(2,1)}, bf16[256,2048]{1,0:T(8,128)(2,1)S(1)}, u32[]{:S(2)}, u32[]{:S(2)}) %collective-permute-start.18) | collective-permute-done | bytes 1048608 | tf_op jit(solution)/shard_map/ppermute | solution.py:775
  525.6 6.0 fusion.18.refs_5_
  531.7 12.3 %gate_backward.1 = (bf16[1024,1024]{1,0:T(8,128)(2,1)}, bf16[1024,3072]{1,0:T(8,128)(2,1)}, f32[8,256]{1,0:T(8,128)}, bf16[4,128,256]{2,1,0:T(8,128)(2,1)}) custom-call(f32[4,128,256]{2,1,0:T(8,128)} %get-tuple-element.55.refs_0_.refs_14_, f32[1024,1024]{1,0:T(8,128)} %get-tuple-element.45.refs_3_.refs_1_, ...), custom_call_target="tpu_custom_call" | custom-call | flops 11000000512 | bytes 11000000 | tf_op jit(solution)/shard_map/gate_backward/pallas_call | solution.py:411
  548.3 9.8 convolution_convert_fusion.3.refs_18_
  563.8 14.7 %collective-permute-done.22 = bf16[4,128,256]{2,1,0:T(8,128)(2,1)} collective-permute-done((bf16[4,128,256]{2,1,0:T(8,128)(2,1)}, bf16[4,128,256]{2,1,0:T(8,128)(2,1)}, u32[]{:S(2)}, u32[]{:S(2)}) %collective-permute-start.22) | collective-permute-done | bytes 262176 | tf_op jit(solution)/shard_map/ppermute | solution.py:748
  584.2 11.3 %collective-permute-done.24 = bf16[4,128,256]{2,1,0:T(8,128)(2,1)} collective-permute-done((bf16[4,128,256]{2,1,0:T(8,128)(2,1)}, bf16[4,128,256]{2,1,0:T(8,128)(2,1)}, u32[]{:S(2)}, u32[]{:S(2)}) %collective-permute-start.24) | collective-permute-done | bytes 262176 | tf_op jit(solution)/shard_map/ppermute | solution.py:748
  599.6 3.6 fusion.38.refs_19_
  603.2 3.7 collective-permute-start.20
  612.8 51.0 %delta_backward.1 = (bf16[1024,3072]{1,0:T(8,128)(2,1)}, f32[8,2048]{1,0:T(8,128)}, f32[8,2048]{1,0:T(8,128)}, f32[8,1024]{1,0:T(8,128)}, f32[4,8,2048]{2,1,0:T(8,128)}, /*index=5*/f32[8,128]{1,0:T(8,128)}) custom-call(s32[2]{0:T(128)} %pad_add_fusion.refs_0_, f32[16]{0:T(128)} %compare_convert_fusion.refs_0_.refs_1_, ...), custom_call_target="tpu_custom_call", output_to_operand_aliasing={{0}: (17, {})} | custom-call | flops 49999998976 | bytes 50000000 | tf_op jit(solution)/shard_map/delta_backward/pallas_call | solution.py:641
  666.3 4.8 fusion.46
  675.9 7.1 fusion.21
  683.1 13.4 %fusion.16 = f32[1024,2048]{1,0:T(8,128)} fusion(bf16[2048,2048]{1,0:T(8,128)(2,1)} %all-gather.7.cloned.1.call-done, bf16[1024,3072]{1,0:T(8,128)(2,1)S(1)} %copy-done.3), kind=kOutput, calls=%fused_computation.20 | convolution fusion | flops 8589934592 | bytes 20971520 | tf_op jit(solution)/shard_map/tc,dc->td/dot_general | solution.py:756
  696.5 6.4 fusion.11
  702.9 6.8 collective-permute-done.31.refs_1_
  721.9 8.3 collective-permute-done.35
  730.3 4.8 collective-permute-done.36
  741.3 5.0 collective-permute-done.37.refs_3_
  747.2 4.2 collective-permute-start.40
  756.9 15.7 %collective-permute-done.40 = bf16[256,2048]{1,0:T(8,128)(2,1)} collective-permute-done((bf16[256,2048]{1,0:T(8,128)(2,1)}, bf16[256,2048]{1,0:T(8,128)(2,1)}, u32[]{:S(2)}, u32[]{:S(2)}) %collective-permute-start.40) | collective-permute-done | bytes 1048608 | tf_op jit(solution)/shard_map/ppermute | solution.py:795
  772.5 4.4 add_convert_fusion.2
  782.6 23.1 %collective-permute-start.42 = (f32[4352]{0:T(1024)S(1)}, f32[4352]{0:T(1024)S(1)}, u32[]{:S(2)}, u32[]{:S(2)}) collective-permute-start(f32[4352]{0:T(1024)S(1)} %slice_add_fusion.2), channel_id=1, source_target_pairs={{0,2},{1,3},{2,0},{3,1},{4,6},{5,7},{6,4},{7,5},{8,10},{9,11},{10,... | collective-permute-start | bytes 52232 | tf_op jit(solution)/shard_map/ppermute | solution.py:834
  815.3 20.1 %convolution_convert_fusion.1.refs_0_ = bf16[2048,3072]{1,0:T(8,128)(2,1)} fusion(bf16[1024,3072]{1,0:T(8,128)(2,1)} %fusion.39, bf16[1024,2048]{1,0:T(8,128)(2,1)} %param.23, f32[2048]{0:T(1024)S(1)} %bitcast.43, f32[1024]{0:T(1024)S(1)} %copy-done.64), kind=kOutput, calls=%fused_computation.1 | convolution fusion | flops 12899581952 | bytes 23080960 | tf_op jit(solution)/shard_map/td,tc->dc/dot_general | solution.py:760
  835.4 4.1 collective-permute-done.46.refs_2_
  856.9 3.9 fusion.33
  860.8 4.6 collective-permute-start.47
  877.6 5.6 collective-permute-done.47.refs_1_
  885.9 4.0 collective-permute-done.50
  893.6 4.7 collective-permute-start.53
  902.1 10.2 %collective-permute-done.51 = bf16[256,2048]{1,0:T(8,128)(2,1)} collective-permute-done((bf16[256,2048]{1,0:T(8,128)(2,1)}, bf16[256,2048]{1,0:T(8,128)(2,1)}, u32[]{:S(2)}, u32[]{:S(2)}) %collective-permute-start.51) | collective-permute-done | bytes 1048608 | tf_op jit(solution)/shard_map/ppermute | solution.py:775
  915.8 28.2 %collective-permute-done.53 = bf16[256,1408]{1,0:T(8,128)(2,1)S(1)} collective-permute-done((bf16[256,1408]{1,0:T(8,128)(2,1)}, bf16[256,1408]{1,0:T(8,128)(2,1)S(1)}, u32[]{:S(2)}, u32[]{:S(2)}) %collective-permute-start.53) | collective-permute-done | bytes 720928 | tf_op jit(solution)/shard_map/ppermute | solution.py:834
  947.5 17.0 %collective-permute-done.52 = bf16[256,2048]{1,0:T(8,128)(2,1)S(1)} collective-permute-done((bf16[256,2048]{1,0:T(8,128)(2,1)}, bf16[256,2048]{1,0:T(8,128)(2,1)S(1)}, u32[]{:S(2)}, u32[]{:S(2)}) %collective-permute-start.52) | collective-permute-done | bytes 1048608 | tf_op jit(solution)/shard_map/ppermute | solution.py:775
  971.2 4.4 convert_element_type.256
  (432 shorter events, 218.9 us)
Async XLA Ops:
  7.3 60.4 %all-gather.7.cloned.1.call-start = ((), (), s32[]{:S(2)}) async-start(), calls=%async_computation.4 | async-start | bytes 9437184 | tf_op jit(solution)/shard_map/all_gather | solution.py:764
  9.8 141.9 %all-gather.9.cloned.1.call-start = ((), (), s32[]{:S(2)}) async-start(), calls=%async_computation.5 | async-start | bytes 9437184 | tf_op jit(solution)/shard_map/all_gather | solution.py:764
  12.1 149.8 %all-gather.15.cloned.1.call-start = ((), (), s32[]{:S(2)}) async-start(), calls=%async_computation.12 | async-start | bytes 3538944 | tf_op jit(solution)/shard_map/all_gather | solution.py:914
  12.2 71.7 %collective-permute-start.1 = (bf16[256,1376]{0,1:T(8,128)(2,1)S(1)}, bf16[256,1376]{0,1:T(8,128)(2,1)S(1)}, u32[]{:S(2)}, u32[]{:S(2)}) collective-permute-start(bf16[256,1376]{0,1:T(8,128)(2,1)S(1)} %copy-done.51), channel_id=1, source_target_pairs={{0,2},{1,3},{2,0},{3,1},{4,6},{5,7},{6,4},{7,5},{8,10},{9,11},{10,... | collective-permute-start | bytes 2113544 | tf_op jit(solution)/shard_map/ppermute | solution.py:834
  16.3 68.7 %collective-permute-start.2 = (bf16[256,1376]{0,1:T(8,128)(2,1)S(1)}, bf16[256,1376]{0,1:T(8,128)(2,1)S(1)}, u32[]{:S(2)}, u32[]{:S(2)}) collective-permute-start(bf16[256,1376]{0,1:T(8,128)(2,1)S(1)} %copy-done.52), channel_id=1, source_target_pairs={{0,2},{1,3},{2,0},{3,1},{4,6},{5,7},{6,4},{7,5},{8,10},{9,11},{10,... | collective-permute-start | bytes 2113544 | tf_op jit(solution)/shard_map/ppermute | solution.py:834
  16.5 69.6 %collective-permute-start.3 = (bf16[256,384]{1,0:T(8,128)(2,1)S(1)}, bf16[256,384]{1,0:T(8,128)(2,1)S(1)}, u32[]{:S(2)}, u32[]{:S(2)}) collective-permute-start(bf16[256,384]{1,0:T(8,128)(2,1)S(1)} %copy.115), channel_id=1, source_target_pairs={{0,2},{1,3},{2,0},{3,1},{4,6},{5,7},{6,4},{7,5},{8,10},{9,11},{10,... | collective-permute-start | bytes 589832 | tf_op jit(solution)/shard_map/ppermute | solution.py:834
  33.1 118.6 %copy-start.63 = (f32[1024]{0:T(1024)}, f32[1024]{0:T(1024)S(1)}, u32[]{:S(2)}) copy-start(f32[1024]{0:T(1024)S(1)} %add_rsqrt_fusion) | copy-start | bytes 12292
  80.4 5.7 collective-permute-start
  117.4 203.4 %all-gather.11.cloned.1.call-start = ((), (), s32[]{:S(2)}) async-start(), calls=%async_computation.6 | async-start | bytes 25952256 | tf_op jit(solution)/shard_map/all_gather | solution.py:764
  122.8 231.3 %all-gather.13.cloned.1.call-start = ((), (), s32[]{:S(2)}) async-start(), calls=%async_computation.7 | async-start | bytes 12976128 | tf_op jit(solution)/shard_map/all_gather | solution.py:764
  123.9 25.8 %collective-permute-start.11 = (bf16[256,992]{0,1:T(8,128)(2,1)S(1)}, bf16[256,992]{0,1:T(8,128)(2,1)S(1)}, u32[]{:S(2)}, u32[]{:S(2)}) collective-permute-start(bf16[256,992]{0,1:T(8,128)(2,1)S(1)} %slice.155), channel_id=1, source_target_pairs={{0,2},{1,3},{2,0},{3,1},{4,6},{5,7},{6,4},{7,5},{8,10},{9,11},{10,... | collective-permute-start | bytes 1523720 | tf_op jit(solution)/shard_map/ppermute | solution.py:834
  150.8 457.4 %reduce-scatter.5.cloned.1.call-start = ((), (), s32[]{:S(2)}) async-start(), calls=%async_computation.8 | async-start | bytes 25952256 | tf_op jit(solution)/shard_map/reduce_scatter | solution.py:768
  182.8 25.1 %collective-permute-start.4 = (bf16[256,2048]{1,0:T(8,128)(2,1)S(1)}, bf16[256,2048]{1,0:T(8,128)(2,1)S(1)}, u32[]{:S(2)}, u32[]{:S(2)}) collective-permute-start(bf16[256,2048]{1,0:T(8,128)(2,1)S(1)} %get-tuple-element.171), channel_id=1, source_target_pairs={{0,1},{4,5},{8,9},{12,13},{16,17},{20,21},{24,25},{28,29}} | collective-permute-start | bytes 3145736 | tf_op jit(solution)/shard_map/ppermute | solution.py:795
  185.3 29.7 %collective-permute-start.7 = (bf16[256,2048]{1,0:T(8,128)(2,1)S(1)}, bf16[256,2048]{1,0:T(8,128)(2,1)}, u32[]{:S(2)}, u32[]{:S(2)}) collective-permute-start(bf16[256,2048]{1,0:T(8,128)(2,1)S(1)} %get-tuple-element.172), channel_id=1, source_target_pairs={{3,2},{7,6},{11,10},{15,14},{19,18},{23,22},{27,26},{31,30}} | collective-permute-start | bytes 3145736 | tf_op jit(solution)/shard_map/ppermute | solution.py:796
  209.5 26.2 %collective-permute-start.5 = (bf16[256,2048]{1,0:T(8,128)(2,1)S(1)}, bf16[256,2048]{1,0:T(8,128)(2,1)}, u32[]{:S(2)}, u32[]{:S(2)}) collective-permute-start(bf16[256,2048]{1,0:T(8,128)(2,1)S(1)} %add_convert_fusion.7), channel_id=1, source_target_pairs={{0,1},{1,2},{4,5},{5,6},{8,9},{9,10},{12,13},{13,14},{16,17},{17,1... | collective-permute-start | bytes 3145736 | tf_op jit(solution)/shard_map/ppermute | solution.py:795
  238.7 6.8 collective-permute-start.8
  239.4 26.0 %collective-permute-start.6 = (bf16[256,2048]{1,0:T(8,128)(2,1)S(1)}, bf16[256,2048]{1,0:T(8,128)(2,1)}, u32[]{:S(2)}, u32[]{:S(2)}) collective-permute-start(bf16[256,2048]{1,0:T(8,128)(2,1)S(1)} %get-tuple-element.169), channel_id=1, source_target_pairs={{0,1},{1,2},{2,3},{4,5},{5,6},{6,7},{8,9},{9,10},{10,11},{12,13},{... | collective-permute-start | bytes 3145736 | tf_op jit(solution)/shard_map/ppermute | solution.py:795
  247.2 43.9 %collective-permute-start.9 = (bf16[256,2048]{1,0:T(8,128)(2,1)S(1)}, bf16[256,2048]{1,0:T(8,128)(2,1)}, u32[]{:S(2)}, u32[]{:S(2)}) collective-permute-start(bf16[256,2048]{1,0:T(8,128)(2,1)S(1)} %add_convert_fusion.4), channel_id=1, source_target_pairs={{3,2},{2,1},{1,0},{7,6},{6,5},{5,4},{11,10},{10,9},{9,8},{15,14},{... | collective-permute-start | bytes 3145736 | tf_op jit(solution)/shard_map/ppermute | solution.py:796
  295.7 21.7 %collective-permute-start.10 = (bf16[256,2048]{1,0:T(8,128)(2,1)}, bf16[256,2048]{1,0:T(8,128)(2,1)}, u32[]{:S(2)}, u32[]{:S(2)}) collective-permute-start(bf16[256,2048]{1,0:T(8,128)(2,1)} %multiply_convert_fusion), channel_id=1, source_target_pairs={{0,1},{1,0},{2,3},{3,2},{4,5},{5,4},{6,7},{7,6},{8,9},{9,8},{10,11... | collective-permute-start | bytes 3145736 | tf_op jit(solution)/shard_map/ppermute | solution.py:834
  399.7 25.5 %collective-permute-start.12 = (bf16[256,2048]{1,0:T(8,128)(2,1)}, bf16[256,2048]{1,0:T(8,128)(2,1)S(1)}, u32[]{:S(2)}, u32[]{:S(2)}) collective-permute-start(bf16[256,2048]{1,0:T(8,128)(2,1)} %slice.282), channel_id=1, source_target_pairs={{0,1},{1,0},{2,3},{3,2},{4,5},{5,4},{6,7},{7,6},{8,9},{9,8},{10,11... | collective-permute-start | bytes 3145736 | tf_op jit(solution)/shard_map/ppermute | solution.py:834
  426.3 415.9 %reduce-scatter.9.cloned.1.call-start = ((), (), s32[]{:S(2)}) async-start(), calls=%async_computation.10 | async-start | bytes 4718592 | tf_op jit(solution)/shard_map/reduce_scatter | solution.py:768
  433.1 25.7 %collective-permute-start.13 = (bf16[256,2048]{1,0:T(8,128)(2,1)}, bf16[256,2048]{1,0:T(8,128)(2,1)S(1)}, u32[]{:S(2)}, u32[]{:S(2)}) collective-permute-start(bf16[256,2048]{1,0:T(8,128)(2,1)} %tie.24), channel_id=1, source_target_pairs={{0,1},{1,2},{2,3},{4,5},{5,6},{6,7},{8,9},{9,10},{10,11},{12,13},{... | collective-permute-start | bytes 3145736 | tf_op jit(solution)/shard_map/ppermute | solution.py:774
  436.7 26.3 %collective-permute-start.16 = (bf16[256,2048]{1,0:T(8,128)(2,1)}, bf16[256,2048]{1,0:T(8,128)(2,1)}, u32[]{:S(2)}, u32[]{:S(2)}) collective-permute-start(bf16[256,2048]{1,0:T(8,128)(2,1)} %tie.24), channel_id=1, source_target_pairs={{3,2},{2,1},{1,0},{7,6},{6,5},{5,4},{11,10},{10,9},{9,8},{15,14},{... | collective-permute-start | bytes 3145736 | tf_op jit(solution)/shard_map/ppermute | solution.py:775
  460.8 17.1 %collective-permute-start.14 = (bf16[256,2048]{1,0:T(8,128)(2,1)}, bf16[256,2048]{1,0:T(8,128)(2,1)}, u32[]{:S(2)}, u32[]{:S(2)}) collective-permute-start(bf16[256,2048]{1,0:T(8,128)(2,1)} %tie.25), channel_id=1, source_target_pairs={{1,2},{2,3},{5,6},{6,7},{9,10},{10,11},{13,14},{14,15},{17,18},{18... | collective-permute-start | bytes 3145736 | tf_op jit(solution)/shard_map/ppermute | solution.py:774
  465.3 28.6 %collective-permute-start.17 = (bf16[256,2048]{1,0:T(8,128)(2,1)}, bf16[256,2048]{1,0:T(8,128)(2,1)}, u32[]{:S(2)}, u32[]{:S(2)}) collective-permute-start(bf16[256,2048]{1,0:T(8,128)(2,1)} %tie.27), channel_id=1, source_target_pairs={{2,1},{1,0},{6,5},{5,4},{10,9},{9,8},{14,13},{13,12},{18,17},{17,1... | collective-permute-start | bytes 3145736 | tf_op jit(solution)/shard_map/ppermute | solution.py:775
  480.3 17.2 %collective-permute-start.15 = (bf16[256,2048]{1,0:T(8,128)(2,1)}, bf16[256,2048]{1,0:T(8,128)(2,1)S(1)}, u32[]{:S(2)}, u32[]{:S(2)}) collective-permute-start(bf16[256,2048]{1,0:T(8,128)(2,1)} %tie.26), channel_id=1, source_target_pairs={{2,3},{6,7},{10,11},{14,15},{18,19},{22,23},{26,27},{30,31}} | collective-permute-start | bytes 3145736 | tf_op jit(solution)/shard_map/ppermute | solution.py:774
  496.2 24.4 %collective-permute-start.18 = (bf16[256,2048]{1,0:T(8,128)(2,1)}, bf16[256,2048]{1,0:T(8,128)(2,1)S(1)}, u32[]{:S(2)}, u32[]{:S(2)}) collective-permute-start(bf16[256,2048]{1,0:T(8,128)(2,1)} %tie.28), channel_id=1, source_target_pairs={{1,0},{5,4},{9,8},{13,12},{17,16},{21,20},{25,24},{29,28}} | collective-permute-start | bytes 3145736 | tf_op jit(solution)/shard_map/ppermute | solution.py:775
  543.9 3.6 collective-permute-start.21
  558.2 286.1 %reduce-scatter.11.cloned.1.call-start = ((), (), s32[]{:S(2)}) async-start(), calls=%async_computation.11 | async-start | bytes 12976128 | tf_op jit(solution)/shard_map/reduce_scatter | solution.py:768
  558.2 20.2 %collective-permute-start.22 = (bf16[4,128,256]{2,1,0:T(8,128)(2,1)}, bf16[4,128,256]{2,1,0:T(8,128)(2,1)}, u32[]{:S(2)}, u32[]{:S(2)}) collective-permute-start(bf16[4,128,256]{2,1,0:T(8,128)(2,1)} %get-tuple-element.57), channel_id=1, source_target_pairs={{8,0},{12,4},{16,8},{20,12},{24,16},{28,20},{9,1},{13,5},{17,9},{2... | collective-permute-start | bytes 786440 | tf_op jit(solution)/shard_map/ppermute | solution.py:748
  559.7 416.0 %reduce-scatter.7.cloned.1.call-start = ((), (), s32[]{:S(2)}) async-start(), calls=%async_computation.9 | async-start | bytes 14155776 | tf_op jit(solution)/shard_map/reduce_scatter | solution.py:768
  559.7 39.9 %collective-permute-start.19 = (bf16[256,2048]{1,0:T(8,128)(2,1)S(1)}, bf16[256,2048]{1,0:T(8,128)(2,1)}, u32[]{:S(2)}, u32[]{:S(2)}) collective-permute-start(bf16[256,2048]{1,0:T(8,128)(2,1)S(1)} %copy-done.35), channel_id=1, source_target_pairs={{0,1},{1,0},{2,3},{3,2},{4,5},{5,4},{6,7},{7,6},{8,9},{9,8},{10,11... | collective-permute-start | bytes 3145736 | tf_op jit(solution)/shard_map/ppermute | solution.py:834
  559.8 22.1 %collective-permute-start.23 = (bf16[4,128,256]{2,1,0:T(8,128)(2,1)}, bf16[4,128,256]{2,1,0:T(8,128)(2,1)}, u32[]{:S(2)}, u32[]{:S(2)}) collective-permute-start(bf16[4,128,256]{2,1,0:T(8,128)(2,1)} %get-tuple-element.57), channel_id=1, source_target_pairs={{12,0},{16,4},{20,8},{24,12},{28,16},{13,1},{17,5},{21,9},{25,13},... | collective-permute-start | bytes 786440 | tf_op jit(solution)/shard_map/ppermute | solution.py:748
  561.1 34.4 %collective-permute-start.24 = (bf16[4,128,256]{2,1,0:T(8,128)(2,1)}, bf16[4,128,256]{2,1,0:T(8,128)(2,1)}, u32[]{:S(2)}, u32[]{:S(2)}) collective-permute-start(bf16[4,128,256]{2,1,0:T(8,128)(2,1)} %get-tuple-element.57), channel_id=1, source_target_pairs={{16,0},{20,4},{24,8},{28,12},{17,1},{21,5},{25,9},{29,13},{18,2},{... | collective-permute-start | bytes 786440 | tf_op jit(solution)/shard_map/ppermute | solution.py:748
  562.4 34.9 %collective-permute-start.25 = (bf16[4,128,256]{2,1,0:T(8,128)(2,1)}, bf16[4,128,256]{2,1,0:T(8,128)(2,1)}, u32[]{:S(2)}, u32[]{:S(2)}) collective-permute-start(bf16[4,128,256]{2,1,0:T(8,128)(2,1)} %get-tuple-element.57), channel_id=1, source_target_pairs={{20,0},{24,4},{28,8},{21,1},{25,5},{29,9},{22,2},{26,6},{30,10},{2... | collective-permute-start | bytes 786440 | tf_op jit(solution)/shard_map/ppermute | solution.py:748
  578.4 19.9 %collective-permute-start.26 = (bf16[4,128,256]{2,1,0:T(8,128)(2,1)}, bf16[4,128,256]{2,1,0:T(8,128)(2,1)S(1)}, u32[]{:S(2)}, u32[]{:S(2)}) collective-permute-start(bf16[4,128,256]{2,1,0:T(8,128)(2,1)} %get-tuple-element.57), channel_id=1, source_target_pairs={{24,0},{28,4},{25,1},{29,5},{26,2},{30,6},{27,3},{31,7}} | collective-permute-start | bytes 786440 | tf_op jit(solution)/shard_map/ppermute | solution.py:748
  581.9 16.5 %collective-permute-start.27 = (bf16[4,128,256]{2,1,0:T(8,128)(2,1)}, bf16[4,128,256]{2,1,0:T(8,128)(2,1)S(1)}, u32[]{:S(2)}, u32[]{:S(2)}) collective-permute-start(bf16[4,128,256]{2,1,0:T(8,128)(2,1)} %get-tuple-element.57), channel_id=1, source_target_pairs={{28,0},{29,1},{30,2},{31,3}} | collective-permute-start | bytes 786440 | tf_op jit(solution)/shard_map/ppermute | solution.py:748
  603.2 69.6 %collective-permute-start.20 = (bf16[256,2048]{1,0:T(8,128)(2,1)}, bf16[256,2048]{1,0:T(8,128)(2,1)S(1)}, u32[]{:S(2)}, u32[]{:S(2)}) collective-permute-start(bf16[256,2048]{1,0:T(8,128)(2,1)} %fusion.38.refs_19_), channel_id=1, source_target_pairs={{0,1},{1,2},{2,3},{4,5},{5,6},{6,7},{8,9},{9,10},{10,11},{12,13},{... | collective-permute-start | bytes 3145736 | tf_op jit(solution)/shard_map/ppermute | solution.py:774
  606.9 65.9 %collective-permute-start.28 = (bf16[256,2048]{1,0:T(8,128)(2,1)}, bf16[256,2048]{1,0:T(8,128)(2,1)S(1)}, u32[]{:S(2)}, u32[]{:S(2)}) collective-permute-start(bf16[256,2048]{1,0:T(8,128)(2,1)} %fusion.38.refs_19_), channel_id=1, source_target_pairs={{3,2},{2,1},{1,0},{7,6},{6,5},{5,4},{11,10},{10,9},{9,8},{15,14},{... | collective-permute-start | bytes 3145736 | tf_op jit(solution)/shard_map/ppermute | solution.py:775
  610.8 62.1 %collective-permute-start.29 = (bf16[256,1408]{1,0:T(8,128)(2,1)}, bf16[256,1408]{1,0:T(8,128)(2,1)S(1)}, u32[]{:S(2)}, u32[]{:S(2)}) collective-permute-start(bf16[256,1408]{1,0:T(8,128)(2,1)} %get-tuple-element.176), channel_id=1, source_target_pairs={{0,2},{1,3},{2,0},{3,1},{4,6},{5,7},{6,4},{7,5},{8,10},{9,11},{10,... | collective-permute-start | bytes 2162696 | tf_op jit(solution)/shard_map/ppermute | solution.py:834
  663.8 11.5 %collective-permute-start.30 = (f32[8,2048]{1,0:T(8,128)}, f32[8,2048]{1,0:T(8,128)S(1)}, u32[]{:S(2)}, u32[]{:S(2)}) collective-permute-start(f32[8,2048]{1,0:T(8,128)} %get-tuple-element.61), channel_id=1, source_target_pairs={{4,0},{8,4},{12,8},{16,12},{20,16},{24,20},{28,24},{5,1},{9,5},{13... | collective-permute-start | bytes 196616 | tf_op jit(solution)/shard_map/ppermute | solution.py:748
  674.4 35.3 %collective-permute-start.31 = (bf16[256,1408]{1,0:T(8,128)(2,1)}, bf16[256,1408]{1,0:T(8,128)(2,1)S(1)}, u32[]{:S(2)}, u32[]{:S(2)}) collective-permute-start(bf16[256,1408]{1,0:T(8,128)(2,1)} %tie.32), channel_id=1, source_target_pairs={{0,2},{1,3},{2,0},{3,1},{4,6},{5,7},{6,4},{7,5},{8,10},{9,11},{10,... | collective-permute-start | bytes 2162696 | tf_op jit(solution)/shard_map/ppermute | solution.py:834
  713.8 24.6 %collective-permute-start.33 = (bf16[256,2048]{1,0:T(8,128)(2,1)}, bf16[256,2048]{1,0:T(8,128)(2,1)}, u32[]{:S(2)}, u32[]{:S(2)}) collective-permute-start(bf16[256,2048]{1,0:T(8,128)(2,1)} %get-tuple-element.166), channel_id=1, source_target_pairs={{0,1},{4,5},{8,9},{12,13},{16,17},{20,21},{24,25},{28,29}} | collective-permute-start | bytes 3145736 | tf_op jit(solution)/shard_map/ppermute | solution.py:795
  718.3 23.0 %collective-permute-start.32 = (bf16[256,2048]{1,0:T(8,128)(2,1)}, bf16[256,2048]{1,0:T(8,128)(2,1)S(1)}, u32[]{:S(2)}, u32[]{:S(2)}) collective-permute-start(bf16[256,2048]{1,0:T(8,128)(2,1)} %tie.34), channel_id=1, source_target_pairs={{1,2},{2,3},{5,6},{6,7},{9,10},{10,11},{13,14},{14,15},{17,18},{18... | collective-permute-start | bytes 3145736 | tf_op jit(solution)/shard_map/ppermute | solution.py:774
  719.0 27.2 %collective-permute-start.37 = (bf16[256,2048]{1,0:T(8,128)(2,1)}, bf16[256,2048]{1,0:T(8,128)(2,1)S(1)}, u32[]{:S(2)}, u32[]{:S(2)}) collective-permute-start(bf16[256,2048]{1,0:T(8,128)(2,1)} %tie.35), channel_id=1, source_target_pairs={{2,1},{1,0},{6,5},{5,4},{10,9},{9,8},{14,13},{13,12},{18,17},{17,1... | collective-permute-start | bytes 3145736 | tf_op jit(solution)/shard_map/ppermute | solution.py:775
  720.4 1.4 collective-permute-start.34
  721.8 8.4 collective-permute-start.35
  730.2 4.9 collective-permute-start.36
  735.8 21.1 %collective-permute-start.44 = (bf16[256,2048]{1,0:T(8,128)(2,1)}, bf16[256,2048]{1,0:T(8,128)(2,1)}, u32[]{:S(2)}, u32[]{:S(2)}) collective-permute-start(bf16[256,2048]{1,0:T(8,128)(2,1)} %get-tuple-element.165), channel_id=1, source_target_pairs={{3,2},{7,6},{11,10},{15,14},{19,18},{23,22},{27,26},{31,30}} | collective-permute-start | bytes 3145736 | tf_op jit(solution)/shard_map/ppermute | solution.py:796
  747.2 25.3 %collective-permute-start.40 = (bf16[256,2048]{1,0:T(8,128)(2,1)}, bf16[256,2048]{1,0:T(8,128)(2,1)}, u32[]{:S(2)}, u32[]{:S(2)}) collective-permute-start(bf16[256,2048]{1,0:T(8,128)(2,1)} %tie.36.refs_1_), channel_id=1, source_target_pairs={{0,1},{1,2},{4,5},{5,6},{8,9},{9,10},{12,13},{13,14},{16,17},{17,1... | collective-permute-start | bytes 3145736 | tf_op jit(solution)/shard_map/ppermute | solution.py:795
  753.7 54.3 %collective-permute-start.38 = (bf16[256,2048]{1,0:T(8,128)(2,1)}, bf16[256,2048]{1,0:T(8,128)(2,1)S(1)}, u32[]{:S(2)}, u32[]{:S(2)}) collective-permute-start(bf16[256,2048]{1,0:T(8,128)(2,1)} %tie.37), channel_id=1, source_target_pairs={{2,3},{6,7},{10,11},{14,15},{18,19},{22,23},{26,27},{30,31}} | collective-permute-start | bytes 3145736 | tf_op jit(solution)/shard_map/ppermute | solution.py:774
  755.4 52.6 %collective-permute-start.39 = (bf16[256,2048]{1,0:T(8,128)(2,1)}, bf16[256,2048]{1,0:T(8,128)(2,1)S(1)}, u32[]{:S(2)}, u32[]{:S(2)}) collective-permute-start(bf16[256,2048]{1,0:T(8,128)(2,1)} %tie.38), channel_id=1, source_target_pairs={{1,0},{5,4},{9,8},{13,12},{17,16},{21,20},{25,24},{29,28}} | collective-permute-start | bytes 3145736 | tf_op jit(solution)/shard_map/ppermute | solution.py:775
  776.9 34.1 %collective-permute-start.45 = (bf16[256,2048]{1,0:T(8,128)(2,1)}, bf16[256,2048]{1,0:T(8,128)(2,1)}, u32[]{:S(2)}, u32[]{:S(2)}) collective-permute-start(bf16[256,2048]{1,0:T(8,128)(2,1)} %tie.40), channel_id=1, source_target_pairs={{3,2},{2,1},{7,6},{6,5},{11,10},{10,9},{15,14},{14,13},{19,18},{18... | collective-permute-start | bytes 3145736 | tf_op jit(solution)/shard_map/ppermute | solution.py:796
  778.6 4.0 collective-permute-start.41
  782.6 24.8 %collective-permute-start.42 = (f32[4352]{0:T(1024)S(1)}, f32[4352]{0:T(1024)S(1)}, u32[]{:S(2)}, u32[]{:S(2)}) collective-permute-start(f32[4352]{0:T(1024)S(1)} %slice_add_fusion.2), channel_id=1, source_target_pairs={{0,2},{1,3},{2,0},{3,1},{4,6},{5,7},{6,4},{7,5},{8,10},{9,11},{10,... | collective-permute-start | bytes 52232 | tf_op jit(solution)/shard_map/ppermute | solution.py:834
  809.4 26.1 %collective-permute-start.43 = (bf16[256,2048]{1,0:T(8,128)(2,1)}, bf16[256,2048]{1,0:T(8,128)(2,1)S(1)}, u32[]{:S(2)}, u32[]{:S(2)}) collective-permute-start(bf16[256,2048]{1,0:T(8,128)(2,1)} %tie.39), channel_id=1, source_target_pairs={{0,1},{1,2},{2,3},{4,5},{5,6},{6,7},{8,9},{9,10},{10,11},{12,13},{... | collective-permute-start | bytes 3145736 | tf_op jit(solution)/shard_map/ppermute | solution.py:795
  814.0 25.5 %collective-permute-start.46 = (bf16[256,2048]{1,0:T(8,128)(2,1)}, bf16[256,2048]{1,0:T(8,128)(2,1)S(1)}, u32[]{:S(2)}, u32[]{:S(2)}) collective-permute-start(bf16[256,2048]{1,0:T(8,128)(2,1)} %tie.41), channel_id=1, source_target_pairs={{3,2},{2,1},{1,0},{7,6},{6,5},{5,4},{11,10},{10,9},{9,8},{15,14},{... | collective-permute-start | bytes 3145736 | tf_op jit(solution)/shard_map/ppermute | solution.py:796
  860.8 22.4 %collective-permute-start.47 = (bf16[256,2048]{1,0:T(8,128)(2,1)}, bf16[256,2048]{1,0:T(8,128)(2,1)}, u32[]{:S(2)}, u32[]{:S(2)}) collective-permute-start(bf16[256,2048]{1,0:T(8,128)(2,1)} %fusion.33), channel_id=1, source_target_pairs={{0,1},{1,2},{2,3},{4,5},{5,6},{6,7},{8,9},{9,10},{10,11},{12,13},{... | collective-permute-start | bytes 3145736 | tf_op jit(solution)/shard_map/ppermute | solution.py:774
  866.8 23.2 %collective-permute-start.50 = (bf16[256,2048]{1,0:T(8,128)(2,1)}, bf16[256,2048]{1,0:T(8,128)(2,1)}, u32[]{:S(2)}, u32[]{:S(2)}) collective-permute-start(bf16[256,2048]{1,0:T(8,128)(2,1)} %fusion.33), channel_id=1, source_target_pairs={{3,2},{2,1},{1,0},{7,6},{6,5},{5,4},{11,10},{10,9},{9,8},{15,14},{... | collective-permute-start | bytes 3145736 | tf_op jit(solution)/shard_map/ppermute | solution.py:775
  883.2 16.1 %collective-permute-start.48 = (bf16[256,2048]{1,0:T(8,128)(2,1)}, bf16[256,2048]{1,0:T(8,128)(2,1)}, u32[]{:S(2)}, u32[]{:S(2)}) collective-permute-start(bf16[256,2048]{1,0:T(8,128)(2,1)} %collective-permute-done.47.refs_1_), channel_id=1, source_target_pairs={{1,2},{2,3},{5,6},{6,7},{9,10},{10,11},{13,14},{14,15},{17,18},{18... | collective-permute-start | bytes 3145736 | tf_op jit(solution)/shard_map/ppermute | solution.py:774
  890.0 22.2 %collective-permute-start.51 = (bf16[256,2048]{1,0:T(8,128)(2,1)}, bf16[256,2048]{1,0:T(8,128)(2,1)}, u32[]{:S(2)}, u32[]{:S(2)}) collective-permute-start(bf16[256,2048]{1,0:T(8,128)(2,1)} %collective-permute-done.50), channel_id=1, source_target_pairs={{2,1},{1,0},{6,5},{5,4},{10,9},{9,8},{14,13},{13,12},{18,17},{17,1... | collective-permute-start | bytes 3145736 | tf_op jit(solution)/shard_map/ppermute | solution.py:775
  893.6 50.4 %collective-permute-start.53 = (bf16[256,1408]{1,0:T(8,128)(2,1)}, bf16[256,1408]{1,0:T(8,128)(2,1)S(1)}, u32[]{:S(2)}, u32[]{:S(2)}) collective-permute-start(bf16[256,1408]{1,0:T(8,128)(2,1)} %tie.43), channel_id=1, source_target_pairs={{0,2},{1,3},{2,0},{3,1},{4,6},{5,7},{6,4},{7,5},{8,10},{9,11},{10,... | collective-permute-start | bytes 2162696 | tf_op jit(solution)/shard_map/ppermute | solution.py:834
  899.3 46.3 %collective-permute-start.49 = (bf16[256,2048]{1,0:T(8,128)(2,1)}, bf16[256,2048]{1,0:T(8,128)(2,1)}, u32[]{:S(2)}, u32[]{:S(2)}) collective-permute-start(bf16[256,2048]{1,0:T(8,128)(2,1)} %collective-permute-done.48), channel_id=1, source_target_pairs={{2,3},{6,7},{10,11},{14,15},{18,19},{22,23},{26,27},{30,31}} | collective-permute-start | bytes 3145736 | tf_op jit(solution)/shard_map/ppermute | solution.py:774
  912.2 52.2 %collective-permute-start.52 = (bf16[256,2048]{1,0:T(8,128)(2,1)}, bf16[256,2048]{1,0:T(8,128)(2,1)S(1)}, u32[]{:S(2)}, u32[]{:S(2)}) collective-permute-start(bf16[256,2048]{1,0:T(8,128)(2,1)} %collective-permute-done.51), channel_id=1, source_target_pairs={{1,0},{5,4},{9,8},{13,12},{17,16},{21,20},{25,24},{29,28}} | collective-permute-start | bytes 3145736 | tf_op jit(solution)/shard_map/ppermute | solution.py:775
  (86 other events, 1087.3 us)
Sparse Core Ops, SparseCore 0:
  10.6 57.0 all-gather.6
  70.2 54.5 all-gather.8
  127.3 32.3 all-gather.14
  161.4 120.9 all-gather.10
  284.1 69.8 all-gather.12
  426.4 150.8 reduce-scatter.4
  581.2 62.0 reduce-scatter.8
  647.1 89.1 reduce-scatter.10
  840.6 91.0 reduce-scatter.6

commit v2 on v1

--- a/solution.py
+++ b/solution.py
@@ -705,7 +705,7 @@
 
 
 def swiglu_kernel(units, gate_ref, up_ref, grad_ref, hidden_ref, grads_ref):
-    gate, up = gate_ref[...], up_ref[...]
+    gate, up = gate_ref[...].astype(f32), up_ref[...].astype(f32)
     act, s = silu(gate)
     hidden_ref[...] = low(act * up)
     grad = grad_ref[...].astype(f32)
@@ -925,8 +925,8 @@
     normed_two = jnp.concatenate([own_two, swapped(own_two, "tp", 1)], axis=0)
     cot_pair = pair(cotangent)
     grad_hidden = low(rows_times(cot_pair, full_down))
-    gate_mlp = rows_times(normed_two, full_mlp_gate)
-    up_mlp = rows_times(tie(normed_two, gate_mlp, grad_hidden), full_mlp_up)
+    gate_mlp = low(rows_times(normed_two, full_mlp_gate))
+    up_mlp = low(rows_times(tie(normed_two, gate_mlp, grad_hidden), full_mlp_up))
     hidden, grad_both = swiglu_both(gate_mlp, up_mlp, grad_hidden)
     grad_two_part = times_back(grad_both[:, :all_units], full_mlp_gate) + times_back(
         grad_both[:, all_units:], full_mlp_up
@@ -982,7 +982,10 @@
         * (tokens_f * lax.rsqrt(jnp.mean(tokens_f * tokens_f, axis=-1, keepdims=True) + eps)),
         axis=0,
     )
-    grad_ab = jnp.einsum("td,ct->dc", normed, dab, preferred_element_type=f32)
+    grad_normed = tie(low(grad_normed), back_up)
+    grad_ab = jnp.einsum(
+        "td,ct->dc", normed, tie(dab, grad_normed), preferred_element_type=f32
+    )
     ab_at, gain_at = 4 * wide, 4 * wide + 2 * heads * width
     hp_at = gain_at + DV + 2 * width
     smalls = [
@@ -993,16 +996,15 @@
         grad_mlp_gain_part,
         jnp.sum(dhp, axis=1),
     ]
-    grad_normed = tie(low(grad_normed), back_up)
     payload, send, total = line_steps(grad_normed, "tp")
     came.append(next_hop(after(came[0], grad_normed), "tp", 1))
     moved = send(0, payload(0, None))
-    by_seq = tree_sum(jnp.concatenate(smalls), "seq", 0)
+    by_seq = exchange_step(exchange_step(jnp.concatenate(smalls), "seq", 0), "seq", 1)
     pair = after(payload(1, moved), by_seq, *came[1])
     came.append(next_hop(after(came[1], pair[0]), "tp", 2))
     moved = send(1, pair)
-    by_all = tree_sum(by_seq[gain_at:hp_at], "tp", 0)
-    moved = send(2, after(payload(2, moved), by_all, *came[2]))
+    by_seq = tree_sum(tie(by_seq, pair[0]), "seq", 2)
+    moved = send(2, after(payload(2, moved), by_seq, *came[2]))
     term_proj = tie(weight_grad(normed, d_all), *moved)
     grad_one = total(moved)
     block_out = assembled(block_own, came, "tp")
@@ -1012,8 +1014,12 @@
     own_grad = low(grad_middle + grad_tokens_norm)
     came = [next_hop((own_grad, own_grad), "tp", 0)]
     came.append(next_hop(came[0], "tp", 1))
-    back_down = swapped(tie(grad_w_down[:, half_units:], came[0][0]), "tp", 2)
     came.append(next_hop(came[1], "tp", 2))
+    back_down = swapped(tie(grad_w_down[:, half_units:], came[2][0]), "tp", 2)
+    by_seq, back_gate, back_up, grad_w_out = (
+        tie(v, came[0][0]) for v in (by_seq, back_gate, back_up, grad_w_out)
+    )
+    by_all = tree_sum(tie(by_seq[gain_at:hp_at], came[1][0]), "tp", 0)
     grad_tokens = assembled(own_grad, came, "tp").astype(f32)
 
     grad_w_gate = grad_w_both[:, :units].astype(f32) + back_gate[:, :units].astype(f32)

time: 998 us -> 978 us (0.980)
  starting transfers between devices: 122 us -> 97.9 us
  waiting for transfers between devices: 358 us -> 377 us
  local copies, waits for them, and re-layouts: 107 us -> 94.4 us
    ppermute x15, starting transfers between devices: 46 us -> 19.8 us  [swapped(): lax.ppermute(block, axis, [(i, i ^ bit) for i in range(lax.axis_size(axis...]
    ppermute x9, waiting for transfers between devices: 71.8 us -> 60.8 us  [next_hop(): lax.ppermute(pair[1], axis, [(n - 1 - i, n - 2 - i) for i in range(step,...]
    ppermute x6, waiting for transfers between devices: 29.7 us -> 39.9 us  [send(): lax.ppermute(pair[1], axis, [(n - 1 - i, n - 2 - i) for i in range(step +...]
    unnamed x207 -> x201, local copies, waits for them, and re-layouts: 49.6 us -> 43.6 us
    convert_element_type x10 -> x11, other arithmetic: 27.7 us -> 26.2 us  [low(): return v.astype(bf16)]
  transfers between devices with their start and end apart: 63 -> 63, of which waited for: 33 -> 31; matrix products, arithmetic and copies ran while one was open for 31% -> 31% of each run, Pallas kernels for 11% -> 11%
where the time goes in v2:
time: 978 us; the launch traced here: 967 us
  waiting for transfers between devices  377 us (39%)
  matrix products  197 us (20%)
  Pallas kernels  114 us (12%)
  starting transfers between devices  97.9 us (10%)
  local copies, waits for them, and re-layouts  94.4 us (10%)
  other arithmetic  61.3 us (6%)
  between operations  16 us (2%)
    ppermute x15, waiting for transfers between devices, swapped(): lax.ppermute(block, axis, [(i, i ^ bit) for i in range(lax.axis_size(axis...  91.7 us
    ppermute x6, waiting for transfers between devices, send(): lax.ppermute(pair[0], axis, [(i, i + 1) for i in range(step + 1)])  84.2 us
    dot_general x6, matrix products, rows_times(): return jnp.dot(left, right, preferred_element_type=f32)  65.6 us
    ppermute x9, waiting for transfers between devices, next_hop(): lax.ppermute(pair[1], axis, [(n - 1 - i, n - 2 - i) for i in range(step,...  60.8 us
    dot_general x4, matrix products, weight_grad(): return low(jnp.einsum('td,tc->dc', left, right, preferred_element_type=f32))  60.7 us
    dot_general x6, matrix products, times_back(): return jnp.einsum('tc,dc->td', left, right, preferred_element_type=f32)  59.1 us
    pallas_call x1, Pallas kernels, backward_local(): pl.pallas_call(ordered(partial(backward_kernel, heads, blocks), 17, 1 + l...  50.5 us
    unnamed x201, local copies, waits for them, and re-layouts  43.6 us
  transfers between devices with their start and end apart: 63, of which 31 were waited for; matrix products, arithmetic and copies ran while one was open for 31% of the time, Pallas kernels for 11%

profile of v2, /device:TPU:0, one launch (start us, length us, event | category | flops | bytes accessed | tf_op | source)
XLA Modules:
  0.0 967.1 jit_solution(15080110955554656590)
XLA Ops:
  12.2 4.1 collective-permute-start.1
  19.6 9.7 %all_gather.21 = bf16[2048,16]{0,1:T(8,128)(2,1)S(1)} all-gather(bf16[256,16]{0,1:T(8,128)(2,1)S(1)} %concatenate.31), channel_id=1, replica_groups=mesh['seq'=8,'tp'=4] {'seq'}, dimensions={0}, use_global_device_ids=true | all-gather | bytes 73728 | tf_op jit(solution)/shard_map/all_gather | solution.py:764
  35.1 32.7 %all-gather.7.cloned.1.call-done = bf16[2048,2048]{1,0:T(8,128)(2,1)} async-done(((bf16[256,2048]{1,0:T(8,128)(2,1)}), bf16[2048,2048]{1,0:T(8,128)(2,1)}) %all-gather.7.cloned.1.call-update) | async-done | bytes 8388624 | tf_op jit(solution)/shard_map/all_gather | solution.py:764
  67.7 12.6 %fusion.57.refs_3_.refs_4_.refs_5_ = f32[1024,2048]{1,0:T(8,128)S(1)} fusion(bf16[2048,2048]{1,0:T(8,128)(2,1)} %all-gather.7.cloned.1.call-done, bf16[1024,2048]{1,0:T(8,128)(2,1)} %param.23, f32[2048]{0:T(1024)S(1)} %bitcast.42, f32[1024]{0:T(1024)S(1)} %add_rsqrt_fusion), kind=kOutput, calls=%fused_computation.159 | convolution fusion | flops 8598323200 | bytes 20983808 | tf_op jit(solution)/shard_map/dot_general | solution.py:752
  86.8 30.5 %delta_forward.1 = (f32[8,1024]{1,0:T(8,128)}, bf16[8,4,128,128]{3,2,1,0:T(8,128)(2,1)}, bf16[1024,1024]{1,0:T(8,128)(2,1)}, bf16[1024,512]{1,0:T(8,128)(2,1)}, ...) custom-call(f32[16]{0:T(128)} %compare_convert_fusion.refs_0_.refs_1, ...), custom_call_target="tpu_custom_call" | custom-call | flops 30000001024 | bytes 30000000 | tf_op jit(solution)/shard_map/delta_forward/pallas_call | solution.py:255
  127.7 21.9 %collective-permute-done.11 = bf16[256,992]{0,1:T(8,128)(2,1)S(1)} collective-permute-done((bf16[256,992]{0,1:T(8,128)(2,1)S(1)}, bf16[256,992]{0,1:T(8,128)(2,1)S(1)}, u32[]{:S(2)}, u32[]{:S(2)}) %collective-permute-start.11) | collective-permute-done | bytes 507936 | tf_op jit(solution)/shard_map/ppermute | solution.py:834
  151.6 10.2 %fusion.26.refs_5_.refs_3_ = f32[1024,1024]{1,0:T(8,128)} fusion(bf16[2048,2048]{1,0:T(8,128)(2,1)} %all-gather.9.cloned.1.call-done, bf16[1024,2048]{1,0:T(8,128)(2,1)} %param.23, f32[2048]{0:T(1024)S(1)} %bitcast.43, f32[1024]{0:T(1024)S(1)} %add_rsqrt_fusion), kind=kOutput, calls=%fused_computation.31 | convolution fusion | flops 4303355904 | bytes 12595200 | tf_op jit(solution)/shard_map/dot_general | solution.py:752
  161.9 11.0 %gate_forward.1 = (bf16[1024,1024]{1,0:T(8,128)(2,1)}, f32[4,128,256]{2,1,0:T(8,128)}, f32[4,128,256]{2,1,0:T(8,128)}) custom-call(s32[2]{0:T(128)} %pad_add_fusion.refs_0_, bf16[8,4,128,384]{3,2,1,0:T(8,128)(2,1)} %bitcast.50, f32[4,128,256]{2,1,0:T(8,128)} %refs_2_.1, f32[1024,1024]{1,0:T(8,128)} %get-tuple-element.45.refs_3_.refs_1_, ...), custom_call_target="tpu_custom_call" | custom-call | flops 10000000000 | bytes 10000000 | tf_op jit(solution)/shard_map/gate_forward/pallas_call | solution.py:340
  172.9 7.6 convolution_convert_fusion.5
  186.8 20.9 %collective-permute-done.4 = bf16[256,2048]{1,0:T(8,128)(2,1)S(1)} collective-permute-done((bf16[256,2048]{1,0:T(8,128)(2,1)S(1)}, bf16[256,2048]{1,0:T(8,128)(2,1)S(1)}, u32[]{:S(2)}, u32[]{:S(2)}) %collective-permute-start.4) | collective-permute-done | bytes 1048608 | tf_op jit(solution)/shard_map/ppermute | solution.py:795
  209.4 5.4 collective-permute-start.5
  214.8 20.8 %collective-permute-done.5 = bf16[256,2048]{1,0:T(8,128)(2,1)} collective-permute-done((bf16[256,2048]{1,0:T(8,128)(2,1)S(1)}, bf16[256,2048]{1,0:T(8,128)(2,1)}, u32[]{:S(2)}, u32[]{:S(2)}) %collective-permute-start.5) | collective-permute-done | bytes 1048608 | tf_op jit(solution)/shard_map/ppermute | solution.py:795
  239.3 6.1 collective-permute-start.6
  248.4 16.9 %collective-permute-done.6 = bf16[256,2048]{1,0:T(8,128)(2,1)} collective-permute-done((bf16[256,2048]{1,0:T(8,128)(2,1)S(1)}, bf16[256,2048]{1,0:T(8,128)(2,1)}, u32[]{:S(2)}, u32[]{:S(2)}) %collective-permute-start.6) | collective-permute-done | bytes 1048608 | tf_op jit(solution)/shard_map/ppermute | solution.py:795
  265.3 25.6 %collective-permute-done.9 = bf16[256,2048]{1,0:T(8,128)(2,1)} collective-permute-done((bf16[256,2048]{1,0:T(8,128)(2,1)S(1)}, bf16[256,2048]{1,0:T(8,128)(2,1)}, u32[]{:S(2)}, u32[]{:S(2)}) %collective-permute-start.9) | collective-permute-done | bytes 1048608 | tf_op jit(solution)/shard_map/ppermute | solution.py:796
  290.9 3.4 multiply_reduce_fusion.2
  300.0 17.2 %collective-permute-done.10 = bf16[256,2048]{1,0:T(8,128)(2,1)} collective-permute-done((bf16[256,2048]{1,0:T(8,128)(2,1)}, bf16[256,2048]{1,0:T(8,128)(2,1)}, u32[]{:S(2)}, u32[]{:S(2)}) %collective-permute-start.10) | collective-permute-done | bytes 1048608 | tf_op jit(solution)/shard_map/ppermute | solution.py:834
  317.3 3.2 pad_maximum_fusion.refs_0_
  320.5 12.0 %fusion.13.refs_1_.gate_ref = bf16[512,2816]{1,0:T(8,128)(2,1)} fusion(bf16[2048,5632]{0,1:T(8,128)(2,1)} %all-gather.11.cloned.1.call-done, bf16[256,2048]{1,0:T(8,128)(2,1)} %collective-permute-done.10, bf16[256,2048]{1,0:T(8,128)(2,1)} %multiply_convert_fusion), kind=kOutput, calls=%fused_computation.19 | convolution fusion | flops 5911216128 | bytes 16515072 | tf_op jit(solution)/shard_map/dot_general | solution.py:752
  332.5 12.7 %fusion.16.refs_2_.grad_ref = bf16[512,2816]{1,0:T(8,128)(2,1)} fusion(bf16[2048,5632]{0,1:T(8,128)(2,1)} %all-gather.11.cloned.1.call-done, bf16[256,2048]{1,0:T(8,128)(2,1)S(1)} %copy-done.48, bf16[256,2048]{1,0:T(8,128)(2,1)S(1)} %get-tuple-element.167), kind=kOutput, calls=%fused_computation.20 | convolution fusion | flops 5911216128 | bytes 16515072 | tf_op jit(solution)/shard_map/dot_general | solution.py:752
  345.2 8.8 all-gather.13.cloned.1.call-done
  354.0 12.1 %convolution_convert_fusion.3.up_ref = bf16[512,2816]{1,0:T(8,128)(2,1)} fusion(bf16[512,2048]{1,0:T(8,128)(2,1)} %tie.29, bf16[2048,2816]{0,1:T(8,128)(2,1)} %all-gather.13.cloned.1.call-done), kind=kOutput, calls=%fused_computation.21 | convolution fusion | flops 5907021824 | bytes 16515072 | tf_op jit(solution)/shard_map/dot_general | solution.py:752
  366.2 10.1 %swiglu_both.1 = (bf16[512,2816]{1,0:T(8,128)(2,1)}, bf16[512,5632]{1,0:T(8,128)(2,1)}) custom-call(bf16[512,2816]{1,0:T(8,128)(2,1)} %fusion.13.refs_1_.gate_ref, bf16[512,2816]{1,0:T(8,128)(2,1)} %convolution_convert_fusion.3.up_ref, bf16[512,2816]{1,0:T(8,128)(2,1)} %fusion.16.refs_2_.grad_ref), custom_call_target="tpu_custom_call" | custom-call | flops 8000000000 | bytes 8000000 | tf_op jit(solution)/shard_map/swiglu_both/pallas_call | solution.py:721
  376.3 10.0 %fusion.31 = f32[512,2048]{1,0:T(8,128)S(1)} fusion(bf16[2048,2816]{0,1:T(8,128)(2,1)} %all-gather.13.cloned.1.call-done, bf16[512,5632]{1,0:T(8,128)(2,1)} %get-tuple-element.49), kind=kOutput, calls=%fused_computation.40 | convolution fusion | flops 5905580032 | bytes 18612224 | tf_op jit(solution)/shard_map/tc,dc->td/dot_general | solution.py:756
  386.3 9.1 fusion.28
  399.9 19.7 %convolution_convert_fusion.refs_0_ = bf16[2048,5632]{1,0:T(8,128)(2,1)} fusion(bf16[512,5632]{1,0:T(8,128)(2,1)} %get-tuple-element.49, bf16[256,2048]{1,0:T(8,128)(2,1)} %collective-permute-done.10, bf16[256,2048]{1,0:T(8,128)(2,1)} %multiply_convert_fusion), kind=kOutput, calls=%fused_computation | convolution fusion | flops 11826888704 | bytes 30932992 | tf_op jit(solution)/shard_map/td,tc->dc/dot_general | solution.py:760
  419.6 4.3 collective-permute-done.12.refs_1_
  431.8 3.6 collective-permute-start.13
  436.7 11.8 %fusion = f32[512,2048]{1,0:T(8,128)S(1)} fusion(bf16[512,2816]{1,0:T(8,128)(2,1)} %get-tuple-element.48, bf16[2048,5632]{0,1:T(8,128)(2,1)} %all-gather.11.cloned.1.call-done), kind=kOutput, calls=%fused_computation.5 | convolution fusion | flops 5905580032 | bytes 18612224 | tf_op jit(solution)/shard_map/tc,dc->td/dot_general | solution.py:756
  449.8 7.7 collective-permute-done.13
  465.5 11.0 %convolution_convert_fusion.2.refs_1_.refs_7_ = bf16[2048,2816]{1,0:T(8,128)(2,1)} fusion(bf16[512,2816]{1,0:T(8,128)(2,1)} %get-tuple-element.48, bf16[256,2048]{1,0:T(8,128)(2,1)} %get-tuple-element.168, bf16[256,2048]{1,0:T(8,128)(2,1)S(1)} %copy-done.33), kind=kOutput, calls=%fused_computation.2 | convolution fusion | flops 5915541504 | bytes 16515072 | tf_op jit(solution)/shard_map/td,tc->dc/dot_general | solution.py:760
  479.8 12.9 %collective-permute-done.17 = bf16[256,2048]{1,0:T(8,128)(2,1)} collective-permute-done((bf16[256,2048]{1,0:T(8,128)(2,1)}, bf16[256,2048]{1,0:T(8,128)(2,1)}, u32[]{:S(2)}, u32[]{:S(2)}) %collective-permute-start.17) | collective-permute-done | bytes 1048608 | tf_op jit(solution)/shard_map/ppermute | solution.py:775
  497.1 22.5 %collective-permute-done.18 = bf16[256,2048]{1,0:T(8,128)(2,1)} collective-permute-done((bf16[256,2048]{1,0:T(8,128)(2,1)}, bf16[256,2048]{1,0:T(8,128)(2,1)}, u32[]{:S(2)}, u32[]{:S(2)}) %collective-permute-start.18) | collective-permute-done | bytes 1048608 | tf_op jit(solution)/shard_map/ppermute | solution.py:775
  525.9 6.1 fusion.21.refs_5_
  532.0 11.6 %gate_backward.1 = (bf16[1024,1024]{1,0:T(8,128)(2,1)}, bf16[1024,3072]{1,0:T(8,128)(2,1)}, f32[8,256]{1,0:T(8,128)}, bf16[4,128,256]{2,1,0:T(8,128)(2,1)}) custom-call(f32[4,128,256]{2,1,0:T(8,128)} %get-tuple-element.55.refs_0_.refs_14_, f32[1024,1024]{1,0:T(8,128)} %get-tuple-element.45.refs_3_.refs_1_, ...), custom_call_target="tpu_custom_call" | custom-call | flops 11000000512 | bytes 11000000 | tf_op jit(solution)/shard_map/gate_backward/pallas_call | solution.py:411
  552.3 18.7 %collective-permute-done.22 = bf16[4,128,256]{2,1,0:T(8,128)(2,1)S(1)} collective-permute-done((bf16[4,128,256]{2,1,0:T(8,128)(2,1)}, bf16[4,128,256]{2,1,0:T(8,128)(2,1)S(1)}, u32[]{:S(2)}, u32[]{:S(2)}) %collective-permute-start.22) | collective-permute-done | bytes 262176 | tf_op jit(solution)/shard_map/ppermute | solution.py:748
  574.2 6.0 collective-permute-done.24
  582.3 9.7 collective-permute-done.26
  593.5 9.8 %convolution_convert_fusion.4.refs_18_ = bf16[2048,1024]{1,0:T(8,128)(2,1)} fusion(bf16[1024,2048]{1,0:T(8,128)(2,1)} %tie.37, bf16[1024,1024]{1,0:T(8,128)(2,1)} %get-tuple-element.47), kind=kOutput, calls=%fused_computation.24 | convolution fusion | flops 4297064448 | bytes 10485760 | tf_op jit(solution)/shard_map/td,tc->dc/dot_general | solution.py:760
  605.7 3.3 collective-permute-start.20
  615.3 50.5 %delta_backward.1 = (bf16[1024,3072]{1,0:T(8,128)(2,1)}, f32[8,2048]{1,0:T(8,128)}, f32[8,2048]{1,0:T(8,128)}, f32[8,1024]{1,0:T(8,128)}, f32[4,8,2048]{2,1,0:T(8,128)}, /*index=5*/f32[8,128]{1,0:T(8,128)}) custom-call(s32[2]{0:T(128)} %pad_add_fusion.refs_0_, f32[16]{0:T(128)} %compare_convert_fusion.refs_0_.refs_1_, ...), custom_call_target="tpu_custom_call", output_to_operand_aliasing={{0}: (17, {})} | custom-call | flops 49999998976 | bytes 50000000 | tf_op jit(solution)/shard_map/delta_backward/pallas_call | solution.py:641
  674.1 7.1 fusion.24
  681.3 13.4 %fusion.19 = f32[1024,2048]{1,0:T(8,128)} fusion(bf16[2048,2048]{1,0:T(8,128)(2,1)} %all-gather.7.cloned.1.call-done, bf16[1024,3072]{1,0:T(8,128)(2,1)S(1)} %copy-done.4), kind=kOutput, calls=%fused_computation.22 | convolution fusion | flops 8589934592 | bytes 20971520 | tf_op jit(solution)/shard_map/tc,dc->td/dot_general | solution.py:756
  694.7 6.2 fusion.11
  700.9 6.7 collective-permute-done.31.refs_1_.refs_0_
  712.1 4.3 collective-permute-start.33
  716.4 3.8 fusion.54
  725.3 3.6 collective-permute-done.35
  729.6 8.4 collective-permute-done.33
  740.9 6.7 collective-permute-done.36.refs_3_
  755.4 17.1 %collective-permute-done.39 = bf16[256,2048]{1,0:T(8,128)(2,1)} collective-permute-done((bf16[256,2048]{1,0:T(8,128)(2,1)}, bf16[256,2048]{1,0:T(8,128)(2,1)}, u32[]{:S(2)}, u32[]{:S(2)}) %collective-permute-start.39) | collective-permute-done | bytes 1048608 | tf_op jit(solution)/shard_map/ppermute | solution.py:795
  772.5 4.5 add_convert_fusion.2
  778.7 6.9 collective-permute-done.40
  788.5 3.7 collective-permute-start.41
  796.4 20.2 %convolution_convert_fusion.1.refs_0_ = bf16[2048,3072]{1,0:T(8,128)(2,1)} fusion(bf16[1024,3072]{1,0:T(8,128)(2,1)} %fusion.42, bf16[1024,2048]{1,0:T(8,128)(2,1)} %param.23, f32[2048]{0:T(1024)S(1)} %bitcast.45, f32[1024]{0:T(1024)S(1)} %copy-done.63), kind=kOutput, calls=%fused_computation.1 | convolution fusion | flops 12899581952 | bytes 23080960 | tf_op jit(solution)/shard_map/td,tc->dc/dot_general | solution.py:760
  816.6 14.3 %collective-permute-done.44.refs_2_ = bf16[256,2048]{1,0:T(8,128)(2,1)S(1)} collective-permute-done((bf16[256,2048]{1,0:T(8,128)(2,1)}, bf16[256,2048]{1,0:T(8,128)(2,1)S(1)}, u32[]{:S(2)}, u32[]{:S(2)}) %collective-permute-start.44) | collective-permute-done | bytes 1048608 | tf_op jit(solution)/shard_map/ppermute | solution.py:796
  841.9 4.9 collective-permute-start.45
  848.9 15.5 %collective-permute-done.45.refs_1_ = bf16[256,2048]{1,0:T(8,128)(2,1)} collective-permute-done((bf16[256,2048]{1,0:T(8,128)(2,1)S(1)}, bf16[256,2048]{1,0:T(8,128)(2,1)}, u32[]{:S(2)}, u32[]{:S(2)}) %collective-permute-start.45) | collective-permute-done | bytes 1048608 | tf_op jit(solution)/shard_map/ppermute | solution.py:774
  866.2 3.7 collective-permute-done.48
  880.1 14.6 %collective-permute-done.49 = bf16[256,2048]{1,0:T(8,128)(2,1)} collective-permute-done((bf16[256,2048]{1,0:T(8,128)(2,1)}, bf16[256,2048]{1,0:T(8,128)(2,1)}, u32[]{:S(2)}, u32[]{:S(2)}) %collective-permute-start.49) | collective-permute-done | bytes 1048608 | tf_op jit(solution)/shard_map/ppermute | solution.py:775
  897.5 3.6 collective-permute-start.51
  902.3 15.1 %collective-permute-done.51 = f32[4352]{0:T(1024)S(1)} collective-permute-done((f32[4352]{0:T(1024)}, f32[4352]{0:T(1024)S(1)}, u32[]{:S(2)}, u32[]{:S(2)}) %collective-permute-start.51) | collective-permute-done | bytes 17440 | tf_op jit(solution)/shard_map/ppermute | solution.py:834
  925.3 13.0 %collective-permute-done.52 = f32[4352]{0:T(1024)S(1)} collective-permute-done((f32[4352]{0:T(1024)S(1)}, f32[4352]{0:T(1024)S(1)}, u32[]{:S(2)}, u32[]{:S(2)}) %collective-permute-start.52) | collective-permute-done | bytes 17440 | tf_op jit(solution)/shard_map/ppermute | solution.py:834
  947.6 4.4 convert_element_type.264
  (432 shorter events, 205.1 us)
Async XLA Ops:
  7.3 60.4 %all-gather.7.cloned.1.call-start = ((), (), s32[]{:S(2)}) async-start(), calls=%async_computation.4 | async-start | bytes 9437184 | tf_op jit(solution)/shard_map/all_gather | solution.py:764
  9.8 141.9 %all-gather.9.cloned.1.call-start = ((), (), s32[]{:S(2)}) async-start(), calls=%async_computation.5 | async-start | bytes 9437184 | tf_op jit(solution)/shard_map/all_gather | solution.py:764
  12.1 149.8 %all-gather.15.cloned.1.call-start = ((), (), s32[]{:S(2)}) async-start(), calls=%async_computation.12 | async-start | bytes 3538944 | tf_op jit(solution)/shard_map/all_gather | solution.py:914
  12.2 71.7 %collective-permute-start.1 = (bf16[256,1376]{0,1:T(8,128)(2,1)S(1)}, bf16[256,1376]{0,1:T(8,128)(2,1)S(1)}, u32[]{:S(2)}, u32[]{:S(2)}) collective-permute-start(bf16[256,1376]{0,1:T(8,128)(2,1)S(1)} %copy-done.50), channel_id=1, source_target_pairs={{0,2},{1,3},{2,0},{3,1},{4,6},{5,7},{6,4},{7,5},{8,10},{9,11},{10,... | collective-permute-start | bytes 2113544 | tf_op jit(solution)/shard_map/ppermute | solution.py:834
  16.3 68.7 %collective-permute-start.2 = (bf16[256,1376]{0,1:T(8,128)(2,1)S(1)}, bf16[256,1376]{0,1:T(8,128)(2,1)S(1)}, u32[]{:S(2)}, u32[]{:S(2)}) collective-permute-start(bf16[256,1376]{0,1:T(8,128)(2,1)S(1)} %copy-done.51), channel_id=1, source_target_pairs={{0,2},{1,3},{2,0},{3,1},{4,6},{5,7},{6,4},{7,5},{8,10},{9,11},{10,... | collective-permute-start | bytes 2113544 | tf_op jit(solution)/shard_map/ppermute | solution.py:834
  16.5 69.6 %collective-permute-start.3 = (bf16[256,384]{1,0:T(8,128)(2,1)S(1)}, bf16[256,384]{1,0:T(8,128)(2,1)S(1)}, u32[]{:S(2)}, u32[]{:S(2)}) collective-permute-start(bf16[256,384]{1,0:T(8,128)(2,1)S(1)} %copy.122), channel_id=1, source_target_pairs={{0,2},{1,3},{2,0},{3,1},{4,6},{5,7},{6,4},{7,5},{8,10},{9,11},{10,... | collective-permute-start | bytes 589832 | tf_op jit(solution)/shard_map/ppermute | solution.py:834
  33.1 118.5 %copy-start.62 = (f32[1024]{0:T(1024)}, f32[1024]{0:T(1024)S(1)}, u32[]{:S(2)}) copy-start(f32[1024]{0:T(1024)S(1)} %add_rsqrt_fusion) | copy-start | bytes 12292
  80.4 5.7 collective-permute-start
  117.4 203.2 %all-gather.11.cloned.1.call-start = ((), (), s32[]{:S(2)}) async-start(), calls=%async_computation.6 | async-start | bytes 25952256 | tf_op jit(solution)/shard_map/all_gather | solution.py:764
  122.7 231.3 %all-gather.13.cloned.1.call-start = ((), (), s32[]{:S(2)}) async-start(), calls=%async_computation.7 | async-start | bytes 12976128 | tf_op jit(solution)/shard_map/all_gather | solution.py:764
  123.9 25.8 %collective-permute-start.11 = (bf16[256,992]{0,1:T(8,128)(2,1)S(1)}, bf16[256,992]{0,1:T(8,128)(2,1)S(1)}, u32[]{:S(2)}, u32[]{:S(2)}) collective-permute-start(bf16[256,992]{0,1:T(8,128)(2,1)S(1)} %slice.153), channel_id=1, source_target_pairs={{0,2},{1,3},{2,0},{3,1},{4,6},{5,7},{6,4},{7,5},{8,10},{9,11},{10,... | collective-permute-start | bytes 1523720 | tf_op jit(solution)/shard_map/ppermute | solution.py:834
  150.8 459.6 %reduce-scatter.5.cloned.1.call-start = ((), (), s32[]{:S(2)}) async-start(), calls=%async_computation.8 | async-start | bytes 25952256 | tf_op jit(solution)/shard_map/reduce_scatter | solution.py:768
  182.7 25.0 %collective-permute-start.4 = (bf16[256,2048]{1,0:T(8,128)(2,1)S(1)}, bf16[256,2048]{1,0:T(8,128)(2,1)S(1)}, u32[]{:S(2)}, u32[]{:S(2)}) collective-permute-start(bf16[256,2048]{1,0:T(8,128)(2,1)S(1)} %get-tuple-element.171), channel_id=1, source_target_pairs={{0,1},{4,5},{8,9},{12,13},{16,17},{20,21},{24,25},{28,29}} | collective-permute-start | bytes 3145736 | tf_op jit(solution)/shard_map/ppermute | solution.py:795
  185.2 29.6 %collective-permute-start.7 = (bf16[256,2048]{1,0:T(8,128)(2,1)S(1)}, bf16[256,2048]{1,0:T(8,128)(2,1)}, u32[]{:S(2)}, u32[]{:S(2)}) collective-permute-start(bf16[256,2048]{1,0:T(8,128)(2,1)S(1)} %get-tuple-element.172), channel_id=1, source_target_pairs={{3,2},{7,6},{11,10},{15,14},{19,18},{23,22},{27,26},{31,30}} | collective-permute-start | bytes 3145736 | tf_op jit(solution)/shard_map/ppermute | solution.py:796
  209.4 26.2 %collective-permute-start.5 = (bf16[256,2048]{1,0:T(8,128)(2,1)S(1)}, bf16[256,2048]{1,0:T(8,128)(2,1)}, u32[]{:S(2)}, u32[]{:S(2)}) collective-permute-start(bf16[256,2048]{1,0:T(8,128)(2,1)S(1)} %add_convert_fusion.7), channel_id=1, source_target_pairs={{0,1},{1,2},{4,5},{5,6},{8,9},{9,10},{12,13},{13,14},{16,17},{17,1... | collective-permute-start | bytes 3145736 | tf_op jit(solution)/shard_map/ppermute | solution.py:795
  238.6 6.8 collective-permute-start.8
  239.3 26.0 %collective-permute-start.6 = (bf16[256,2048]{1,0:T(8,128)(2,1)S(1)}, bf16[256,2048]{1,0:T(8,128)(2,1)}, u32[]{:S(2)}, u32[]{:S(2)}) collective-permute-start(bf16[256,2048]{1,0:T(8,128)(2,1)S(1)} %get-tuple-element.169), channel_id=1, source_target_pairs={{0,1},{1,2},{2,3},{4,5},{5,6},{6,7},{8,9},{9,10},{10,11},{12,13},{... | collective-permute-start | bytes 3145736 | tf_op jit(solution)/shard_map/ppermute | solution.py:795
  247.1 43.8 %collective-permute-start.9 = (bf16[256,2048]{1,0:T(8,128)(2,1)S(1)}, bf16[256,2048]{1,0:T(8,128)(2,1)}, u32[]{:S(2)}, u32[]{:S(2)}) collective-permute-start(bf16[256,2048]{1,0:T(8,128)(2,1)S(1)} %add_convert_fusion.4), channel_id=1, source_target_pairs={{3,2},{2,1},{1,0},{7,6},{6,5},{5,4},{11,10},{10,9},{9,8},{15,14},{... | collective-permute-start | bytes 3145736 | tf_op jit(solution)/shard_map/ppermute | solution.py:796
  295.6 21.7 %collective-permute-start.10 = (bf16[256,2048]{1,0:T(8,128)(2,1)}, bf16[256,2048]{1,0:T(8,128)(2,1)}, u32[]{:S(2)}, u32[]{:S(2)}) collective-permute-start(bf16[256,2048]{1,0:T(8,128)(2,1)} %multiply_convert_fusion), channel_id=1, source_target_pairs={{0,1},{1,0},{2,3},{3,2},{4,5},{5,4},{6,7},{7,6},{8,9},{9,8},{10,11... | collective-permute-start | bytes 3145736 | tf_op jit(solution)/shard_map/ppermute | solution.py:834
  398.5 25.5 %collective-permute-start.12 = (bf16[256,2048]{1,0:T(8,128)(2,1)}, bf16[256,2048]{1,0:T(8,128)(2,1)S(1)}, u32[]{:S(2)}, u32[]{:S(2)}) collective-permute-start(bf16[256,2048]{1,0:T(8,128)(2,1)} %slice.280), channel_id=1, source_target_pairs={{0,1},{1,0},{2,3},{3,2},{4,5},{5,4},{6,7},{7,6},{8,9},{9,8},{10,11... | collective-permute-start | bytes 3145736 | tf_op jit(solution)/shard_map/ppermute | solution.py:834
  425.0 408.5 %reduce-scatter.11.cloned.1.call-start = ((), (), s32[]{:S(2)}) async-start(), calls=%async_computation.11 | async-start | bytes 12976128 | tf_op jit(solution)/shard_map/reduce_scatter | solution.py:768
  431.8 25.7 %collective-permute-start.13 = (bf16[256,2048]{1,0:T(8,128)(2,1)}, bf16[256,2048]{1,0:T(8,128)(2,1)S(1)}, u32[]{:S(2)}, u32[]{:S(2)}) collective-permute-start(bf16[256,2048]{1,0:T(8,128)(2,1)} %tie.31), channel_id=1, source_target_pairs={{0,1},{1,2},{2,3},{4,5},{5,6},{6,7},{8,9},{9,10},{10,11},{12,13},{... | collective-permute-start | bytes 3145736 | tf_op jit(solution)/shard_map/ppermute | solution.py:774
  435.4 26.3 %collective-permute-start.16 = (bf16[256,2048]{1,0:T(8,128)(2,1)}, bf16[256,2048]{1,0:T(8,128)(2,1)}, u32[]{:S(2)}, u32[]{:S(2)}) collective-permute-start(bf16[256,2048]{1,0:T(8,128)(2,1)} %tie.31), channel_id=1, source_target_pairs={{3,2},{2,1},{1,0},{7,6},{6,5},{5,4},{11,10},{10,9},{9,8},{15,14},{... | collective-permute-start | bytes 3145736 | tf_op jit(solution)/shard_map/ppermute | solution.py:775
  459.5 17.1 %collective-permute-start.14 = (bf16[256,2048]{1,0:T(8,128)(2,1)}, bf16[256,2048]{1,0:T(8,128)(2,1)}, u32[]{:S(2)}, u32[]{:S(2)}) collective-permute-start(bf16[256,2048]{1,0:T(8,128)(2,1)} %tie.32), channel_id=1, source_target_pairs={{1,2},{2,3},{5,6},{6,7},{9,10},{10,11},{13,14},{14,15},{17,18},{18... | collective-permute-start | bytes 3145736 | tf_op jit(solution)/shard_map/ppermute | solution.py:774
  464.0 28.7 %collective-permute-start.17 = (bf16[256,2048]{1,0:T(8,128)(2,1)}, bf16[256,2048]{1,0:T(8,128)(2,1)}, u32[]{:S(2)}, u32[]{:S(2)}) collective-permute-start(bf16[256,2048]{1,0:T(8,128)(2,1)} %tie.34), channel_id=1, source_target_pairs={{2,1},{1,0},{6,5},{5,4},{10,9},{9,8},{14,13},{13,12},{18,17},{17,1... | collective-permute-start | bytes 3145736 | tf_op jit(solution)/shard_map/ppermute | solution.py:775
  479.1 17.4 %collective-permute-start.15 = (bf16[256,2048]{1,0:T(8,128)(2,1)}, bf16[256,2048]{1,0:T(8,128)(2,1)S(1)}, u32[]{:S(2)}, u32[]{:S(2)}) collective-permute-start(bf16[256,2048]{1,0:T(8,128)(2,1)} %tie.33), channel_id=1, source_target_pairs={{2,3},{6,7},{10,11},{14,15},{18,19},{22,23},{26,27},{30,31}} | collective-permute-start | bytes 3145736 | tf_op jit(solution)/shard_map/ppermute | solution.py:774
  495.1 24.5 %collective-permute-start.18 = (bf16[256,2048]{1,0:T(8,128)(2,1)}, bf16[256,2048]{1,0:T(8,128)(2,1)}, u32[]{:S(2)}, u32[]{:S(2)}) collective-permute-start(bf16[256,2048]{1,0:T(8,128)(2,1)} %tie.35), channel_id=1, source_target_pairs={{1,0},{5,4},{9,8},{13,12},{17,16},{21,20},{25,24},{29,28}} | collective-permute-start | bytes 3145736 | tf_op jit(solution)/shard_map/ppermute | solution.py:775
  496.4 421.8 %reduce-scatter.9.cloned.1.call-start = ((), (), s32[]{:S(2)}) async-start(), calls=%async_computation.10 | async-start | bytes 4718592 | tf_op jit(solution)/shard_map/reduce_scatter | solution.py:768
  543.6 6.7 collective-permute-start.21
  545.0 26.0 %collective-permute-start.22 = (bf16[4,128,256]{2,1,0:T(8,128)(2,1)}, bf16[4,128,256]{2,1,0:T(8,128)(2,1)S(1)}, u32[]{:S(2)}, u32[]{:S(2)}) collective-permute-start(bf16[4,128,256]{2,1,0:T(8,128)(2,1)} %get-tuple-element.57), channel_id=1, source_target_pairs={{8,0},{12,4},{16,8},{20,12},{24,16},{28,20},{9,1},{13,5},{17,9},{2... | collective-permute-start | bytes 786440 | tf_op jit(solution)/shard_map/ppermute | solution.py:748
  546.4 27.1 %collective-permute-start.23 = (bf16[4,128,256]{2,1,0:T(8,128)(2,1)}, bf16[4,128,256]{2,1,0:T(8,128)(2,1)S(1)}, u32[]{:S(2)}, u32[]{:S(2)}) collective-permute-start(bf16[4,128,256]{2,1,0:T(8,128)(2,1)} %get-tuple-element.57), channel_id=1, source_target_pairs={{12,0},{16,4},{20,8},{24,12},{28,16},{13,1},{17,5},{21,9},{25,13},... | collective-permute-start | bytes 786440 | tf_op jit(solution)/shard_map/ppermute | solution.py:748
  547.7 32.5 %collective-permute-start.24 = (bf16[4,128,256]{2,1,0:T(8,128)(2,1)}, bf16[4,128,256]{2,1,0:T(8,128)(2,1)S(1)}, u32[]{:S(2)}, u32[]{:S(2)}) collective-permute-start(bf16[4,128,256]{2,1,0:T(8,128)(2,1)} %get-tuple-element.57), channel_id=1, source_target_pairs={{16,0},{20,4},{24,8},{28,12},{17,1},{21,5},{25,9},{29,13},{18,2},{... | collective-permute-start | bytes 786440 | tf_op jit(solution)/shard_map/ppermute | solution.py:748
  549.0 32.7 %collective-permute-start.25 = (bf16[4,128,256]{2,1,0:T(8,128)(2,1)}, bf16[4,128,256]{2,1,0:T(8,128)(2,1)S(1)}, u32[]{:S(2)}, u32[]{:S(2)}) collective-permute-start(bf16[4,128,256]{2,1,0:T(8,128)(2,1)} %get-tuple-element.57), channel_id=1, source_target_pairs={{20,0},{24,4},{28,8},{21,1},{25,5},{29,9},{22,2},{26,6},{30,10},{2... | collective-permute-start | bytes 786440 | tf_op jit(solution)/shard_map/ppermute | solution.py:748
  550.3 41.7 %collective-permute-start.26 = (bf16[4,128,256]{2,1,0:T(8,128)(2,1)}, bf16[4,128,256]{2,1,0:T(8,128)(2,1)S(1)}, u32[]{:S(2)}, u32[]{:S(2)}) collective-permute-start(bf16[4,128,256]{2,1,0:T(8,128)(2,1)} %get-tuple-element.57), channel_id=1, source_target_pairs={{24,0},{28,4},{25,1},{29,5},{26,2},{30,6},{27,3},{31,7}} | collective-permute-start | bytes 786440 | tf_op jit(solution)/shard_map/ppermute | solution.py:748
  571.1 21.7 %collective-permute-start.27 = (bf16[4,128,256]{2,1,0:T(8,128)(2,1)}, bf16[4,128,256]{2,1,0:T(8,128)(2,1)S(1)}, u32[]{:S(2)}, u32[]{:S(2)}) collective-permute-start(bf16[4,128,256]{2,1,0:T(8,128)(2,1)} %get-tuple-element.57), channel_id=1, source_target_pairs={{28,0},{29,1},{30,2},{31,3}} | collective-permute-start | bytes 786440 | tf_op jit(solution)/shard_map/ppermute | solution.py:748
  573.5 29.7 %collective-permute-start.19 = (bf16[256,2048]{1,0:T(8,128)(2,1)}, bf16[256,2048]{1,0:T(8,128)(2,1)}, u32[]{:S(2)}, u32[]{:S(2)}) collective-permute-start(bf16[256,2048]{1,0:T(8,128)(2,1)} %tie.36), channel_id=1, source_target_pairs={{0,1},{1,0},{2,3},{3,2},{4,5},{5,4},{6,7},{7,6},{8,9},{9,8},{10,11... | collective-permute-start | bytes 3145736 | tf_op jit(solution)/shard_map/ppermute | solution.py:834
  605.7 64.2 %collective-permute-start.20 = (bf16[256,2048]{1,0:T(8,128)(2,1)S(1)}, bf16[256,2048]{1,0:T(8,128)(2,1)S(1)}, u32[]{:S(2)}, u32[]{:S(2)}) collective-permute-start(bf16[256,2048]{1,0:T(8,128)(2,1)S(1)} %fusion.41.refs_19_), channel_id=1, source_target_pairs={{0,1},{1,2},{2,3},{4,5},{5,6},{6,7},{8,9},{9,10},{10,11},{12,13},{... | collective-permute-start | bytes 3145736 | tf_op jit(solution)/shard_map/ppermute | solution.py:774
  609.0 61.9 %collective-permute-start.28 = (bf16[256,2048]{1,0:T(8,128)(2,1)S(1)}, bf16[256,2048]{1,0:T(8,128)(2,1)S(1)}, u32[]{:S(2)}, u32[]{:S(2)}) collective-permute-start(bf16[256,2048]{1,0:T(8,128)(2,1)S(1)} %fusion.41.refs_19_), channel_id=1, source_target_pairs={{3,2},{2,1},{1,0},{7,6},{6,5},{5,4},{11,10},{10,9},{9,8},{15,14},{... | collective-permute-start | bytes 3145736 | tf_op jit(solution)/shard_map/ppermute | solution.py:775
  613.3 58.6 %collective-permute-start.29 = (bf16[256,1408]{1,0:T(8,128)(2,1)}, bf16[256,1408]{1,0:T(8,128)(2,1)}, u32[]{:S(2)}, u32[]{:S(2)}) collective-permute-start(bf16[256,1408]{1,0:T(8,128)(2,1)} %get-tuple-element.176), channel_id=1, source_target_pairs={{0,2},{1,3},{2,0},{3,1},{4,6},{5,7},{6,4},{7,5},{8,10},{9,11},{10,... | collective-permute-start | bytes 2162696 | tf_op jit(solution)/shard_map/ppermute | solution.py:834
  666.6 6.9 collective-permute-start.30
  672.2 35.4 %collective-permute-start.31 = (bf16[256,1408]{1,0:T(8,128)(2,1)}, bf16[256,1408]{1,0:T(8,128)(2,1)S(1)}, u32[]{:S(2)}, u32[]{:S(2)}) collective-permute-start(bf16[256,1408]{1,0:T(8,128)(2,1)} %tie.39), channel_id=1, source_target_pairs={{0,2},{1,3},{2,0},{3,1},{4,6},{5,7},{6,4},{7,5},{8,10},{9,11},{10,... | collective-permute-start | bytes 2162696 | tf_op jit(solution)/shard_map/ppermute | solution.py:834
  708.5 32.4 %collective-permute-start.32 = (bf16[256,2048]{1,0:T(8,128)(2,1)}, bf16[256,2048]{1,0:T(8,128)(2,1)S(1)}, u32[]{:S(2)}, u32[]{:S(2)}) collective-permute-start(bf16[256,2048]{1,0:T(8,128)(2,1)} %tie.41), channel_id=1, source_target_pairs={{1,2},{2,3},{5,6},{6,7},{9,10},{10,11},{13,14},{14,15},{17,18},{18... | collective-permute-start | bytes 3145736 | tf_op jit(solution)/shard_map/ppermute | solution.py:774
  712.1 25.9 %collective-permute-start.33 = (bf16[256,2048]{1,0:T(8,128)(2,1)S(1)}, bf16[256,2048]{1,0:T(8,128)(2,1)}, u32[]{:S(2)}, u32[]{:S(2)}) collective-permute-start(bf16[256,2048]{1,0:T(8,128)(2,1)S(1)} %get-tuple-element.166), channel_id=1, source_target_pairs={{0,1},{4,5},{8,9},{12,13},{16,17},{20,21},{24,25},{28,29}} | collective-permute-start | bytes 3145736 | tf_op jit(solution)/shard_map/ppermute | solution.py:795
  720.8 26.9 %collective-permute-start.36 = (bf16[256,2048]{1,0:T(8,128)(2,1)}, bf16[256,2048]{1,0:T(8,128)(2,1)S(1)}, u32[]{:S(2)}, u32[]{:S(2)}) collective-permute-start(bf16[256,2048]{1,0:T(8,128)(2,1)} %tie.43), channel_id=1, source_target_pairs={{2,1},{1,0},{6,5},{5,4},{10,9},{9,8},{14,13},{13,12},{18,17},{17,1... | collective-permute-start | bytes 3145736 | tf_op jit(solution)/shard_map/ppermute | solution.py:775
  722.1 1.4 collective-permute-start.34
  723.6 5.4 collective-permute-start.35
  723.6 31.8 %collective-permute-start.42 = (bf16[256,2048]{1,0:T(8,128)(2,1)}, bf16[256,2048]{1,0:T(8,128)(2,1)}, u32[]{:S(2)}, u32[]{:S(2)}) collective-permute-start(bf16[256,2048]{1,0:T(8,128)(2,1)} %get-tuple-element.165), channel_id=1, source_target_pairs={{3,2},{7,6},{11,10},{15,14},{19,18},{23,22},{27,26},{31,30}} | collective-permute-start | bytes 3145736 | tf_op jit(solution)/shard_map/ppermute | solution.py:796
  748.7 23.8 %collective-permute-start.39 = (bf16[256,2048]{1,0:T(8,128)(2,1)}, bf16[256,2048]{1,0:T(8,128)(2,1)}, u32[]{:S(2)}, u32[]{:S(2)}) collective-permute-start(bf16[256,2048]{1,0:T(8,128)(2,1)} %tie.44.refs_1_), channel_id=1, source_target_pairs={{0,1},{1,2},{4,5},{5,6},{8,9},{9,10},{12,13},{13,14},{16,17},{17,1... | collective-permute-start | bytes 3145736 | tf_op jit(solution)/shard_map/ppermute | solution.py:795
  751.4 203.8 %reduce-scatter.7.cloned.1.call-start = ((), (), s32[]{:S(2)}) async-start(), calls=%async_computation.9 | async-start | bytes 14155776 | tf_op jit(solution)/shard_map/reduce_scatter | solution.py:768
  752.4 34.7 %collective-permute-start.37 = (bf16[256,2048]{1,0:T(8,128)(2,1)}, bf16[256,2048]{1,0:T(8,128)(2,1)S(1)}, u32[]{:S(2)}, u32[]{:S(2)}) collective-permute-start(bf16[256,2048]{1,0:T(8,128)(2,1)} %tie.45), channel_id=1, source_target_pairs={{2,3},{6,7},{10,11},{14,15},{18,19},{22,23},{26,27},{30,31}} | collective-permute-start | bytes 3145736 | tf_op jit(solution)/shard_map/ppermute | solution.py:774
  754.1 33.0 %collective-permute-start.38 = (bf16[256,2048]{1,0:T(8,128)(2,1)}, bf16[256,2048]{1,0:T(8,128)(2,1)S(1)}, u32[]{:S(2)}, u32[]{:S(2)}) collective-permute-start(bf16[256,2048]{1,0:T(8,128)(2,1)} %tie.46), channel_id=1, source_target_pairs={{1,0},{5,4},{9,8},{13,12},{17,16},{21,20},{25,24},{29,28}} | collective-permute-start | bytes 3145736 | tf_op jit(solution)/shard_map/ppermute | solution.py:775
  777.0 15.1 %collective-permute-start.43 = (bf16[256,2048]{1,0:T(8,128)(2,1)}, bf16[256,2048]{1,0:T(8,128)(2,1)}, u32[]{:S(2)}, u32[]{:S(2)}) collective-permute-start(bf16[256,2048]{1,0:T(8,128)(2,1)} %tie.49), channel_id=1, source_target_pairs={{3,2},{2,1},{7,6},{6,5},{11,10},{10,9},{15,14},{14,13},{19,18},{18... | collective-permute-start | bytes 3145736 | tf_op jit(solution)/shard_map/ppermute | solution.py:796
  778.7 6.9 collective-permute-start.40
  788.5 28.1 %collective-permute-start.41 = (bf16[256,2048]{1,0:T(8,128)(2,1)}, bf16[256,2048]{1,0:T(8,128)(2,1)S(1)}, u32[]{:S(2)}, u32[]{:S(2)}) collective-permute-start(bf16[256,2048]{1,0:T(8,128)(2,1)} %tie.48), channel_id=1, source_target_pairs={{0,1},{1,2},{2,3},{4,5},{5,6},{6,7},{8,9},{9,10},{10,11},{12,13},{... | collective-permute-start | bytes 3145736 | tf_op jit(solution)/shard_map/ppermute | solution.py:795
  795.1 35.7 %collective-permute-start.44 = (bf16[256,2048]{1,0:T(8,128)(2,1)}, bf16[256,2048]{1,0:T(8,128)(2,1)S(1)}, u32[]{:S(2)}, u32[]{:S(2)}) collective-permute-start(bf16[256,2048]{1,0:T(8,128)(2,1)} %tie.50), channel_id=1, source_target_pairs={{3,2},{2,1},{1,0},{7,6},{6,5},{5,4},{11,10},{10,9},{9,8},{15,14},{... | collective-permute-start | bytes 3145736 | tf_op jit(solution)/shard_map/ppermute | solution.py:796
  841.9 22.6 %collective-permute-start.45 = (bf16[256,2048]{1,0:T(8,128)(2,1)S(1)}, bf16[256,2048]{1,0:T(8,128)(2,1)}, u32[]{:S(2)}, u32[]{:S(2)}) collective-permute-start(bf16[256,2048]{1,0:T(8,128)(2,1)S(1)} %fusion.36), channel_id=1, source_target_pairs={{0,1},{1,2},{2,3},{4,5},{5,6},{6,7},{8,9},{9,10},{10,11},{12,13},{... | collective-permute-start | bytes 3145736 | tf_op jit(solution)/shard_map/ppermute | solution.py:774
  846.9 23.0 %collective-permute-start.48 = (bf16[256,2048]{1,0:T(8,128)(2,1)S(1)}, bf16[256,2048]{1,0:T(8,128)(2,1)}, u32[]{:S(2)}, u32[]{:S(2)}) collective-permute-start(bf16[256,2048]{1,0:T(8,128)(2,1)S(1)} %fusion.36), channel_id=1, source_target_pairs={{3,2},{2,1},{1,0},{7,6},{6,5},{5,4},{11,10},{10,9},{9,8},{15,14},{... | collective-permute-start | bytes 3145736 | tf_op jit(solution)/shard_map/ppermute | solution.py:775
  864.4 8.9 collective-permute-start.46
  869.9 24.7 %collective-permute-start.49 = (bf16[256,2048]{1,0:T(8,128)(2,1)}, bf16[256,2048]{1,0:T(8,128)(2,1)}, u32[]{:S(2)}, u32[]{:S(2)}) collective-permute-start(bf16[256,2048]{1,0:T(8,128)(2,1)} %collective-permute-done.48), channel_id=1, source_target_pairs={{2,1},{1,0},{6,5},{5,4},{10,9},{9,8},{14,13},{13,12},{18,17},{17,1... | collective-permute-start | bytes 3145736 | tf_op jit(solution)/shard_map/ppermute | solution.py:775
  873.3 65.6 %collective-permute-start.47 = (bf16[256,2048]{1,0:T(8,128)(2,1)}, bf16[256,2048]{1,0:T(8,128)(2,1)}, u32[]{:S(2)}, u32[]{:S(2)}) collective-permute-start(bf16[256,2048]{1,0:T(8,128)(2,1)} %collective-permute-done.46.refs_1_), channel_id=1, source_target_pairs={{2,3},{6,7},{10,11},{14,15},{18,19},{22,23},{26,27},{30,31}} | collective-permute-start | bytes 3145736 | tf_op jit(solution)/shard_map/ppermute | solution.py:774
  894.6 46.1 %collective-permute-start.50 = (bf16[256,2048]{1,0:T(8,128)(2,1)}, bf16[256,2048]{1,0:T(8,128)(2,1)}, u32[]{:S(2)}, u32[]{:S(2)}) collective-permute-start(bf16[256,2048]{1,0:T(8,128)(2,1)} %collective-permute-done.49), channel_id=1, source_target_pairs={{1,0},{5,4},{9,8},{13,12},{17,16},{21,20},{25,24},{29,28}} | collective-permute-start | bytes 3145736 | tf_op jit(solution)/shard_map/ppermute | solution.py:775
  897.5 19.9 %collective-permute-start.51 = (f32[4352]{0:T(1024)}, f32[4352]{0:T(1024)S(1)}, u32[]{:S(2)}, u32[]{:S(2)}) collective-permute-start(f32[4352]{0:T(1024)} %tie.52), channel_id=1, source_target_pairs={{0,1},{1,0},{2,3},{3,2},{4,5},{5,4},{6,7},{7,6},{8,9},{9,8},{10,11... | collective-permute-start | bytes 52232 | tf_op jit(solution)/shard_map/ppermute | solution.py:834
  918.1 20.1 %collective-permute-start.52 = (f32[4352]{0:T(1024)S(1)}, f32[4352]{0:T(1024)S(1)}, u32[]{:S(2)}, u32[]{:S(2)}) collective-permute-start(f32[4352]{0:T(1024)S(1)} %add.318), channel_id=1, source_target_pairs={{0,2},{1,3},{2,0},{3,1},{4,6},{5,7},{6,4},{7,5},{8,10},{9,11},{10,... | collective-permute-start | bytes 52232 | tf_op jit(solution)/shard_map/ppermute | solution.py:834
  938.9 14.7 %collective-permute-start.53 = (bf16[256,1408]{1,0:T(8,128)(2,1)}, bf16[256,1408]{1,0:T(8,128)(2,1)S(1)}, u32[]{:S(2)}, u32[]{:S(2)}) collective-permute-start(bf16[256,1408]{1,0:T(8,128)(2,1)} %tie.57), channel_id=1, source_target_pairs={{0,2},{1,3},{2,0},{3,1},{4,6},{5,7},{6,4},{7,5},{8,10},{9,11},{10,... | collective-permute-start | bytes 2162696 | tf_op jit(solution)/shard_map/ppermute | solution.py:834
  (81 other events, 935.5 us)
Sparse Core Ops, SparseCore 0:
  10.6 57.0 all-gather.6
  70.2 54.5 all-gather.8
  127.3 32.3 all-gather.14
  161.4 120.9 all-gather.10
  284.1 69.8 all-gather.12
  425.1 164.3 reduce-scatter.4
  592.9 91.3 reduce-scatter.10
  751.5 49.6 reduce-scatter.8
  831.9 90.2 reduce-scatter.6
